TPU v7x, 32 devices: a whole 2x2x4 slice. The times are simulated.
32 devices in a mesh: dp: 4 (over x, core), ctx: 8 (over z, y).
Axes of the slice: x: 2, y: 2, z: 4, core: 2. Of those that a mesh axis runs over, the one named last changes fastest.
Arguments:
- tokens: bfloat16 [4, 1024, 768], P('dp', 'ctx'), may hold values from -6 to 6
- segment_numbers: int32 [4, 1024], P('dp', 'ctx'), may hold values from 0 to 7, as said below
- cotangent: bfloat16 [4, 1024, 768], P('dp', 'ctx'), may hold values from -6 to 6
- query_key_value_weight: bfloat16 [768, 2304], P(('dp', 'ctx')), may hold values from -0.21875 to 0.21875
- query_key_value_bias: bfloat16 [2304], P(('dp', 'ctx')), may hold values from -3 to 3
- output_matrix: bfloat16 [768, 768], P(('dp', 'ctx')), may hold values from -1.75 to 1.75
- output_bias: bfloat16 [768], P(('dp', 'ctx')), may hold values from -2 to 2
- up_matrix: bfloat16 [768, 3072], P(('dp', 'ctx')), may hold values from -0.21875 to 0.21875
- up_input_bias: bfloat16 [3072], P(('dp', 'ctx')), may hold values from -3 to 3
- down_matrix: bfloat16 [3072, 768], P(('dp', 'ctx')), may hold values from -0.109375 to 0.109375
- down_output_bias: bfloat16 [768], P(('dp', 'ctx')), may hold values from -2 to 2
- first_gain: bfloat16 [768], P(('dp', 'ctx')), may hold values from 0.099609375 to 1.8984375
- first_shift: bfloat16 [768], P(('dp', 'ctx')), may hold values from -2 to 2
- second_gain: bfloat16 [768], P(('dp', 'ctx')), may hold values from 0.099609375 to 1.8984375
- second_shift: bfloat16 [768], P(('dp', 'ctx')), may hold values from -2 to 2
Outputs:
- mixed: bfloat16 [4, 1024, 768], P('dp', 'ctx')
- tokens_grad: bfloat16 [4, 1024, 768], P('dp', 'ctx')
- qkv_weight_grad: float32 [768, 2304], P(('dp', 'ctx'))
- qkv_bias_grad: float32 [2304], P(('dp', 'ctx'))
- out_weight_grad: float32 [768, 768], P(('dp', 'ctx'))
- out_bias_grad: float32 [768], P(('dp', 'ctx'))
- up_weight_grad: float32 [768, 3072], P(('dp', 'ctx'))
- up_bias_grad: float32 [3072], P(('dp', 'ctx'))
- down_weight_grad: float32 [3072, 768], P(('dp', 'ctx'))
- down_bias_grad: float32 [768], P(('dp', 'ctx'))
- first_gain_grad: float32 [768], P(('dp', 'ctx'))
- first_shift_grad: float32 [768], P(('dp', 'ctx'))
- second_gain_grad: float32 [768], P(('dp', 'ctx'))
- second_shift_grad: float32 [768], P(('dp', 'ctx'))
Inputs may be any that keep to these rules, and one draw needn't show every extreme that they name: `segment_numbers`: within each sequence the numbers start at 0 and never fall, each number marking one document of consecutive tokens. The sequences of the even indices of dp hold exactly 3 documents. In such a sequence the first document ends within its first 128 tokens and the last starts within its last 128 tokens. Every other sequence holds exactly 8 documents.
All inputs are finite; a program needn't handle non-finite values.
Results may differ from a plain program's by a relative error of at most 0.0099.
Values may be sent and summed in bfloat16 or wider, within the bound.
No kernel may reach another device: no remote copies, remote signals or barrier semaphores. Data moves between devices by JAX's collectives and lax.ppermute only.
A program may use at most 192 MiB of HBM per device.

v0:
```python
from functools import partial
import math

import jax
import jax.numpy as jnp
from jax import lax
from jax.sharding import PartitionSpec as P

HD = 64
ROT = 16


eps = 1e-05


def rotation_tables(position):
    half = ROT // 2
    freq = 10000.0 ** (-jnp.arange(half, dtype=jnp.float32) * 2.0 / ROT)
    angle = position.astype(jnp.float32)[..., None] * freq
    return (jnp.cos(angle)[..., None, :], jnp.sin(angle)[..., None, :])


def rotate(field, cosine, sine):
    half = ROT // 2
    first = field[..., :half]
    second = field[..., half:ROT]
    return jnp.concatenate(
        [first * cosine - second * sine, second * cosine + first * sine, field[..., ROT:]], axis=-1
    )


def rotate_back(grad, cosine, sine):
    half = ROT // 2
    first = grad[..., :half]
    second = grad[..., half:ROT]
    return jnp.concatenate(
        [first * cosine + second * sine, second * cosine - first * sine, grad[..., ROT:]], axis=-1
    )


def over_blocks(step, carry, piece, start_offset):
    width = piece[0].shape[1]
    block_length = math.gcd(width, 512)
    token_count = width // block_length

    def advance(number, state):
        offset = number * block_length
        part = tuple((lax.dynamic_slice_in_dim(p, offset, block_length, 1) for p in piece))
        return step(state, part, start_offset + offset)

    return lax.fori_loop(0, token_count, advance, carry)


def scores_masked(query_rows, key, query_index, query_segment, key_index, key_segment):
    seqs, width = (key.shape[0], key.shape[1])
    keys = key.reshape(seqs, width, query_rows.shape[2], HD)
    score_matrix = jnp.einsum(
        "sqhd,skhd->shqk", query_rows, keys, preferred_element_type=jnp.float32
    ) * HD ** (-0.5)
    allowed_pairs = (key_index[None, None, :] <= query_index[None, :, None]) & (
        key_segment[:, None, :] == query_segment[:, :, None]
    )
    return (score_matrix, allowed_pairs[:, None])


def per_device(
    tokens,
    segment_numbers,
    cotangent,
    query_key_value_weight,
    query_key_value_bias,
    output_matrix,
    output_bias,
    up_matrix,
    up_input_bias,
    down_matrix,
    down_output_bias,
    first_gain,
    first_shift,
    second_gain,
    second_shift,
):
    seqs, block, width = tokens.shape
    heads = width // HD
    rows = seqs * block
    scale = HD ** (-0.5)
    w_qkv, b_qkv, w_out, b_out, w_up, b_up, w_down, b_down, g_one, s_one, g_two, s_two = (
        lax.all_gather(query_key_value_weight, ("dp", "ctx"), axis=0, tiled=True),
        lax.all_gather(query_key_value_bias, ("dp", "ctx"), axis=0, tiled=True),
        lax.all_gather(output_matrix, ("dp", "ctx"), axis=0, tiled=True),
        lax.all_gather(output_bias, ("dp", "ctx"), axis=0, tiled=True),
        lax.all_gather(up_matrix, ("dp", "ctx"), axis=0, tiled=True),
        lax.all_gather(up_input_bias, ("dp", "ctx"), axis=0, tiled=True),
        lax.all_gather(down_matrix, ("dp", "ctx"), axis=0, tiled=True),
        lax.all_gather(down_output_bias, ("dp", "ctx"), axis=0, tiled=True),
        lax.all_gather(first_gain, ("dp", "ctx"), axis=0, tiled=True),
        lax.all_gather(first_shift, ("dp", "ctx"), axis=0, tiled=True),
        lax.all_gather(second_gain, ("dp", "ctx"), axis=0, tiled=True),
        lax.all_gather(second_shift, ("dp", "ctx"), axis=0, tiled=True),
    )
    seg_all = lax.all_gather(segment_numbers, "ctx", axis=1, tiled=True)
    length = seg_all.shape[1]
    index_all = jnp.arange(length, dtype=jnp.int32)
    fresh = jnp.concatenate(
        [jnp.ones((seqs, 1), jnp.bool_), seg_all[:, 1:] != seg_all[:, :-1]], axis=1
    )
    starts = lax.cummax(jnp.where(fresh, index_all[None, :], jnp.zeros_like(seg_all)), axis=1)
    offset = lax.axis_index("ctx") * block
    query_index = offset + jnp.arange(block, dtype=jnp.int32)
    position = query_index[None, :] - lax.dynamic_slice_in_dim(starts, offset, block, 1)
    cosine, sine = rotation_tables(position)
    xval = tokens.reshape(rows, width).astype(jnp.float32)
    mean = jnp.mean(xval, axis=-1, keepdims=True)
    centered = xval - mean
    inverse = lax.rsqrt(jnp.mean(centered * centered, axis=-1, keepdims=True) + eps)
    normed = centered * inverse
    first_input = (normed * g_one.astype(jnp.float32) + s_one.astype(jnp.float32)).astype(
        jnp.bfloat16
    )
    second_input = (normed * g_two.astype(jnp.float32) + s_two.astype(jnp.float32)).astype(
        jnp.bfloat16
    )
    query_key_value = jnp.dot(
        first_input, w_qkv, preferred_element_type=jnp.float32
    ) + b_qkv.astype(jnp.float32)
    query_key_value = query_key_value.reshape(seqs, block, 3 * width)
    query_block = rotate(
        query_key_value[..., :width].reshape(seqs, block, heads, HD), cosine, sine
    ).astype(jnp.bfloat16)
    key_b = (
        rotate(
            query_key_value[..., width : 2 * width].reshape(seqs, block, heads, HD), cosine, sine
        )
        .astype(jnp.bfloat16)
        .reshape(seqs, block, width)
    )
    value_b = query_key_value[..., 2 * width :].astype(jnp.bfloat16)

    def forward_step(carry, piece, start_offset):
        top, total, acc = carry
        key, value_rows = piece
        token_count = key.shape[1]
        key_index = start_offset + jnp.arange(token_count, dtype=jnp.int32)
        key_segment = lax.dynamic_slice_in_dim(seg_all, start_offset, token_count, 1)
        score_matrix, allowed_pairs = scores_masked(
            query_block, key, query_index, segment_numbers, key_index, key_segment
        )
        masked = jnp.where(allowed_pairs, score_matrix, -1e30)
        new_top = jnp.maximum(top, jnp.max(masked, axis=-1))
        weights = jnp.where(allowed_pairs, jnp.exp(masked - new_top[..., None]), 0.0)
        decay = jnp.exp(top - new_top)
        values = value_rows.reshape(seqs, token_count, heads, HD)
        total = total * decay + jnp.sum(weights, axis=-1)
        acc = acc * decay[..., None] + jnp.einsum(
            "shqk,skhd->shqd",
            weights.astype(jnp.bfloat16),
            values,
            preferred_element_type=jnp.float32,
        )
        return (new_top, total, acc)

    init = (
        jnp.full((seqs, heads, block), -1e30, jnp.float32),
        jnp.zeros((seqs, heads, block), jnp.float32),
        jnp.zeros((seqs, heads, block, HD), jnp.float32),
    )
    top, total, acc = over_blocks(
        forward_step,
        init,
        (
            lax.all_gather(key_b, "ctx", axis=1, tiled=True),
            lax.all_gather(value_b, "ctx", axis=1, tiled=True),
        ),
        jnp.int32(0),
    )
    attended_output = acc / total[..., None]
    log_sum_exp = top + jnp.log(total)
    attended_rows = attended_output.transpose(0, 2, 1, 3).reshape(rows, width)
    attended_b = attended_rows.astype(jnp.bfloat16)
    attention_block = jnp.dot(attended_b, w_out, preferred_element_type=jnp.float32) + b_out.astype(
        jnp.float32
    )
    pre_activation = jnp.dot(second_input, w_up, preferred_element_type=jnp.float32) + b_up.astype(
        jnp.float32
    )
    hidden_state, gelu_back = jax.vjp(partial(jax.nn.gelu, approximate=False), pre_activation)
    hidden_b = hidden_state.astype(jnp.bfloat16)
    feed_forward = jnp.dot(hidden_b, w_down, preferred_element_type=jnp.float32) + b_down.astype(
        jnp.float32
    )
    mixed = (xval + attention_block + feed_forward).astype(jnp.bfloat16).reshape(seqs, block, width)
    v_qkv, v_out, v_up, v_down, h_one, h_two = (
        lax.all_gather(query_key_value_weight, ("dp", "ctx"), axis=0, tiled=True),
        lax.all_gather(output_matrix, ("dp", "ctx"), axis=0, tiled=True),
        lax.all_gather(up_matrix, ("dp", "ctx"), axis=0, tiled=True),
        lax.all_gather(down_matrix, ("dp", "ctx"), axis=0, tiled=True),
        lax.all_gather(first_gain, ("dp", "ctx"), axis=0, tiled=True),
        lax.all_gather(second_gain, ("dp", "ctx"), axis=0, tiled=True),
    )
    kv_all = (
        lax.all_gather(key_b, "ctx", axis=1, tiled=True),
        lax.all_gather(value_b, "ctx", axis=1, tiled=True),
    )
    cot_b = cotangent.reshape(rows, width)
    cot = cot_b.astype(jnp.float32)
    grad_down_w = jnp.dot(hidden_b.T, cot_b, preferred_element_type=jnp.float32)
    grad_down_b = jnp.sum(cot, axis=0)
    grad_out_w = jnp.dot(attended_b.T, cot_b, preferred_element_type=jnp.float32)
    hidden_grad = jnp.dot(cot_b, v_down.T, preferred_element_type=jnp.float32)
    pre_grad = gelu_back(hidden_grad)[0].astype(jnp.bfloat16)
    grad_up_w = jnp.dot(second_input.T, pre_grad, preferred_element_type=jnp.float32)
    grad_up_b = jnp.sum(pre_grad.astype(jnp.float32), axis=0)
    second_grad = jnp.dot(pre_grad, v_up.T, preferred_element_type=jnp.float32)
    attended_grad = jnp.dot(cot_b, v_out.T, preferred_element_type=jnp.float32).astype(jnp.bfloat16)
    output_gradient_block = attended_grad.reshape(seqs, block, heads, HD)
    outgrad_f = output_gradient_block.astype(jnp.float32)
    delta_terms = jnp.sum(outgrad_f.transpose(0, 2, 1, 3) * attended_output, axis=-1)

    def pair_gradients(
        query_portion,
        gradient_portion,
        logsum_portion,
        delta_portion,
        query_position,
        query_segment,
        key,
        value_rows,
        key_index,
        key_segment,
    ):
        token_count = key.shape[1]
        score_matrix, allowed_pairs = scores_masked(
            query_portion, key, query_position, query_segment, key_index, key_segment
        )
        weights = jnp.where(allowed_pairs, jnp.exp(score_matrix - logsum_portion[..., None]), 0.0)
        values = value_rows.reshape(seqs, token_count, heads, HD)
        prob_grad = jnp.einsum(
            "sqhd,skhd->shqk", gradient_portion, values, preferred_element_type=jnp.float32
        )
        score_grad = (weights * (prob_grad - delta_portion[..., None])).astype(jnp.bfloat16)
        return (weights, score_grad)

    def query_step(carry, piece, start_offset):
        key, value_rows = piece
        token_count = key.shape[1]
        key_index = start_offset + jnp.arange(token_count, dtype=jnp.int32)
        key_segment = lax.dynamic_slice_in_dim(seg_all, start_offset, token_count, 1)
        weights, score_grad = pair_gradients(
            query_block,
            output_gradient_block,
            log_sum_exp,
            delta_terms,
            query_index,
            segment_numbers,
            key,
            value_rows,
            key_index,
            key_segment,
        )
        keys = key.reshape(seqs, token_count, heads, HD)
        return (
            carry
            + jnp.einsum("shqk,skhd->shqd", score_grad, keys, preferred_element_type=jnp.float32)
            * scale
        )

    query_grad = over_blocks(
        query_step, jnp.zeros((seqs, heads, block, HD), jnp.float32), kv_all, 0
    )
    token_count = block * lax.axis_size("ctx")
    block_length = math.gcd(token_count, 512)

    def one_block(number):
        begin_offset = number * block_length
        key = lax.dynamic_slice_in_dim(kv_all[0], begin_offset, block_length, 1)
        value_rows = lax.dynamic_slice_in_dim(kv_all[1], begin_offset, block_length, 1)
        key_index = begin_offset + jnp.arange(block_length, dtype=jnp.int32)
        key_segment = lax.dynamic_slice_in_dim(seg_all, begin_offset, block_length, 1)
        weights, score_grad = pair_gradients(
            query_block,
            output_gradient_block,
            log_sum_exp,
            delta_terms,
            query_index,
            segment_numbers,
            key,
            value_rows,
            key_index,
            key_segment,
        )
        key_grad = (
            jnp.einsum(
                "shqk,sqhd->skhd", score_grad, query_block, preferred_element_type=jnp.float32
            )
            * scale
        )
        value_grad = jnp.einsum(
            "shqk,sqhd->skhd",
            weights.astype(jnp.bfloat16),
            output_gradient_block,
            preferred_element_type=jnp.float32,
        )
        paired = jnp.concatenate(
            [
                key_grad.reshape(seqs, block_length, width),
                value_grad.reshape(seqs, block_length, width),
            ],
            axis=-1,
        )
        return paired.transpose(1, 0, 2)

    parts = lax.map(one_block, jnp.arange(token_count // block_length, dtype=jnp.int32))
    kv_grad = lax.psum_scatter(
        parts.reshape(token_count, seqs, 2 * width), "ctx", scatter_dimension=0, tiled=True
    ).transpose(1, 0, 2)
    query_back = rotate_back(query_grad.transpose(0, 2, 1, 3), cosine, sine).reshape(
        seqs, block, width
    )
    key_back = rotate_back(
        kv_grad[..., :width].reshape(seqs, block, heads, HD), cosine, sine
    ).reshape(seqs, block, width)
    qkv_grad = (
        jnp.concatenate([query_back, key_back, kv_grad[..., width:]], axis=-1)
        .reshape(rows, 3 * width)
        .astype(jnp.bfloat16)
    )
    grad_qkv_w = jnp.dot(first_input.T, qkv_grad, preferred_element_type=jnp.float32)
    grad_qkv_b = jnp.sum(qkv_grad.astype(jnp.float32), axis=0)
    first_grad = jnp.dot(qkv_grad, v_qkv.T, preferred_element_type=jnp.float32)
    grad_g_one = jnp.sum(normed * first_grad, axis=0)
    grad_s_one = jnp.sum(first_grad, axis=0)
    grad_g_two = jnp.sum(normed * second_grad, axis=0)
    grad_s_two = jnp.sum(second_grad, axis=0)
    normed_grad = first_grad * h_one.astype(jnp.float32) + second_grad * h_two.astype(jnp.float32)
    inner = (
        normed_grad
        - jnp.mean(normed_grad, axis=-1, keepdims=True)
        - normed * jnp.mean(normed_grad * normed, axis=-1, keepdims=True)
    )
    tokens_grad = (cot + inner * inverse).astype(jnp.bfloat16).reshape(seqs, block, width)
    shards = (
        lax.psum_scatter(grad_qkv_w, ("dp", "ctx"), scatter_dimension=0, tiled=True),
        lax.psum_scatter(grad_qkv_b, ("dp", "ctx"), scatter_dimension=0, tiled=True),
        lax.psum_scatter(grad_out_w, ("dp", "ctx"), scatter_dimension=0, tiled=True),
        lax.psum_scatter(grad_down_b, ("dp", "ctx"), scatter_dimension=0, tiled=True),
        lax.psum_scatter(grad_up_w, ("dp", "ctx"), scatter_dimension=0, tiled=True),
        lax.psum_scatter(grad_up_b, ("dp", "ctx"), scatter_dimension=0, tiled=True),
        lax.psum_scatter(grad_down_w, ("dp", "ctx"), scatter_dimension=0, tiled=True),
        lax.psum_scatter(grad_down_b, ("dp", "ctx"), scatter_dimension=0, tiled=True),
        lax.psum_scatter(grad_g_one, ("dp", "ctx"), scatter_dimension=0, tiled=True),
        lax.psum_scatter(grad_s_one, ("dp", "ctx"), scatter_dimension=0, tiled=True),
        lax.psum_scatter(grad_g_two, ("dp", "ctx"), scatter_dimension=0, tiled=True),
        lax.psum_scatter(grad_s_two, ("dp", "ctx"), scatter_dimension=0, tiled=True),
    )
    return (mixed, tokens_grad) + tuple(shards)


def solution(mesh):
    in_specs = (
        P("dp", "ctx", None),
        P("dp", "ctx"),
        P("dp", "ctx", None),
        P(("dp", "ctx"), None),
        P(("dp", "ctx")),
        P(("dp", "ctx"), None),
        P(("dp", "ctx")),
        P(("dp", "ctx"), None),
        P(("dp", "ctx")),
        P(("dp", "ctx"), None),
        P(("dp", "ctx")),
        P(("dp", "ctx")),
        P(("dp", "ctx")),
        P(("dp", "ctx")),
        P(("dp", "ctx")),
    )
    out_specs = (
        P("dp", "ctx", None),
        P("dp", "ctx", None),
        P(("dp", "ctx"), None),
        P(("dp", "ctx")),
        P(("dp", "ctx"), None),
        P(("dp", "ctx")),
        P(("dp", "ctx"), None),
        P(("dp", "ctx")),
        P(("dp", "ctx"), None),
        P(("dp", "ctx")),
        P(("dp", "ctx")),
        P(("dp", "ctx")),
        P(("dp", "ctx")),
        P(("dp", "ctx")),
    )
    return jax.shard_map(
        per_device, mesh=mesh, in_specs=in_specs, out_specs=out_specs, check_vma=False
    )
```

profile of v0, /device:TPU:18, one launch (start us, length us, event | category | flops | bytes accessed | tf_op | source)
XLA Modules:
  0.0 989.9 jit_solution(18247322999316496076)
XLA Ops:
  15.5 42.2 %all-reduce.16 = (bf16[3072]{0:T(1024)(128)(2,1)}, bf16[768]{0:T(1024)(128)(2,1)}, bf16[768]{0:T(1024)(128)(2,1)}, bf16[768]{0:T(1024)(128)(2,1)}, bf16[2304]{0:...) all-reduce(bf16[3072]{0:T(1024)(128)(2,1)S(1)} %dynamic-update-slic, ...), channel_id=1, replica_groups=mesh['dp'=4,'ctx'=8] {'dp','ctx'}, use_global_device_ids=true, to_apply=%add.6 | all-reduce | flops 9984 | bytes 39936
  59.8 11.1 %all-gather.7.cloned.1.call-done = bf16[768,2304]{1,0:T(8,128)(2,1)} async-done(((bf16[24,2304]{1,0:T(8,128)(2,1)}), bf16[768,2304]{1,0:T(8,128)(2,1)}) %all-gather.7.cloned.1.call-update) | async-done | bytes 3538960 | tf_op jit(solution)/shard_map/all_gather | solution.py:88
  70.9 2.8 fusion.53
  74.5 14.3 %all_gather.53 = s32[1,1024]{1,0:T(1,128)S(1)} all-gather(s32[1,128]{1,0:T(1,128)} %param.22), channel_id=1, replica_groups=mesh['dp'=4,'ctx'=8] {'ctx'}, dimensions={1}, use_global_device_ids=true | all-gather | bytes 4608 | tf_op jit(solution)/shard_map/all_gather | solution.py:101
  92.7 34.0 %all-gather.13.cloned.1.call-done = bf16[768,768]{1,0:T(8,128)(2,1)} async-done(((bf16[24,768]{1,0:T(8,128)(2,1)}), bf16[768,768]{1,0:T(8,128)(2,1)}) %all-gather.13.cloned.1.call-update) | async-done | bytes 1179664 | tf_op jit(solution)/shard_map/all_gather | solution.py:90
  126.7 1.8 convolution_convert_fusion
  129.4 44.4 %all-gather.11.cloned.1.call-done = bf16[1,1024,768]{2,1,0:T(8,128)(2,1)} async-done(((bf16[1,128,768]{2,1,0:T(8,128)(2,1)}), bf16[1,1024,768]{2,1,0:T(8,128)(2,1)}) %all-gather.11.cloned.1.call-update) | async-done | bytes 1572880 | tf_op jit(solution)/shard_map/all_gather | solution.py:172
  173.8 2.6 copy.70
  176.4 43.4 %all-gather.9.cloned.1.call-done = bf16[1,1024,768]{1,2,0:T(8,128)(2,1)} async-done(((bf16[1,128,768]{1,2,0:T(8,128)(2,1)}), bf16[1,1024,768]{1,2,0:T(8,128)(2,1)}) %all-gather.9.cloned.1.call-update) | async-done | bytes 1572880 | tf_op jit(solution)/shard_map/all_gather | solution.py:171
  219.8 15.8 %while.44 = (s32[]{:T(128)}, f32[1,12,128]{2,1,0:T(8,128)S(1)}, f32[1,12,128]{2,1,0:T(8,128)S(1)}, f32[1,12,128,64]{2,3,1,0:T(8,128)}, s32[1,1024]{1,0:T(1,128)S...) while((s32[]{:T(128)}, f32[1,12,128]{2,1,0:T(8,128)S(1)}, ...), condition=%wide.region_7.8_spmd.clone, body=%wide.region_4.0_spmd.clone.sunk | while | flops 212051584 | bytes 15511247 | solution.py:51
  220.7 2.4 constant_dynamic-slice_fusion.18
  223.9 2.9 fusion.188
  228.6 2.5 constant_dynamic-slice_fusion.18
  231.8 3.0 fusion.188
  235.7 2.4 fusion.94
  238.1 36.6 %while.43 = (s32[]{:T(128)}, f32[2,512,1,1536]{3,1,0,2:T(8,128)}, s32[2]{0:T(128)S(1)}, s32[1,1024]{1,0:T(1,128)S(1)}, s32[1,128]{1,0:T(1,128)}, /*index=5*/bf16...) while((s32[]{:T(128)}, f32[2,512,1,1536]{3,1,0,2:T(8,128)}, ...), condition=%wide.region_12.13_spmd.clone, body=%wide.region_11.12_spmd.clone.sunk | while | flops 411894400 | bytes 44267920 | solution.py:312
  240.9 2.4 constant_dynamic-slice_fusion.15
  244.3 4.0 convolution_multiply_fusion.2
  248.2 1.7 fusion.181
  250.3 2.4 copy.99
  252.6 3.8 constant_dynamic-update-slice_fusion.2
  259.2 2.4 constant_dynamic-slice_fusion.15
  262.6 4.0 convolution_multiply_fusion.2
  266.5 1.7 fusion.181
  268.6 2.4 copy.99
  271.0 3.8 constant_dynamic-update-slice_fusion.2
  275.8 1.9 fusion.102
  278.4 6.7 all-gather.15.cloned.1.call-done
  285.1 8.4 multiply_convert_fusion
  293.5 56.8 %all-gather.17.cloned.1.call-done = bf16[3072,768]{1,0:T(8,128)(2,1)} async-done(((bf16[96,768]{1,0:T(8,128)(2,1)}), bf16[3072,768]{1,0:T(8,128)(2,1)}) %all-gather.17.cloned.1.call-update) | async-done | bytes 4718608 | tf_op jit(solution)/shard_map/all_gather | solution.py:94
  350.3 5.6 convert_reduce_fusion
  355.9 5.2 fusion.121
  361.2 5.1 fusion.100
  367.7 18.8 %while.45 = (s32[]{:T(128)}, f32[1,12,128,64]{2,3,1,0:T(8,128)}, s32[1,1024]{1,0:T(1,128)S(1)}, s32[1,128]{1,0:T(1,128)}, bf16[1,1024,768]{1,2,0:T(8,128)(2,1)S(...) while((s32[]{:T(128)}, f32[1,12,128,64]{2,3,1,0:T(8,128)}, ...), condition=%wide.region_10.11_spmd.clone, body=%wide.region_9.10_spmd.clone.sunk | while | flops 307200640 | bytes 13131477 | solution.py:51
  370.5 2.3 fusion.194
  372.8 4.2 fusion.195
  379.8 2.3 fusion.194
  382.1 4.4 fusion.195
  387.5 82.6 %reduce-scatter.6.cloned.1.call-done = f32[128,1,1536]{2,0,1:T(8,128)} async-done(((f32[1024,1,1536]{2,0,1:T(8,128)}), f32[128,1,1536]{2,0,1:T(8,128)}) %reduce-scatter.6.cloned.1.call-update) | async-done | bytes 786448 | tf_op jit(solution)/shard_map/reduce_scatter | solution.py:313
  472.7 4.1 fusion.64
  478.0 3.2 convolution_add_fusion.3
  482.8 3.4 fusion.95
  486.2 4.3 fusion.124
  491.4 40.8 %all-reduce.15 = (f32[2304]{0:T(1024)S(1)}, f32[768]{0:T(1024)S(1)}, f32[3072]{0:T(1024)S(1)}, f32[768]{0:T(1024)S(1)}, f32[768]{0:T(1024)S(1)}, /*index=5*/f32[768]{0:T(1024)S(1)}, f32[768]{0:T(1024)S(1)}) all-reduce(f32[2304]{0:T(1024)S(1)} %convert_reduce_fusion.1, ...), channel_id=4, replica_groups=mesh['dp'=4,'ctx'=8] {'dp','ctx'}, use_global_device_ids=true, to_apply=%region_18.19.clone | all-reduce | flops 9216 | bytes 73728
  535.8 38.7 %reduce-scatter.10.cloned.1.call-done = f32[24,768]{1,0:T(8,128)} async-done(((f32[768,768]{1,0:T(8,128)}), f32[24,768]{1,0:T(8,128)}) %reduce-scatter.10.cloned.1.call-update) | async-done | bytes 73744 | tf_op jit(solution)/shard_map/reduce_scatter | solution.py:344
  574.5 142.2 %reduce-scatter.12.cloned.1.call-done = f32[24,3072]{1,0:T(8,128)} async-done(((f32[768,3072]{1,0:T(8,128)}), f32[24,3072]{1,0:T(8,128)}) %reduce-scatter.12.cloned.1.call-update) | async-done | bytes 294928 | tf_op jit(solution)/shard_map/reduce_scatter | solution.py:346
  716.7 140.9 %reduce-scatter.14.cloned.1.call-done = f32[96,768]{1,0:T(8,128)} async-done(((f32[3072,768]{1,0:T(8,128)}), f32[96,768]{1,0:T(8,128)}) %reduce-scatter.14.cloned.1.call-update) | async-done | bytes 294928 | tf_op jit(solution)/shard_map/reduce_scatter | solution.py:348
  857.5 125.3 %reduce-scatter.8.cloned.1.call-done = f32[24,2304]{1,0:T(8,128)} async-done(((f32[768,2304]{1,0:T(8,128)}), f32[24,2304]{1,0:T(8,128)}) %reduce-scatter.8.cloned.1.call-update) | async-done | bytes 221200 | tf_op jit(solution)/shard_map/reduce_scatter | solution.py:342
  (229 shorter events, 47.0 us)
Async XLA Ops:
  7.2 63.7 %all-gather.7.cloned.1.call-start = ((), (), s32[]{:S(2)}) async-start(), calls=%async_computation.5 | async-start | bytes 3649536 | tf_op jit(solution)/shard_map/all_gather | solution.py:88
  7.9 118.8 %all-gather.13.cloned.1.call-start = ((), (), s32[]{:S(2)}) async-start(), calls=%async_computation.8 | async-start | bytes 1216512 | tf_op jit(solution)/shard_map/all_gather | solution.py:90
  8.7 165.1 %all-gather.11.cloned.1.call-start = ((), (), s32[]{:S(2)}) async-start(), calls=%async_computation.7 | async-start | bytes 1769472 | tf_op jit(solution)/shard_map/all_gather | solution.py:172
  57.6 16.1 %copy-start.15 = (f32[768]{0:T(1024)}, f32[768]{0:T(1024)S(1)}, u32[]{:S(2)}) copy-start(f32[768]{0:T(1024)S(1)} %convert_element_type.149) | copy-start | bytes 9220
  58.7 15.1 %copy-start.23 = (f32[128]{0:T(128)}, f32[128]{0:T(128)S(1)}, u32[]{:S(2)}) copy-start(f32[128]{0:T(128)S(1)} %broadcast_multiply_fusion.2) | copy-start | bytes 1540
  59.8 13.9 %copy-start.26 = (f32[128]{0:T(128)}, f32[128]{0:T(128)S(1)}, u32[]{:S(2)}) copy-start(f32[128]{0:T(128)S(1)} %add_rsqrt_fusion) | copy-start | bytes 1540
  74.5 145.3 %all-gather.9.cloned.1.call-start = ((), (), s32[]{:S(2)}) async-start(), calls=%async_computation.6 | async-start | bytes 1769472 | tf_op jit(solution)/shard_map/all_gather | solution.py:171
  90.0 36.7 %copy-start.9 = (bf16[1,128,768]{2,1,0:T(8,128)(2,1)S(1)}, bf16[1,128,768]{2,1,0:T(8,128)(2,1)}, u32[]{:S(2)}) copy-start(bf16[1,128,768]{2,1,0:T(8,128)(2,1)} %param.23) | copy-start | bytes 589828
  91.2 193.8 %all-gather.15.cloned.1.call-start = ((), (), s32[]{:S(2)}) async-start(), calls=%async_computation.9 | async-start | bytes 4866048 | tf_op jit(solution)/shard_map/all_gather | solution.py:92
  91.8 258.5 %all-gather.17.cloned.1.call-start = ((), (), s32[]{:S(2)}) async-start(), calls=%async_computation.10 | async-start | bytes 4866048 | tf_op jit(solution)/shard_map/all_gather | solution.py:94
  92.4 377.8 %reduce-scatter.6.cloned.1.call-start = ((), (), s32[]{:S(2)}) async-start(), calls=%async_computation.11 | async-start | bytes 7077888 | tf_op jit(solution)/shard_map/reduce_scatter | solution.py:313
  238.1 1.3 copy-start.35
  243.3 0.9 copy-start.3
  248.2 1.7 copy-start.1
  252.6 3.8 copy-start.36
  256.4 1.3 copy-start.35
  261.6 0.9 copy-start.3
  266.5 1.7 copy-start.1
  271.0 3.8 copy-start.36
  274.7 0.9 copy-start.10
  274.7 1.0 copy-start.12
  274.8 299.7 %reduce-scatter.10.cloned.1.call-start = ((), (), s32[]{:S(2)}) async-start(), calls=%async_computation.13 | async-start | bytes 2433024 | tf_op jit(solution)/shard_map/reduce_scatter | solution.py:344
  277.7 0.7 copy-start.33
  277.7 0.7 copy-start.30
  277.7 7.4 copy-start.2
  277.7 7.4 copy-start.24
  277.7 7.4 copy-start.27
  277.7 438.9 %reduce-scatter.12.cloned.1.call-start = ((), (), s32[]{:S(2)}) async-start(), calls=%async_computation.14 | async-start | bytes 9732096 | tf_op jit(solution)/shard_map/reduce_scatter | solution.py:346
  278.3 77.6 %copy-start.17 = (f32[768]{0:T(1024)}, f32[768]{0:T(1024)S(1)}, u32[]{:S(2)}) copy-start(f32[768]{0:T(1024)S(1)} %convert_element_type.158) | copy-start | bytes 9220
  293.5 67.7 %copy-start.5 = (bf16[128,3072]{1,0:T(8,128)(2,1)}, bf16[128,3072]{1,0:T(8,128)(2,1)S(1)}, u32[]{:S(2)}) copy-start(bf16[128,3072]{1,0:T(8,128)(2,1)S(1)} %get-tuple-element.716) | copy-start | bytes 2359300
  355.9 5.2 copy-start.7
  361.2 496.3 %reduce-scatter.14.cloned.1.call-start = ((), (), s32[]{:S(2)}) async-start(), calls=%async_computation.15 | async-start | bytes 9732096 | tf_op jit(solution)/shard_map/reduce_scatter | solution.py:348
  366.3 1.4 copy-start
  366.3 616.5 %reduce-scatter.8.cloned.1.call-start = ((), (), s32[]{:S(2)}) async-start(), calls=%async_computation.12 | async-start | bytes 7299072 | tf_op jit(solution)/shard_map/reduce_scatter | solution.py:342
  386.5 84.9 %copy-start.20 = (f32[128,8]{0,1:T(8,128)S(1)}, f32[128,8]{0,1:T(8,128)}, u32[]{:S(2)}) copy-start(f32[128,8]{0,1:T(8,128)} %copy-done.19) | copy-start | bytes 12292
  386.5 84.9 %copy-start.22 = (f32[128,8]{0,1:T(8,128)S(1)}, f32[128,8]{0,1:T(8,128)}, u32[]{:S(2)}) copy-start(f32[128,8]{0,1:T(8,128)} %copy-done.21) | copy-start | bytes 12292
  471.2 1.5 copy-start.14
  471.2 1.5 copy-start.16
  471.2 1.5 copy-start.25
  471.2 1.5 copy-start.28
  476.9 1.1 copy-start.6
  478.0 3.2 copy-start.4
  478.0 3.3 copy-start.13
  482.7 3.4 copy-start.8
  482.8 3.4 copy-start.18
  486.2 4.3 copy-start.11
  486.2 5.2 copy-start.29
  532.3 451.1 %copy-start.37 = (f32[24]{0:T(128)}, f32[24]{0:T(128)S(1)}, u32[]{:S(2)}) copy-start(f32[24]{0:T(128)S(1)} %dynamic-slice.1) | copy-start | bytes 292
  (5 other events, 3.2 us)
Sparse Core Ops, SparseCore 0:
  10.9 59.9 all-gather.6
  73.8 52.8 all-gather.12
  129.4 44.3 all-gather.10
  176.3 43.4 all-gather.8
  222.6 62.4 all-gather.14
  287.8 62.4 all-gather.16
  353.9 116.1 reduce-scatter.5
  476.0 98.4 reduce-scatter.9
  582.0 134.6 reduce-scatter.11
  723.0 134.4 reduce-scatter.13
  864.7 118.0 reduce-scatter.7
where the time goes:
time: 993 us; the launch traced here: 990 us
  waiting for transfers between devices  729 us (73%)
  blocking collectives  97.2 us (10%)
  matrix products  80.3 us (8%)
  local copies, waits for them, and re-layouts  48.6 us (5%)
  other arithmetic  18 us (2%)
  between operations  14.5 us (1%)
    reduce_scatter x1, waiting for transfers between devices, per_device(): lax.psum_scatter(grad_up_w, ('dp', 'ctx'), scatter_dimension=0, tiled=True)  142 us
    reduce_scatter x1, waiting for transfers between devices, per_device(): lax.psum_scatter(grad_down_w, ('dp', 'ctx'), scatter_dimension=0, tiled=T...  141 us
    reduce_scatter x1, waiting for transfers between devices, per_device(): lax.psum_scatter(grad_qkv_w, ('dp', 'ctx'), scatter_dimension=0, tiled=True)  125 us
    unnamed x2, blocking collectives  82.9 us
    reduce_scatter x1, waiting for transfers between devices, per_device(): lax.psum_scatter(parts.reshape(token_count, seqs, 2 * width), 'ctx', scat...  82.6 us
    all_gather x1, waiting for transfers between devices, per_device(): lax.all_gather(down_matrix, ('dp', 'ctx'), axis=0, tiled=True)  56.8 us
    all_gather x1, waiting for transfers between devices, per_device(): lax.all_gather(value_b, 'ctx', axis=1, tiled=True)  44.4 us
    all_gather x1, waiting for transfers between devices, per_device(): lax.all_gather(key_b, 'ctx', axis=1, tiled=True)  43.4 us
  transfers between devices with their start and end apart: 11, of which 11 were waited for; matrix products, arithmetic and copies ran while one was open for 14% of the time, Pallas kernels for 0%

commit v1 on v0

--- a/solution.py
+++ b/solution.py
@@ -63,7 +63,7 @@
     return (score_matrix, allowed_pairs[:, None])
 
 
-def per_device(
+def gathered_plan(
     tokens,
     segment_numbers,
     cotangent,
@@ -355,6 +355,315 @@
     return (mixed, tokens_grad) + tuple(shards)
 
 
+def swapped(x, bit):
+    size = lax.axis_size("ctx")
+    return lax.ppermute(x, "ctx", [(i, i ^ bit) for i in range(size)])
+
+
+def slot_order(size):
+    return list(range(0, size, 2)) + list(range(1, size, 2))
+
+
+def gather_slots(x):
+    size = lax.axis_size("ctx")
+    near = jnp.stack([x] + [swapped(x, bit) for bit in range(2, size, 2)])
+    return jnp.concatenate([near, swapped(near, 1)], axis=0)
+
+
+def reduce_slots(parts):
+    size = lax.axis_size("ctx")
+    half = size // 2
+    near = parts[:half].astype(jnp.float32) + swapped(parts[half:], 1).astype(jnp.float32)
+    low = near.astype(jnp.bfloat16)
+    total = near[0]
+    for number in range(1, half):
+        total = total + swapped(low[number], 2 * number).astype(jnp.float32)
+    return total
+
+
+def between(x, offset, mine):
+    nd, nc = lax.axis_size("dp"), lax.axis_size("ctx")
+    pairs = []
+    for d in range(nd):
+        step = offset if mine is None else mine[d]
+        pairs += [
+            (d * nc + c + step, d * nc + c) for c in range(nc) if 0 <= c + step < nc
+        ]
+    return lax.ppermute(x, ("dp", "ctx"), pairs)
+
+
+def split_low(x):
+    high = x.astype(jnp.bfloat16)
+    return high, (x - high.astype(jnp.float32)).astype(jnp.bfloat16)
+
+
+def head_split_plan(
+    tokens,
+    segment_numbers,
+    cotangent,
+    query_key_value_weight,
+    query_key_value_bias,
+    output_matrix,
+    output_bias,
+    up_matrix,
+    up_input_bias,
+    down_matrix,
+    down_output_bias,
+    first_gain,
+    first_shift,
+    second_gain,
+    second_shift,
+):
+    f32, bf16 = jnp.float32, jnp.bfloat16
+    nd, nc = lax.axis_size("dp"), lax.axis_size("ctx")
+    block, width = tokens.shape[1], tokens.shape[2]
+    heads = width // HD
+    per_d = heads // nd
+    held = nd // 2
+    rows = query_key_value_weight.shape[0]
+    units = down_matrix.shape[0]
+    ff = nd * units
+    cols = held * HD
+    length = nc * block
+    d, c = lax.axis_index("dp"), lax.axis_index("ctx")
+    group = c // 3
+    half = c % 3
+    active = half < 2
+    half_in = jnp.minimum(half, 1)
+    order = jnp.asarray(slot_order(nc), jnp.int32)
+    blocks = c ^ order
+
+    qkv_parts = query_key_value_weight.reshape(rows, 3, 2, held, per_d, HD).transpose(4, 2, 0, 1, 3, 5)
+    qkv_parts = qkv_parts.reshape(per_d, 2, rows, 3 * cols)
+    qkv_parts = jnp.concatenate([qkv_parts, jnp.zeros_like(qkv_parts[:, :1])], axis=1)
+    qkv_parts = qkv_parts.reshape(3 * per_d, rows, 3 * cols)[:nc]
+    up_parts = up_matrix.reshape(rows, nd, nc, units).transpose(2, 0, 1, 3).reshape(nc, rows, ff)
+    vector = jnp.concatenate(
+        [
+            query_key_value_bias,
+            up_input_bias,
+            output_bias,
+            down_output_bias,
+            first_gain,
+            first_shift,
+            second_gain,
+            second_shift,
+            segment_numbers.reshape(block).astype(bf16),
+        ]
+    )
+    vector = jnp.pad(vector, (0, width - vector.shape[0]))
+    message = jnp.concatenate([qkv_parts, up_parts], axis=-1)
+    message = jnp.concatenate(
+        [message, jnp.broadcast_to(jnp.pad(vector[None], ((0, 7), (0, 0)))[None], (nc, 8, width))], axis=1
+    )
+    x_all = gather_slots(tokens[0]).reshape(length, width)
+    arrived = lax.all_to_all(message, "ctx", 0, 0, tiled=True)
+    two = [2 if k < nd // 2 else -2 for k in range(nd)]
+    after = between(output_matrix, 1, None)
+    before = between(output_matrix, -1, None)
+    far = between(output_matrix, 0, two)
+    strip = jnp.concatenate([far, before, output_matrix, after, far], axis=0)
+    in_lower = d < nd // 2
+    target = jnp.where(in_lower, half == 0, half == 1)
+    begin = HD * group - rows * (c - 2)
+    begin = jnp.where(target, begin, 0)
+    out_slot = lax.dynamic_slice_in_dim(strip, begin, HD, 0)
+    package = jnp.concatenate(
+        [arrived[:, :rows].reshape(nc * rows, width), down_matrix, out_slot, arrived[:, rows]], axis=0
+    )
+    every = lax.all_gather(package, "dp", axis=0, tiled=False)
+    n1 = nc * rows
+    n2 = n1 + units
+    n3 = n2 + HD
+    w_qkv = every[:, :n1, : 3 * cols].reshape(width, 3 * cols)
+    w_up = every[:, :n1, 3 * cols :].reshape(width, ff)
+    w_down = every[:, n1:n2].reshape(ff, width)
+    w_out = lax.dynamic_slice_in_dim(every[:, n2:n3], held * half_in, held, 0).reshape(cols, width)
+    vectors = every[:, n3:].reshape(nd * nc, width)
+    nb = query_key_value_bias.shape[0]
+    nu = up_input_bias.shape[0]
+    b_qkv = vectors[:, :nb].reshape(3, 2, held, per_d, HD)
+    b_qkv = lax.dynamic_index_in_dim(b_qkv, half_in, 1, False)
+    b_qkv = lax.dynamic_index_in_dim(b_qkv, group, 2, False).reshape(3 * cols)
+    b_qkv = jnp.where(active, b_qkv, 0).astype(f32)
+    b_up = lax.dynamic_index_in_dim(vectors[:, nb : nb + nu].reshape(nd, nc, nu), c, 1, False).reshape(ff).astype(f32)
+    at = nb + nu
+    b_out, b_down, g_one, s_one, g_two, s_two = (
+        vectors[:, at + k * rows : at + (k + 1) * rows].reshape(width).astype(f32) for k in range(6)
+    )
+    at = at + 6 * rows
+    seg = lax.dynamic_slice_in_dim(vectors[:, at : at + block], d * nc, nc, 0)
+    seg = jnp.take(seg, blocks, axis=0).reshape(length).astype(f32)
+    index = (blocks[:, None] * block + jnp.arange(block, dtype=jnp.int32)[None, :]).reshape(length)
+    start = jnp.sum((seg[None, :] < seg[:, None]).astype(f32), axis=1)
+    position = index.astype(f32) - start
+    cosine, sine = rotation_tables(position)
+
+    xval = x_all.astype(f32)
+    mean = jnp.mean(xval, axis=-1, keepdims=True)
+    centered = xval - mean
+    inverse = lax.rsqrt(jnp.mean(centered * centered, axis=-1, keepdims=True) + eps)
+    normed = centered * inverse
+    first_input = (normed * g_one + s_one).astype(bf16)
+    second_input = (normed * g_two + s_two).astype(bf16)
+    qkv = jnp.dot(first_input, w_qkv, preferred_element_type=f32) + b_qkv
+    qkv = qkv.reshape(length, 3, held, HD)
+    query = rotate(qkv[:, 0], cosine, sine).astype(bf16)
+    key = rotate(qkv[:, 1], cosine, sine).astype(bf16)
+    value = qkv[:, 2].astype(bf16)
+    scale = HD ** (-0.5)
+    allowed = (index[None, :] <= index[:, None]) & (seg[None, :] == seg[:, None])
+    scores = jnp.einsum("qhd,khd->hqk", query, key, preferred_element_type=f32) * scale
+    scores = jnp.where(allowed[None], scores, -1e30)
+    top = jnp.max(scores, axis=-1, keepdims=True)
+    weights = jnp.exp(scores - top)
+    weights = weights / jnp.sum(weights, axis=-1, keepdims=True)
+    weights_low = weights.astype(bf16)
+    attended = jnp.einsum("hqk,khd->qhd", weights_low, value, preferred_element_type=f32)
+    attended_low = attended.astype(bf16).reshape(length, cols)
+    pre = jnp.dot(second_input, w_up, preferred_element_type=f32) + b_up
+    hidden, gelu_back = jax.vjp(partial(jax.nn.gelu, approximate=False), pre)
+    hidden_low = hidden.astype(bf16)
+    mixed_part = jnp.dot(attended_low, w_out, preferred_element_type=f32) + jnp.dot(
+        hidden_low, w_down, preferred_element_type=f32
+    )
+    mixed_sum = reduce_slots(mixed_part.astype(bf16).reshape(nc, block, width))
+    mixed = (tokens[0].astype(f32) + (mixed_sum + (b_out + b_down))).astype(bf16)
+
+    g_all = gather_slots(cotangent[0]).reshape(length, width)
+    own = cotangent[0].astype(f32)
+    grad_down_w = jnp.dot(hidden_low.T, g_all, preferred_element_type=f32)
+    grad_out_w = jnp.dot(attended_low.T, g_all, preferred_element_type=f32)
+    hidden_grad = jnp.dot(g_all, w_down.T, preferred_element_type=f32)
+    pre_grad = gelu_back(hidden_grad)[0].astype(bf16)
+    grad_up_w = jnp.dot(second_input.T, pre_grad, preferred_element_type=f32)
+    grad_up_b = jnp.sum(pre_grad.astype(f32), axis=0)
+    second_grad = jnp.dot(pre_grad, w_up.T, preferred_element_type=f32)
+    attended_grad = jnp.dot(g_all, w_out.T, preferred_element_type=f32).astype(bf16).reshape(length, held, HD)
+    delta = jnp.sum(attended_grad.astype(f32) * attended, axis=-1)
+    prob_grad = jnp.einsum("qhd,khd->hqk", attended_grad, value, preferred_element_type=f32)
+    score_grad = (weights * (prob_grad - delta.T[:, :, None])).astype(bf16)
+    query_grad = jnp.einsum("hqk,khd->qhd", score_grad, key, preferred_element_type=f32) * scale
+    key_grad = jnp.einsum("hqk,qhd->khd", score_grad, query, preferred_element_type=f32) * scale
+    value_grad = jnp.einsum("hqk,qhd->khd", weights_low, attended_grad, preferred_element_type=f32)
+    qkv_grad = jnp.stack(
+        [rotate_back(query_grad, cosine, sine), rotate_back(key_grad, cosine, sine), value_grad], axis=1
+    ).astype(bf16)
+    qkv_grad = qkv_grad.reshape(length, 3 * cols)
+    grad_qkv_w = jnp.dot(first_input.T, qkv_grad, preferred_element_type=f32)
+    grad_qkv_b = jnp.sum(qkv_grad.astype(f32), axis=0)
+    first_grad = jnp.dot(qkv_grad, w_qkv.T, preferred_element_type=f32)
+    inner_part = first_grad * g_one + second_grad * g_two
+    inner_sum = reduce_slots(inner_part.astype(bf16).reshape(nc, block, width))
+    own_x = tokens[0].astype(f32)
+    own_centered = own_x - jnp.mean(own_x, axis=-1, keepdims=True)
+    own_inverse = lax.rsqrt(jnp.mean(own_centered * own_centered, axis=-1, keepdims=True) + eps)
+    own_normed = own_centered * own_inverse
+    inner = (
+        inner_sum
+        - jnp.mean(inner_sum, axis=-1, keepdims=True)
+        - own_normed * jnp.mean(inner_sum * own_normed, axis=-1, keepdims=True)
+    )
+    tokens_grad = (own + inner * own_inverse).astype(bf16)
+
+    zero = jnp.zeros((), f32)
+    place = jnp.zeros((3, 2, held, per_d, HD), f32)
+    place = lax.dynamic_update_slice(
+        place,
+        jnp.where(active, grad_qkv_b, 0).reshape(3, 1, held, 1, HD),
+        (0, half_in, 0, group, 0),
+    ).reshape(nd, nc, nb)
+    place_up = lax.dynamic_update_slice(
+        jnp.zeros((nd, nc, nu), f32), grad_up_b.reshape(nd, 1, nu), (0, c, 0)
+    )
+    sums = [
+        jnp.sum(own, axis=0),
+        jnp.sum(normed * first_grad, axis=0),
+        jnp.sum(first_grad, axis=0),
+        jnp.sum(normed * second_grad, axis=0),
+        jnp.sum(second_grad, axis=0),
+    ]
+    vector_grad = jnp.concatenate([place, place_up] + [s.reshape(nd, nc, rows) for s in sums], axis=-1)
+    nv = vector_grad.shape[-1]
+
+    def to_rows(values):
+        high, low = split_low(values)
+        both = jnp.concatenate([high, low], axis=-1)
+        return jnp.pad(both, [(0, 0)] * (both.ndim - 1) + [(0, width - 2 * nv)])
+
+    def from_rows(values):
+        return values[..., :nv].astype(f32) + values[..., nv : 2 * nv].astype(f32)
+
+    out_slots = jnp.zeros((nd, HD, width), bf16)
+    out_slots = lax.dynamic_update_slice(
+        out_slots,
+        jnp.where(active, grad_out_w, 0).astype(bf16).reshape(held, HD, width),
+        (held * half_in, 0, 0),
+    )
+    grads = jnp.concatenate(
+        [
+            jnp.concatenate([grad_qkv_w.astype(bf16), grad_up_w.astype(bf16)], axis=-1).reshape(nd, n1, width),
+            grad_down_w.astype(bf16).reshape(nd, units, width),
+            out_slots,
+            to_rows(vector_grad),
+        ],
+        axis=1,
+    )
+    summed = jnp.sum(lax.all_to_all(grads, "dp", 0, 0, tiled=True).astype(f32), axis=0)
+    down_weight_grad = summed[n1:n2]
+    head_rows = jnp.where(target, summed[n2:n3], 0)
+    strip_grad = lax.dynamic_update_slice(jnp.zeros((5 * rows, width), f32), head_rows, (begin, 0))
+    strip_grad = strip_grad.astype(bf16).reshape(5, rows, width)
+    out_weight_grad = strip_grad[2].astype(f32)
+    out_weight_grad += between(strip_grad[1], 1, None).astype(f32)
+    out_weight_grad += between(strip_grad[3], -1, None).astype(f32)
+    out_weight_grad += between(jnp.where(in_lower, strip_grad[4], strip_grad[0]), 0, [-t for t in two]).astype(f32)
+    back = jnp.concatenate(
+        [
+            summed[:n1].astype(bf16).reshape(nc, rows, width),
+            jnp.pad(to_rows(summed[n3:, :nv] + summed[n3:, nv : 2 * nv])[:, None], ((0, 0), (0, 7), (0, 0))),
+        ],
+        axis=1,
+    )
+    back = lax.all_to_all(back, "ctx", 0, 0, tiled=True)
+    qkv_back = back[:, :rows, : 3 * cols]
+    qkv_back = jnp.pad(qkv_back, ((0, 3 * per_d - nc), (0, 0), (0, 0))).reshape(per_d, 3, rows, 3, held, HD)[:, :2]
+    qkv_weight_grad = qkv_back.transpose(2, 3, 1, 4, 0, 5).reshape(rows, 3 * width).astype(f32)
+    up_weight_grad = (
+        back[:, :rows, 3 * cols :].reshape(nc, rows, nd, units).transpose(1, 2, 0, 3).reshape(rows, nc * ff).astype(f32)
+    )
+    vec = jnp.sum(from_rows(back[:, rows]), axis=0)
+    at = nb + nu
+    small = [vec[at + k * rows : at + (k + 1) * rows] for k in range(5)]
+    return (
+        mixed[None],
+        tokens_grad[None],
+        qkv_weight_grad,
+        vec[:nb],
+        out_weight_grad,
+        small[0],
+        up_weight_grad,
+        vec[nb:at],
+        down_weight_grad,
+        small[0],
+        small[1],
+        small[2],
+        small[3],
+        small[4],
+    )
+
+
+def head_split_fits(nd, nc, width):
+    heads = width // HD
+    return nd % 2 == 0 and heads == 3 * nd and nc == 8 and width // (nd * nc) * 8 == 3 * HD
+
+
+def per_device(tokens, *others):
+    nd, nc = lax.axis_size("dp"), lax.axis_size("ctx")
+    plan = head_split_plan if head_split_fits(nd, nc, tokens.shape[2]) else gathered_plan
+    return plan(tokens, *others)
+
+
 def solution(mesh):
     in_specs = (
         P("dp", "ctx", None),

time: 993 us -> 278 us (0.28)
  waiting for transfers between devices: 729 us -> 49 us
  blocking collectives: 97.2 us -> 28.4 us
  starting transfers between devices: 1.1 us -> 52.2 us
  matrix products: 80.3 us -> 39.8 us
  other arithmetic: 18 us -> 36.5 us
    reduce_scatter x5 -> x0, waiting for transfers between devices: 530 us -> none  [the longest x1 142 us: per_device(): lax.psum_scatter(grad_up_w, ('dp', 'ctx'), scatter_dimension=0, tiled=True)]
    all_gather x6 -> x1, waiting for transfers between devices: 196 us -> 0.01 us  [head_split_plan(): every = lax.all_gather(package, 'dp', axis=0, tiled=False)]
    unnamed x2 -> x0, blocking collectives: 82.9 us -> none
    ppermute x0 -> x22, waiting for transfers between devices: none -> 48.9 us  [the longest x16 45 us: swapped(): return lax.ppermute(x, 'ctx', [(i, i ^ bit) for i in range(size)])]
    dot_general x26 -> x17, matrix products: 80.3 us -> 31.7 us  [the longest x1 5.95 us: head_split_plan(): hidden_grad = jnp.dot(g_all, w_down.T, preferred_element_type=f32)]
    ppermute x0 -> x22, starting transfers between devices: none -> 41.1 us  [the longest x16 20.7 us: swapped(): return lax.ppermute(x, 'ctx', [(i, i ^ bit) for i in range(size)])]
    all_to_all x0 -> x1, blocking collectives: none -> 28.4 us  [head_split_plan(): lax.all_to_all(grads, 'dp', 0, 0, tiled=True).astype(f32)]
    all_gather x1 -> x0, blocking collectives: 14.3 us -> none  [per_device(): seg_all = lax.all_gather(segment_numbers, 'ctx', axis=1, tiled=True)]
  transfers between devices with their start and end apart: 11 -> 25, of which waited for: 11 -> 11; matrix products, arithmetic and copies ran while one was open for 14% -> 17% of each run, Pallas kernels for 0% -> 0%
where the time goes in v1:
time: 278 us; the launch traced here: 272 us
  starting transfers between devices  52.2 us (19%)
  local copies, waits for them, and re-layouts  51.3 us (18%)
  waiting for transfers between devices  49 us (18%)
  matrix products  39.8 us (14%)
  other arithmetic  36.5 us (13%)
  blocking collectives  28.4 us (10%)
  between operations  15.4 us (6%)
    ppermute x16, waiting for transfers between devices, swapped(): return lax.ppermute(x, 'ctx', [(i, i ^ bit) for i in range(size)])  45 us
    all_to_all x1, blocking collectives, head_split_plan(): lax.all_to_all(grads, 'dp', 0, 0, tiled=True).astype(f32)  28.4 us
    ppermute x16, starting transfers between devices, swapped(): return lax.ppermute(x, 'ctx', [(i, i ^ bit) for i in range(size)])  20.7 us
    ppermute x6, starting transfers between devices, between(): return lax.ppermute(x, ('dp', 'ctx'), pairs)  20.4 us
    unnamed x152, local copies, waits for them, and re-layouts  8.47 us
    sub x1, matrix products, head_split_plan(): weights = jnp.exp(scores - top)  8.08 us
    all_to_all x1, starting transfers between devices, head_split_plan(): back = lax.all_to_all(back, 'ctx', 0, 0, tiled=True)  6.75 us
    dot_general x1, matrix products, head_split_plan(): hidden_grad = jnp.dot(g_all, w_down.T, preferred_element_type=f32)  5.95 us
  transfers between devices with their start and end apart: 25, of which 11 were waited for; matrix products, arithmetic and copies ran while one was open for 17% of the time, Pallas kernels for 0%

profile of v1, /device:TPU:18, one launch (start us, length us, event | category | flops | bytes accessed | tf_op | source)
XLA Modules:
  0.0 272.4 jit_solution(5757745453965415865)
XLA Ops:
  7.2 1.6 collective-permute-start
  9.2 1.6 collective-permute-start.2
  10.7 4.4 %collective-permute-start.4 = (bf16[24,768]{1,0:T(8,128)(2,1)}, bf16[24,768]{1,0:T(8,128)(2,1)S(1)}, u32[]{:S(2)}, u32[]{:S(2)}) collective-permute-start(bf16[24,768]{1,0:T(8,128)(2,1)} %param.21), channel_id=1, source_target_pairs={{2,0},{3,1},{4,2},{5,3},{6,4},{7,5},{10,8},{11,9},{12,10},{13,11},... | collective-permute-start | bytes 110600 | tf_op jit(solution)/shard_map/ppermute | solution.py:392
  15.1 3.4 %collective-permute-start.5 = (bf16[24,768]{1,0:T(8,128)(2,1)}, bf16[24,768]{1,0:T(8,128)(2,1)S(1)}, u32[]{:S(2)}, u32[]{:S(2)}) collective-permute-start(bf16[24,768]{1,0:T(8,128)(2,1)} %param.21), channel_id=1, source_target_pairs={{0,1},{1,2},{2,3},{3,4},{4,5},{5,6},{6,7},{8,9},{9,10},{10,11},{11... | collective-permute-start | bytes 110600 | tf_op jit(solution)/shard_map/ppermute | solution.py:392
  19.2 5.4 %concatenate.63 = bf16[440]{0:T(512)(128)(2,1)S(1)} concatenate(bf16[72]{0:T(256)(128)(2,1)} %param.20, bf16[96]{0:T(256)(128)(2,1)} %param.24, bf16[24]{0:T(256)(128)(2,1)} %param.22, bf16[24]{0:T(256)(128)(2,1)} %param.26, bf16[24]{0:T(256)(128)(2,1)} %param.27, bf16[24]{0:T(256)(128)(2,1)} %param.28, bf16[24]{0:T(256)(128)(2,1)} %param.29, bf16[24]{0:T(256)(128)(2,1)} %param.30, ...), dimensions={0} | concatenate | bytes 1760 | tf_op jit(solution)/shard_map/concatenate | solution.py:441
  28.5 4.3 %all-to-all-start = ((bf16[8,32,768]{2,1,0:T(8,128)(2,1)}), bf16[8,32,768]{2,1,0:T(8,128)(2,1)S(1)}, u32[]{:S(2)}, u32[]{:S(2)}) async-start(bf16[8,32,768]{2,1,0:T(8,128)(2,1)} %pad_maximum_fusion.6), calls=%async_computation | async-start | bytes 786432 | tf_op jit(solution)/shard_map/all_to_all | solution.py:460
  34.5 3.4 %collective-permute-start.6 = (bf16[24,768]{1,0:T(8,128)(2,1)S(1)}, bf16[24,768]{1,0:T(8,128)(2,1)S(1)}, u32[]{:S(2)}, u32[]{:S(2)}) collective-permute-start(bf16[24,768]{1,0:T(8,128)(2,1)S(1)} %copy-done.44), channel_id=1, source_target_pairs={{1,0},{2,1},{3,2},{4,3},{5,4},{6,5},{7,6},{9,8},{10,9},{11,10},{12... | collective-permute-start | bytes 110600 | tf_op jit(solution)/shard_map/ppermute | solution.py:392
  37.9 1.5 collective-permute-start.11
  39.4 2.2 collective-permute-done.6
  43.7 1.7 collective-permute-start.13
  47.1 2.4 collective-permute-start.3
  49.5 5.4 %collective-permute-done.12 = bf16[128,768]{1,0:T(8,128)(2,1)} collective-permute-done((bf16[128,768]{1,0:T(8,128)(2,1)S(1)}, bf16[128,768]{1,0:T(8,128)(2,1)}, u32[]{:S(2)}, u32[]{:S(2)}) %collective-permute-start.12) | collective-permute-done | bytes 196640 | tf_op jit(solution)/shard_map/ppermute | solution.py:360
  54.9 3.0 %collective-permute-done.13 = bf16[128,768]{1,0:T(8,128)(2,1)S(1)} collective-permute-done((bf16[128,768]{1,0:T(8,128)(2,1)S(1)}, bf16[128,768]{1,0:T(8,128)(2,1)S(1)}, u32[]{:S(2)}, u32[]{:S(2)}) %collective-permute-start.13) | collective-permute-done | bytes 196640 | tf_op jit(solution)/shard_map/ppermute | solution.py:360
  65.1 1.8 collective-permute-done.3
  67.0 13.3 %collective-permute-done.14 = bf16[4,128,768]{2,1,0:T(8,128)(2,1)S(1)} collective-permute-done((bf16[4,128,768]{2,1,0:T(8,128)(2,1)S(1)}, bf16[4,128,768]{2,1,0:T(8,128)(2,1)S(1)}, u32[]{:S(2)}, u32[]{:S(2)}) %collective-permute-start.14) | collective-permute-done | bytes 786464 | tf_op jit(solution)/shard_map/ppermute | solution.py:360
  83.7 1.8 slice.309
  86.9 2.4 fusion.67
  93.7 2.9 %compare_and_fusion = pred[1024,1024]{0,1:T(8,128)(4,1)} fusion(f32[1024]{0:T(1024)S(1)} %bitcast_convert_fusion, s32[1024]{0:T(1024)} %add_bitcast_fusion), kind=kLoop, calls=%fused_computation.12 | loop fusion | flops 3145728 | bytes 1056768 | tf_op jit(solution)/shard_map/and | solution.py:515
  96.6 1.4 reshape.769
  98.8 1.4 reshape.773
  102.4 2.9 %add_convert_fusion.3 = (bf16[8,128,768]{2,1,0:T(8,128)(2,1)S(1)}, bf16[8,128,768]{2,1,0:T(8,128)(2,1)}) fusion(bf16[8,128,768]{2,1,0:T(8,128)(2,1)S(1)} %constant_dynamic-update-slice_fusion, f32[768]{0:T(1024)} %reshape.769, f32[768]{0:T(1024)S(1)} %reshape.768, f32[8,128]{1,0:T(8,128)} %get-tuple-element.87, f32[8,128]{1,0:T(8,128)} %copy-done.43, ...), kind=kLoop, calls=%fused_computation.23 | loop fusion | flops 7077888 | bytes 4739072 | tf_op jit(solution)/shard_map/convert_element_type | solution.py:507
  110.9 8.1 %fusion.72 = (f32[2,1024]{1,0:T(2,128)S(1)}, f32[2,1024,1024]{1,2,0:T(8,128)}) fusion(pred[1024,1024]{0,1:T(8,128)(4,1)} %compare_and_fusion, bf16[1024,2,48]{0,2,1:T(8,128)(2,1)} %slice.436, bf16[1024,2,8]{0,2,1:T(8,128)(2,1)} %get-tuple-element.76, bf16[1024,2,8]{0,2,1:T(8,128)(2,1)} %get-tuple-element.77, bf16[1024,2,48]{0,2,1:T(8,128)(2,1)} %slice.437, ...), kind=kOutput, calls=%fused_computation.212 | convolution fusion | flops 278397952 | bytes 9969664 | tf_op jit(solution)/shard_map/sub | solution.py:519
  119.0 4.8 %fusion.5 = bf16[2,1024,1024]{1,2,0:T(8,128)(2,1)S(1)} fusion(f32[2,1024,1024]{1,2,0:T(8,128)} %get-tuple-element.94, f32[2,1024]{1,0:T(2,128)S(1)} %get-tuple-element.93), kind=kLoop, calls=%fused_computation.13 | loop fusion | flops 4194304 | bytes 12591104 | tf_op jit(solution)/shard_map/convert_element_type | solution.py:521
  123.8 1.6 multiply_reduce_fusion.3
  125.4 1.4 fusion.17
  127.3 1.8 multiply_convert_fusion
  130.1 1.4 fusion.14
  131.7 1.9 slice.314
  134.7 2.6 fusion.74
  137.3 1.6 convolution_convert_fusion
  140.8 2.6 convolution_add_fusion
  143.6 6.0 %convert_reduce_fusion.3 = (f32[384]{0:T(512)}, bf16[1024,384]{1,0:T(8,128)(2,1)S(1)}, f32[1024,384]{1,0:T(8,128)}) fusion(f32[1024,384]{1,0:T(8,128)S(1)} %convolution_add_fusion, bf16[1024,768]{1,0:T(8,128)(2,1)S(1)} %bitcast.191, bf16[384,768]{1,0:T(8,128)(2,1)S(1)} %bitcast.208), kind=kOutput, calls=%fused_computation.31 | convolution fusion | flops 633077376 | bytes 6096384 | tf_op jit(solution)/shard_map/dot_general | solution.py:537
  149.6 3.6 %fusion.61 = (f32[768]{0:T(1024)}, f32[768]{0:T(1024)}, bf16[1024,768]{1,0:T(8,128)(2,1)S(1)}, f32[768]{0:T(1024)}, f32[768]{0:T(1024)}, /*index=5*/bf16[1024,768]{1,0:T(8,128)(2,1)}) fusion(f32[1024]{0:T(1024)S(1)} %copy-done.55, f32[1024]{0:T(1024)S(1)} %copy-done.54, bf16[8,128,768]{2,1,0:T(8,128)(2,1)S(1)} %constant_dynamic-update-slice_fusion, ...), kind=kOutput, calls=%fused_computation.204 | convolution fusion | flops 616559616 | bytes 9270272 | tf_op jit(solution)/shard_map/dot_general | solution.py:541
  155.9 2.1 multiply_convert_fusion.1
  165.3 2.5 convolution_convert_fusion.2
  168.9 2.4 copy.85
  174.0 1.6 convolution_convert_fusion.1
  177.8 3.8 %collective-permute-start.17 = (bf16[128,768]{1,0:T(8,128)(2,1)S(1)}, bf16[128,768]{1,0:T(8,128)(2,1)S(1)}, u32[]{:S(2)}, u32[]{:S(2)}) collective-permute-start(bf16[128,768]{1,0:T(8,128)(2,1)S(1)} %get-tuple-element.52), channel_id=1, source_target_pairs={{0,4},{1,5},{2,6},{3,7},{4,0},{5,1},{6,2},{7,3},{8,12},{9,13},{10,... | collective-permute-start | bytes 589832 | tf_op jit(solution)/shard_map/ppermute | solution.py:360
  181.5 6.2 %collective-permute-done.7 = bf16[4,128,768]{2,1,0:T(8,128)(2,1)} collective-permute-done((bf16[4,128,768]{2,1,0:T(8,128)(2,1)}, bf16[4,128,768]{2,1,0:T(8,128)(2,1)}, u32[]{:S(2)}, u32[]{:S(2)}) %collective-permute-start.7) | collective-permute-done | bytes 786464 | tf_op jit(solution)/shard_map/ppermute | solution.py:360
  189.1 2.3 collective-permute-start.10
  193.0 7.3 %collective-permute-done.17 = bf16[128,768]{1,0:T(8,128)(2,1)S(1)} collective-permute-done((bf16[128,768]{1,0:T(8,128)(2,1)S(1)}, bf16[128,768]{1,0:T(8,128)(2,1)S(1)}, u32[]{:S(2)}, u32[]{:S(2)}) %collective-permute-start.17) | collective-permute-done | bytes 196640 | tf_op jit(solution)/shard_map/ppermute | solution.py:360
  200.7 5.6 %collective-permute-done.10 = bf16[128,768]{1,0:T(8,128)(2,1)S(1)} collective-permute-done((bf16[128,768]{1,0:T(8,128)(2,1)S(1)}, bf16[128,768]{1,0:T(8,128)(2,1)S(1)}, u32[]{:S(2)}, u32[]{:S(2)}) %collective-permute-start.10) | collective-permute-done | bytes 196640 | tf_op jit(solution)/shard_map/ppermute | solution.py:360
  206.3 2.4 collective-permute-done.9
  211.2 28.4 %all_to_all.15 = bf16[4,360,768]{2,1,0:T(8,128)(2,1)S(1)} all-to-all(bf16[4,360,768]{2,1,0:T(8,128)(2,1)S(1)} %pad_maximum_fusion), channel_id=1, replica_groups=mesh['dp'=4,'ctx'=8] {'dp'}, dimensions={0} | all-to-all | bytes 4423680 | tf_op jit(solution)/shard_map/all_to_all | solution.py:612
  240.9 6.8 %all-to-all-start.2 = ((bf16[8,32,768]{2,1,0:T(8,128)(2,1)}), bf16[8,32,768]{2,1,0:T(8,128)(2,1)S(1)}, u32[]{:S(2)}, u32[]{:S(2)}) async-start(bf16[8,32,768]{2,1,0:T(8,128)(2,1)} %fusion.31), calls=%async_computation.2 | async-start | bytes 786432 | tf_op jit(solution)/shard_map/all_to_all | solution.py:628
  247.7 2.5 collective-permute-start.21
  250.2 3.4 %collective-permute-start.20 = (bf16[24,768]{1,0:T(8,128)(2,1)S(1)}, bf16[24,768]{1,0:T(8,128)(2,1)S(1)}, u32[]{:S(2)}, u32[]{:S(2)}) collective-permute-start(bf16[24,768]{1,0:T(8,128)(2,1)S(1)} %get-tuple-element.72), channel_id=1, source_target_pairs={{0,1},{1,2},{2,3},{3,4},{4,5},{5,6},{6,7},{8,9},{9,10},{10,11},{11... | collective-permute-start | bytes 110600 | tf_op jit(solution)/shard_map/ppermute | solution.py:392
  253.5 3.4 %collective-permute-start.19 = (bf16[24,768]{1,0:T(8,128)(2,1)S(1)}, bf16[24,768]{1,0:T(8,128)(2,1)S(1)}, u32[]{:S(2)}, u32[]{:S(2)}) collective-permute-start(bf16[24,768]{1,0:T(8,128)(2,1)S(1)} %get-tuple-element.71), channel_id=1, source_target_pairs={{1,0},{2,1},{3,2},{4,3},{5,4},{6,5},{7,6},{9,8},{10,9},{11,10},{12... | collective-permute-start | bytes 110600 | tf_op jit(solution)/shard_map/ppermute | solution.py:392
  (304 shorter events, 71.2 us)
Async XLA Ops:
  7.2 36.6 %collective-permute-start = (bf16[128,768]{1,0:T(8,128)(2,1)}, bf16[128,768]{1,0:T(8,128)(2,1)}, u32[]{:S(2)}, u32[]{:S(2)}) collective-permute-start(bf16[128,768]{1,0:T(8,128)(2,1)} %bitcast.194), channel_id=1, source_target_pairs={{0,2},{1,3},{2,0},{3,1},{4,6},{5,7},{6,4},{7,5},{8,10},{9,11},{10,... | collective-permute-start | bytes 589832 | tf_op jit(solution)/shard_map/ppermute | solution.py:360
  8.8 37.1 %collective-permute-start.1 = (bf16[128,768]{1,0:T(8,128)(2,1)}, bf16[128,768]{1,0:T(8,128)(2,1)}, u32[]{:S(2)}, u32[]{:S(2)}) collective-permute-start(bf16[128,768]{1,0:T(8,128)(2,1)} %bitcast.195), channel_id=1, source_target_pairs={{0,4},{1,5},{2,6},{3,7},{4,0},{5,1},{6,2},{7,3},{8,12},{9,13},{10,... | collective-permute-start | bytes 589832 | tf_op jit(solution)/shard_map/ppermute | solution.py:360
  9.2 36.8 %collective-permute-start.2 = (bf16[128,768]{1,0:T(8,128)(2,1)}, bf16[128,768]{1,0:T(8,128)(2,1)}, u32[]{:S(2)}, u32[]{:S(2)}) collective-permute-start(bf16[128,768]{1,0:T(8,128)(2,1)} %bitcast.196), channel_id=1, source_target_pairs={{0,6},{1,7},{2,4},{3,5},{4,2},{5,3},{6,0},{7,1},{8,14},{9,15},{10,... | collective-permute-start | bytes 589832 | tf_op jit(solution)/shard_map/ppermute | solution.py:360
  10.7 23.7 %collective-permute-start.4 = (bf16[24,768]{1,0:T(8,128)(2,1)}, bf16[24,768]{1,0:T(8,128)(2,1)S(1)}, u32[]{:S(2)}, u32[]{:S(2)}) collective-permute-start(bf16[24,768]{1,0:T(8,128)(2,1)} %param.21), channel_id=1, source_target_pairs={{2,0},{3,1},{4,2},{5,3},{6,4},{7,5},{10,8},{11,9},{12,10},{13,11},... | collective-permute-start | bytes 110600 | tf_op jit(solution)/shard_map/ppermute | solution.py:392
  15.1 22.7 %collective-permute-start.5 = (bf16[24,768]{1,0:T(8,128)(2,1)}, bf16[24,768]{1,0:T(8,128)(2,1)S(1)}, u32[]{:S(2)}, u32[]{:S(2)}) collective-permute-start(bf16[24,768]{1,0:T(8,128)(2,1)} %param.21), channel_id=1, source_target_pairs={{0,1},{1,2},{2,3},{3,4},{4,5},{5,6},{6,7},{8,9},{9,10},{10,11},{11... | collective-permute-start | bytes 110600 | tf_op jit(solution)/shard_map/ppermute | solution.py:392
  27.6 6.8 %copy-start.44 = (bf16[24,768]{1,0:T(8,128)(2,1)S(1)}, bf16[24,768]{1,0:T(8,128)(2,1)}, u32[]{:S(2)}) copy-start(bf16[24,768]{1,0:T(8,128)(2,1)} %param.21) | copy-start | bytes 110596
  27.6 10.2 %copy-start.15 = (bf16[1,128,768]{2,1,0:T(8,128)(2,1)S(1)}, bf16[1,128,768]{2,1,0:T(8,128)(2,1)}, u32[]{:S(2)}) copy-start(bf16[1,128,768]{2,1,0:T(8,128)(2,1)} %param.18) | copy-start | bytes 589828
  28.5 13.2 %copy-start.32 = (bf16[96,768]{1,0:T(8,128)(2,1)S(1)}, bf16[96,768]{1,0:T(8,128)(2,1)}, u32[]{:S(2)}) copy-start(bf16[96,768]{1,0:T(8,128)(2,1)} %param.25) | copy-start | bytes 442372
  28.5 13.2 %all-to-all-start = ((bf16[8,32,768]{2,1,0:T(8,128)(2,1)}), bf16[8,32,768]{2,1,0:T(8,128)(2,1)S(1)}, u32[]{:S(2)}, u32[]{:S(2)}) async-start(bf16[8,32,768]{2,1,0:T(8,128)(2,1)} %pad_maximum_fusion.6), calls=%async_computation | async-start | bytes 786432 | tf_op jit(solution)/shard_map/all_to_all | solution.py:460
  32.8 50.1 %all-gather.3.cloned.1.call-start = ((), (), s32[]{:S(2)}) async-start(), calls=%async_computation.3 | async-start | bytes 2764800 | tf_op jit(solution)/shard_map/all_gather | solution.py:474
  33.5 8.1 %copy-start.61 = (s32[8]{0:T(128)}, s32[8]{0:T(128)S(1)}, u32[]{:S(2)}) copy-start(s32[8]{0:T(128)S(1)} %xor_multiply_fusion) | copy-start | bytes 100
  33.5 8.1 %copy-start.52 = (f32[128]{0:T(128)}, f32[128]{0:T(128)S(1)}, u32[]{:S(2)}) copy-start(f32[128]{0:T(128)S(1)} %broadcast_multiply_fusion.2) | copy-start | bytes 1540
  34.5 7.1 %collective-permute-start.6 = (bf16[24,768]{1,0:T(8,128)(2,1)S(1)}, bf16[24,768]{1,0:T(8,128)(2,1)S(1)}, u32[]{:S(2)}, u32[]{:S(2)}) collective-permute-start(bf16[24,768]{1,0:T(8,128)(2,1)S(1)} %copy-done.44), channel_id=1, source_target_pairs={{1,0},{2,1},{3,2},{4,3},{5,4},{6,5},{7,6},{9,8},{10,9},{11,10},{12... | collective-permute-start | bytes 110600 | tf_op jit(solution)/shard_map/ppermute | solution.py:392
  37.9 11.6 %collective-permute-start.11 = (bf16[128,768]{1,0:T(8,128)(2,1)S(1)}, bf16[128,768]{1,0:T(8,128)(2,1)}, u32[]{:S(2)}, u32[]{:S(2)}) collective-permute-start(bf16[128,768]{1,0:T(8,128)(2,1)S(1)} %bitcast.217), channel_id=1, source_target_pairs={{0,2},{1,3},{2,0},{3,1},{4,6},{5,7},{6,4},{7,5},{8,10},{9,11},{10,... | collective-permute-start | bytes 589832 | tf_op jit(solution)/shard_map/ppermute | solution.py:360
  41.6 13.3 %collective-permute-start.12 = (bf16[128,768]{1,0:T(8,128)(2,1)S(1)}, bf16[128,768]{1,0:T(8,128)(2,1)}, u32[]{:S(2)}, u32[]{:S(2)}) collective-permute-start(bf16[128,768]{1,0:T(8,128)(2,1)S(1)} %bitcast.218), channel_id=1, source_target_pairs={{0,4},{1,5},{2,6},{3,7},{4,0},{5,1},{6,2},{7,3},{8,12},{9,13},{10,... | collective-permute-start | bytes 589832 | tf_op jit(solution)/shard_map/ppermute | solution.py:360
  43.7 14.2 %collective-permute-start.13 = (bf16[128,768]{1,0:T(8,128)(2,1)S(1)}, bf16[128,768]{1,0:T(8,128)(2,1)S(1)}, u32[]{:S(2)}, u32[]{:S(2)}) collective-permute-start(bf16[128,768]{1,0:T(8,128)(2,1)S(1)} %bitcast.219), channel_id=1, source_target_pairs={{0,6},{1,7},{2,4},{3,5},{4,2},{5,3},{6,0},{7,1},{8,14},{9,15},{10,... | collective-permute-start | bytes 589832 | tf_op jit(solution)/shard_map/ppermute | solution.py:360
  47.1 19.8 %collective-permute-start.3 = (bf16[4,128,768]{2,1,0:T(8,128)(2,1)S(1)}, bf16[4,128,768]{2,1,0:T(8,128)(2,1)S(1)}, u32[]{:S(2)}, u32[]{:S(2)}) collective-permute-start(bf16[4,128,768]{2,1,0:T(8,128)(2,1)S(1)} %pad_maximum_fusion.2), channel_id=1, source_target_pairs={{0,1},{1,0},{2,3},{3,2},{4,5},{5,4},{6,7},{7,6},{8,9},{9,8},{10,11... | collective-permute-start | bytes 2359304 | tf_op jit(solution)/shard_map/ppermute | solution.py:360
  59.0 21.2 %collective-permute-start.14 = (bf16[4,128,768]{2,1,0:T(8,128)(2,1)S(1)}, bf16[4,128,768]{2,1,0:T(8,128)(2,1)S(1)}, u32[]{:S(2)}, u32[]{:S(2)}) collective-permute-start(bf16[4,128,768]{2,1,0:T(8,128)(2,1)S(1)} %pad_maximum_fusion.3), channel_id=1, source_target_pairs={{0,1},{1,0},{2,3},{3,2},{4,5},{5,4},{6,7},{7,6},{8,9},{9,8},{10,11... | collective-permute-start | bytes 2359304 | tf_op jit(solution)/shard_map/ppermute | solution.py:360
  98.8 6.4 %copy-start.47 = (f32[768]{0:T(1024)}, f32[768]{0:T(1024)S(1)}, u32[]{:S(2)}) copy-start(f32[768]{0:T(1024)S(1)} %reshape.768) | copy-start | bytes 9220
  143.5 6.0 %copy-start.20 = (f32[1024,384]{1,0:T(8,128)}, f32[1024,384]{1,0:T(8,128)S(1)}, u32[]{:S(2)}) copy-start(f32[1024,384]{1,0:T(8,128)S(1)} %convolution_add_fusion) | copy-start | bytes 4718596
  143.5 6.0 %copy-start.5 = (f32[1024,768]{1,0:T(8,128)S(1)}, f32[1024,768]{1,0:T(8,128)}, u32[]{:S(2)}) copy-start(f32[1024,768]{1,0:T(8,128)} %fusion.74) | copy-start | bytes 9437188
  143.5 6.0 %copy-start.24 = (bf16[4,192,384]{2,1,0:T(8,128)(2,1)S(1)}, bf16[4,192,384]{2,1,0:T(8,128)(2,1)}, u32[]{:S(2)}) copy-start(bf16[4,192,384]{2,1,0:T(8,128)(2,1)} %get-tuple-element.36) | copy-start | bytes 1769476
  143.5 6.0 %copy-start.46 = (f32[768]{0:T(1024)S(1)}, f32[768]{0:T(1024)}, u32[]{:S(2)}) copy-start(f32[768]{0:T(1024)} %reshape.772) | copy-start | bytes 9220
  143.5 6.0 %copy-start.48 = (f32[768]{0:T(1024)S(1)}, f32[768]{0:T(1024)}, u32[]{:S(2)}) copy-start(f32[768]{0:T(1024)} %copy-done.47) | copy-start | bytes 9220
  143.5 6.0 %copy-start.49 = (f32[768]{0:T(1024)S(1)}, f32[768]{0:T(1024)}, u32[]{:S(2)}) copy-start(f32[768]{0:T(1024)} %reshape.773) | copy-start | bytes 9220
  154.5 21.2 %collective-permute-start.15 = (bf16[4,128,768]{2,1,0:T(8,128)(2,1)}, bf16[4,128,768]{2,1,0:T(8,128)(2,1)}, u32[]{:S(2)}, u32[]{:S(2)}) collective-permute-start(bf16[4,128,768]{2,1,0:T(8,128)(2,1)} %bitcast.49), channel_id=1, source_target_pairs={{0,1},{1,0},{2,3},{3,2},{4,5},{5,4},{6,7},{7,6},{8,9},{9,8},{10,11... | collective-permute-start | bytes 2359304 | tf_op jit(solution)/shard_map/ppermute | solution.py:360
  161.0 26.7 %collective-permute-start.7 = (bf16[4,128,768]{2,1,0:T(8,128)(2,1)}, bf16[4,128,768]{2,1,0:T(8,128)(2,1)}, u32[]{:S(2)}, u32[]{:S(2)}) collective-permute-start(bf16[4,128,768]{2,1,0:T(8,128)(2,1)} %bitcast.27), channel_id=1, source_target_pairs={{0,1},{1,0},{2,3},{3,2},{4,5},{5,4},{6,7},{7,6},{8,9},{9,8},{10,11... | collective-permute-start | bytes 2359304 | tf_op jit(solution)/shard_map/ppermute | solution.py:360
  177.0 10.7 %copy-start.6 = (bf16[512,768]{1,0:T(8,128)(2,1)S(1)}, bf16[512,768]{1,0:T(8,128)(2,1)}, u32[]{:S(2)}) copy-start(bf16[512,768]{1,0:T(8,128)(2,1)} %get-tuple-element.46) | copy-start | bytes 2359300
  177.1 15.0 %collective-permute-start.18 = (bf16[128,768]{1,0:T(8,128)(2,1)S(1)}, bf16[128,768]{1,0:T(8,128)(2,1)S(1)}, u32[]{:S(2)}, u32[]{:S(2)}) collective-permute-start(bf16[128,768]{1,0:T(8,128)(2,1)S(1)} %get-tuple-element.51), channel_id=1, source_target_pairs={{0,6},{1,7},{2,4},{3,5},{4,2},{5,3},{6,0},{7,1},{8,14},{9,15},{10,... | collective-permute-start | bytes 589832 | tf_op jit(solution)/shard_map/ppermute | solution.py:360
  177.8 22.6 %collective-permute-start.17 = (bf16[128,768]{1,0:T(8,128)(2,1)S(1)}, bf16[128,768]{1,0:T(8,128)(2,1)S(1)}, u32[]{:S(2)}, u32[]{:S(2)}) collective-permute-start(bf16[128,768]{1,0:T(8,128)(2,1)S(1)} %get-tuple-element.52), channel_id=1, source_target_pairs={{0,4},{1,5},{2,6},{3,7},{4,0},{5,1},{6,2},{7,3},{8,12},{9,13},{10,... | collective-permute-start | bytes 589832 | tf_op jit(solution)/shard_map/ppermute | solution.py:360
  181.5 18.8 %collective-permute-start.16 = (bf16[128,768]{1,0:T(8,128)(2,1)S(1)}, bf16[128,768]{1,0:T(8,128)(2,1)S(1)}, u32[]{:S(2)}, u32[]{:S(2)}) collective-permute-start(bf16[128,768]{1,0:T(8,128)(2,1)S(1)} %get-tuple-element.50), channel_id=1, source_target_pairs={{0,2},{1,3},{2,0},{3,1},{4,6},{5,7},{6,4},{7,5},{8,10},{9,11},{10,... | collective-permute-start | bytes 589832 | tf_op jit(solution)/shard_map/ppermute | solution.py:360
  187.7 12.7 %copy-start.53 = (f32[128]{0:T(128)S(1)}, f32[128]{0:T(128)}, u32[]{:S(2)}) copy-start(f32[128]{0:T(128)} %copy-done.52) | copy-start | bytes 1540
  187.7 12.7 %copy-start.60 = (f32[128]{0:T(128)S(1)}, f32[128]{0:T(128)}, u32[]{:S(2)}) copy-start(f32[128]{0:T(128)} %add_rsqrt_fusion.1) | copy-start | bytes 1540
  189.1 19.6 %copy-start.45 = (f32[768]{0:T(1024)S(1)}, f32[768]{0:T(1024)}, u32[]{:S(2)}) copy-start(f32[768]{0:T(1024)} %add.272) | copy-start | bytes 9220
  189.1 17.2 %collective-permute-start.10 = (bf16[128,768]{1,0:T(8,128)(2,1)S(1)}, bf16[128,768]{1,0:T(8,128)(2,1)S(1)}, u32[]{:S(2)}, u32[]{:S(2)}) collective-permute-start(bf16[128,768]{1,0:T(8,128)(2,1)S(1)} %get-tuple-element.54), channel_id=1, source_target_pairs={{0,6},{1,7},{2,4},{3,5},{4,2},{5,3},{6,0},{7,1},{8,14},{9,15},{10,... | collective-permute-start | bytes 589832 | tf_op jit(solution)/shard_map/ppermute | solution.py:360
  191.5 17.2 %collective-permute-start.9 = (bf16[128,768]{1,0:T(8,128)(2,1)S(1)}, bf16[128,768]{1,0:T(8,128)(2,1)S(1)}, u32[]{:S(2)}, u32[]{:S(2)}) collective-permute-start(bf16[128,768]{1,0:T(8,128)(2,1)S(1)} %get-tuple-element.55), channel_id=1, source_target_pairs={{0,4},{1,5},{2,6},{3,7},{4,0},{5,1},{6,2},{7,3},{8,12},{9,13},{10,... | collective-permute-start | bytes 589832 | tf_op jit(solution)/shard_map/ppermute | solution.py:360
  192.1 16.6 %collective-permute-start.8 = (bf16[128,768]{1,0:T(8,128)(2,1)S(1)}, bf16[128,768]{1,0:T(8,128)(2,1)S(1)}, u32[]{:S(2)}, u32[]{:S(2)}) collective-permute-start(bf16[128,768]{1,0:T(8,128)(2,1)S(1)} %get-tuple-element.53), channel_id=1, source_target_pairs={{0,2},{1,3},{2,0},{3,1},{4,6},{5,7},{6,4},{7,5},{8,10},{9,11},{10,... | collective-permute-start | bytes 589832 | tf_op jit(solution)/shard_map/ppermute | solution.py:360
  200.4 9.4 %copy-start.37 = (f32[4,8,24]{2,1,0:T(8,128)S(1)}, f32[4,8,24]{2,1,0:T(8,128)}, u32[]{:S(2)}) copy-start(f32[4,8,24]{2,1,0:T(8,128)} %reshape.763) | copy-start | bytes 9220
  200.4 9.4 %copy-start.38 = (f32[4,8,24]{2,1,0:T(8,128)S(1)}, f32[4,8,24]{2,1,0:T(8,128)}, u32[]{:S(2)}) copy-start(f32[4,8,24]{2,1,0:T(8,128)} %reshape.764) | copy-start | bytes 9220
  200.4 9.4 %copy-start.39 = (f32[4,8,24]{2,1,0:T(8,128)S(1)}, f32[4,8,24]{2,1,0:T(8,128)}, u32[]{:S(2)}) copy-start(f32[4,8,24]{2,1,0:T(8,128)} %reshape.765) | copy-start | bytes 9220
  200.4 9.4 %copy-start.40 = (f32[4,8,72]{2,1,0:T(8,128)S(1)}, f32[4,8,72]{2,1,0:T(8,128)}, u32[]{:S(2)}) copy-start(f32[4,8,72]{2,1,0:T(8,128)} %reshape.759) | copy-start | bytes 27652
  200.4 9.4 %copy-start.42 = (f32[4,8,96]{2,1,0:T(8,128)S(1)}, f32[4,8,96]{2,1,0:T(8,128)}, u32[]{:S(2)}) copy-start(f32[4,8,96]{2,1,0:T(8,128)} %copy-done.41) | copy-start | bytes 36868
  200.7 9.3 %copy-start.2 = (bf16[768,768]{1,0:T(8,128)(2,1)S(1)}, bf16[768,768]{1,0:T(8,128)(2,1)}, u32[]{:S(2)}) copy-start(bf16[768,768]{1,0:T(8,128)(2,1)} %copy.85) | copy-start | bytes 3538948
  200.7 9.3 %copy-start.12 = (bf16[384,768]{1,0:T(8,128)(2,1)S(1)}, bf16[384,768]{1,0:T(8,128)(2,1)}, u32[]{:S(2)}) copy-start(bf16[384,768]{1,0:T(8,128)(2,1)} %convolution_convert_fusion.1) | copy-start | bytes 1769476
  240.9 19.2 %all-to-all-start.2 = ((bf16[8,32,768]{2,1,0:T(8,128)(2,1)}), bf16[8,32,768]{2,1,0:T(8,128)(2,1)S(1)}, u32[]{:S(2)}, u32[]{:S(2)}) async-start(bf16[8,32,768]{2,1,0:T(8,128)(2,1)} %fusion.31), calls=%async_computation.2 | async-start | bytes 786432 | tf_op jit(solution)/shard_map/all_to_all | solution.py:628
  247.7 10.0 %collective-permute-start.21 = (bf16[24,768]{1,0:T(8,128)(2,1)S(1)}, bf16[24,768]{1,0:T(8,128)(2,1)S(1)}, u32[]{:S(2)}, u32[]{:S(2)}) collective-permute-start(bf16[24,768]{1,0:T(8,128)(2,1)S(1)} %get-tuple-element.73), channel_id=1, source_target_pairs={{0,2},{1,3},{2,4},{3,5},{4,6},{5,7},{8,10},{9,11},{10,12},{11,13},... | collective-permute-start | bytes 110600 | tf_op jit(solution)/shard_map/ppermute | solution.py:392
  250.2 8.8 %collective-permute-start.20 = (bf16[24,768]{1,0:T(8,128)(2,1)S(1)}, bf16[24,768]{1,0:T(8,128)(2,1)S(1)}, u32[]{:S(2)}, u32[]{:S(2)}) collective-permute-start(bf16[24,768]{1,0:T(8,128)(2,1)S(1)} %get-tuple-element.72), channel_id=1, source_target_pairs={{0,1},{1,2},{2,3},{3,4},{4,5},{5,6},{6,7},{8,9},{9,10},{10,11},{11... | collective-permute-start | bytes 110600 | tf_op jit(solution)/shard_map/ppermute | solution.py:392
  253.5 5.9 %collective-permute-start.19 = (bf16[24,768]{1,0:T(8,128)(2,1)S(1)}, bf16[24,768]{1,0:T(8,128)(2,1)S(1)}, u32[]{:S(2)}, u32[]{:S(2)}) collective-permute-start(bf16[24,768]{1,0:T(8,128)(2,1)S(1)} %get-tuple-element.71), channel_id=1, source_target_pairs={{1,0},{2,1},{3,2},{4,3},{5,4},{6,5},{7,6},{9,8},{10,9},{11,10},{12... | collective-permute-start | bytes 110600 | tf_op jit(solution)/shard_map/ppermute | solution.py:392
  (45 other events, 114.9 us)
Sparse Core Ops, SparseCore 0:
  42.7 25.6 all-gather.2

commit v2 on v0

--- a/solution.py
+++ b/solution.py
@@ -3,7 +3,10 @@
 
 import jax
 import jax.numpy as jnp
+import numpy as np
 from jax import lax
+from jax.experimental import pallas as pl
+from jax.experimental.pallas import tpu as pltpu
 from jax.sharding import PartitionSpec as P
 
 HD = 64
@@ -63,7 +66,7 @@
     return (score_matrix, allowed_pairs[:, None])
 
 
-def per_device(
+def gathered_plan(
     tokens,
     segment_numbers,
     cotangent,
@@ -355,6 +358,579 @@
     return (mixed, tokens_grad) + tuple(shards)
 
 
+VMEM_LIMIT = 56 * 1024 * 1024
+NT = (((1,), (1,)), ((), ()))
+TN = (((0,), (0,)), ((), ()))
+NN = (((1,), (0,)), ((), ()))
+
+
+def mm(a, b, dims=NN):
+    return lax.dot_general(a, b, dims, preferred_element_type=jnp.float32)
+
+
+def vmem(count):
+    return [pl.BlockSpec(memory_space=pltpu.VMEM)] * count
+
+
+def call(kernel, outs, operands, scratch=(), flops=0, smem=True):
+    specs = vmem(len(operands))
+    if smem:
+        specs[0] = pl.BlockSpec(memory_space=pltpu.SMEM)
+    size = sum(math.prod(o.shape) * o.dtype.itemsize for o in list(outs) + list(operands))
+    return pl.pallas_call(
+        kernel,
+        out_shape=[jax.ShapeDtypeStruct(o.shape, o.dtype) for o in outs],
+        in_specs=specs,
+        out_specs=vmem(len(outs)),
+        scratch_shapes=list(scratch),
+        compiler_params=pltpu.CompilerParams(vmem_limit_bytes=VMEM_LIMIT),
+        cost_estimate=pl.CostEstimate(flops=flops, bytes_accessed=size, transcendentals=0),
+    )(*operands)
+
+
+def like(shape, dtype):
+    return jax.ShapeDtypeStruct(shape, dtype)
+
+
+def slot_order(size):
+    return list(range(0, size, 2)) + list(range(1, size, 2))
+
+
+def swapped(x, bit):
+    size = lax.axis_size("ctx")
+    return lax.ppermute(x, "ctx", [(i, i ^ bit) for i in range(size)])
+
+
+def gather_slots(x):
+    size = lax.axis_size("ctx")
+    near = jnp.stack([x] + [swapped(x, bit) for bit in range(2, size, 2)])
+    return near, swapped(near, 1)
+
+
+def reduce_slots(near, far):
+    near = near.astype(jnp.float32) + swapped(far, 1).astype(jnp.float32)
+    low = near.astype(jnp.bfloat16)
+    total = near[0]
+    for number in range(1, near.shape[0]):
+        total = total + swapped(low[number], 2 * number).astype(jnp.float32)
+    return total
+
+
+def between(x, offset):
+    nd, nc = lax.axis_size("dp"), lax.axis_size("ctx")
+    pairs = [
+        (d * nc + c + offset[d], d * nc + c)
+        for d in range(nd)
+        for c in range(nc)
+        if 0 <= c + offset[d] < nc
+    ]
+    return lax.ppermute(x, ("dp", "ctx"), pairs)
+
+
+def iota(shape, dim):
+    return lax.broadcasted_iota(jnp.int32, shape, dim)
+
+
+def message_kernel(per_d, nd, nc, units, qkv, up, vectors, out):
+    f32 = jnp.float32
+    rows = qkv.shape[0]
+    width = qkv.shape[1] // 3
+    held = nd // 2
+    w = qkv[...].astype(f32)
+    u = up[...].astype(f32)
+    v = vectors[...].astype(f32)
+    for t in range(nc):
+        group, half = t // 3, t % 3
+        pieces = []
+        for part in range(3):
+            for k in range(held):
+                at = part * width + HD * (per_d * (held * half + k) + group)
+                pieces.append(w[:, at : at + HD] if half < 2 else jnp.zeros((rows, HD), f32))
+        for k in range(nd):
+            at = k * nc * units + t * units
+            pieces.append(u[:, at : at + units])
+        out[t] = jnp.concatenate(pieces + [v], axis=1).astype(out.dtype)
+
+
+def tables_kernel(arrived, freq, cosine, sine, begin):
+    f32 = jnp.float32
+    nc, rows, lanes = arrived.shape
+    block = 128
+    head = arrived[:, :, lanes - block :].astype(f32)
+    seg = jnp.sum(jnp.where(iota((nc, rows, block), 1) == 8, head, 0.0), axis=1)
+    row = jnp.concatenate([seg[b : b + 1] for b in range(nc)], axis=1)
+    eye = iota((block, block), 0) == iota((block, block), 1)
+    feature = iota((block, block), 1) % HD
+    for b in range(nc):
+        col = jnp.sum(jnp.where(eye, seg[b : b + 1], 0.0), axis=1, keepdims=True)
+        start = jnp.sum(jnp.where(row < col, 1.0, 0.0), axis=1, keepdims=True)
+        index = (iota((block, 1), 0) + b * block).astype(f32)
+        angle = (index - start) * freq[...]
+        at = pl.ds(b * block, block)
+        cosine[at, :] = jnp.where(feature < ROT, jnp.cos(angle), 1.0)
+        sign = jnp.where(feature < ROT // 2, -1.0, jnp.where(feature < ROT, 1.0, 0.0))
+        sine[at, :] = sign * jnp.sin(angle)
+        begin[at, :] = jnp.broadcast_to(start, (block, block))
+
+
+def turned(t, cosine, sine):
+    lanes = t.shape[1]
+    early = iota(t.shape, 1) % HD < ROT // 2
+    other = jnp.where(early, pltpu.roll(t, lanes - ROT // 2, 1), pltpu.roll(t, ROT // 2, 1))
+    return t * cosine + other * sine
+
+
+def allowed_pairs(begin, first_row, rows, keys):
+    key_index = iota((rows, keys), 1)
+    query_index = iota((rows, keys), 0) + first_row
+    return (key_index <= query_index) & (key_index >= begin.astype(jnp.int32))
+
+
+def head_lanes(shape, h):
+    lane = iota(shape, 1)
+    return (lane >= h * HD) & (lane < (h + 1) * HD)
+
+
+def column_places(meta, nb, cols, width, per_d, held):
+    j = iota((1, 3 * cols), 1)
+    part = jnp.where(j >= 2 * cols, 2, jnp.where(j >= cols, 1, 0))
+    rest = j - part * cols
+    hh = jnp.zeros_like(rest)
+    for k in range(1, held):
+        hh = hh + jnp.where(rest >= k * HD, 1, 0)
+    column = part * width + hh * (per_d * HD) + (rest - hh * HD)
+    column = column + HD * (per_d * held * meta[8] + meta[9])
+    owner = jnp.floor((column.astype(jnp.float32) + 0.5) / nb).astype(jnp.int32)
+    return owner, column - owner * nb
+
+
+def forward_kernel(
+    sizes, meta, near, far, every, down, outs, cosine, sine, begin, own24, pick24, own96, pick96,
+    part_near, part_far, first_in, second_in, normed, query, key, value, attended, stats, hidden, slope, vecs,
+):
+    f32, bf16 = jnp.float32, jnp.bfloat16
+    nd, nc, per_d, held, nb, rows = sizes
+    block, width = near.shape[1], near.shape[2]
+    cols = held * HD
+    ff = down.shape[0]
+    length = nc * block
+    total = nd * nc
+    packed = every[:, :, 3 * cols + ff :].astype(f32).reshape(total, rows, block)
+    kind = iota(packed.shape, 1)
+
+    def of_kind(k):
+        return jnp.sum(jnp.where(kind == k, packed, 0.0), axis=1).astype(bf16)
+
+    owner = iota((total, width), 0)
+    kept = owner == own24[...]
+    flat = []
+    for k in range(2, 8):
+        flat.append(jnp.sum(jnp.where(kept, mm(of_kind(k), pick24[...]), 0.0), axis=0, keepdims=True))
+    out_bias, g_one, s_one, g_two, s_two = flat[0] + flat[1], flat[2], flat[3], flat[4], flat[5]
+    up_owner = iota((total, ff), 0) == own96[...] * nc + meta[10]
+    b_up = jnp.sum(jnp.where(up_owner, mm(of_kind(1), pick96[...]), 0.0), axis=0, keepdims=True)
+    col_owner, col_place = column_places(meta, nb, cols, width, per_d, held)
+    col_pick = (iota((block, 3 * cols), 0) == col_place).astype(f32).astype(bf16)
+    b_qkv = jnp.where(iota((total, 3 * cols), 0) == col_owner, mm(of_kind(0), col_pick), 0.0)
+    b_qkv = jnp.sum(b_qkv, axis=0, keepdims=True) * meta[11].astype(f32)
+    for k, vector in enumerate((g_one, s_one, g_two, s_two, out_bias)):
+        vecs[k : k + 1, :] = vector
+    for i in range(nc):
+        half = near if i < nc // 2 else far
+        x = half[i % (nc // 2)].astype(f32)
+        centered = x - jnp.mean(x, axis=1, keepdims=True)
+        n = centered * lax.rsqrt(jnp.mean(centered * centered, axis=1, keepdims=True) + eps)
+        at = pl.ds(pl.multiple_of(meta[i] * block, block), block)
+        normed[at, :] = n.astype(bf16)
+        first_in[at, :] = (n * g_one + s_one).astype(bf16)
+        second_in[at, :] = (n * g_two + s_two).astype(bf16)
+    w_qkv = every[:, :, : 3 * cols].reshape(width, 3 * cols)
+    w_up = every[:, :, 3 * cols : 3 * cols + ff].reshape(width, ff)
+    step = 2 * block
+    for b in range(length // step):
+        at = pl.ds(b * step, step)
+        t = mm(first_in[at, :], w_qkv) + b_qkv
+        query[at, :] = (turned(t[:, :cols], cosine[at, :], sine[at, :])).astype(bf16)
+        key[at, :] = turned(t[:, cols : 2 * cols], cosine[at, :], sine[at, :]).astype(bf16)
+        value[at, :] = t[:, 2 * cols :].astype(bf16)
+    for b in range(length // step):
+        at = pl.ds(b * step, step)
+        pre = mm(second_in[at, :], w_up) + b_up
+        cdf = 0.5 + 0.5 * lax.erf(pre * (0.5**0.5))
+        hidden[at, :] = (pre * cdf).astype(bf16)
+        slope[at, :] = (cdf + pre * jnp.exp(-0.5 * pre * pre) * ((2 * math.pi) ** -0.5)).astype(bf16)
+    for b in range(length // step):
+        at = pl.ds(b * step, step)
+        keys = (b + 1) * step
+        allowed = allowed_pairs(begin[at, 0:1], b * step, step, keys)
+        q = query[at, :]
+        result = jnp.zeros((step, cols), f32)
+        for h in range(held):
+            mine = head_lanes((step, cols), h)
+            s = mm(jnp.where(mine, q, jnp.zeros_like(q)), key[:keys, :], NT) * (HD**-0.5)
+            s = jnp.where(allowed, s, -1e30)
+            top = jnp.max(s, axis=1, keepdims=True)
+            p = jnp.exp(s - top)
+            inverse = 1.0 / jnp.sum(p, axis=1, keepdims=True)
+            result = jnp.where(mine, mm((p * inverse).astype(bf16), value[:keys, :]), result)
+            stats[at, 2 * h : 2 * h + 1] = top
+            stats[at, 2 * h + 1 : 2 * h + 2] = inverse
+        attended[at, :] = result
+    w_out = outs[pl.ds(held * meta[8], held)].reshape(cols, width)
+    for i in range(nc):
+        half = part_near if i < nc // 2 else part_far
+        at = pl.ds(pl.multiple_of(meta[i] * block, block), block)
+        part = mm(attended[at, :].astype(bf16), w_out) + mm(hidden[at, :], down[...])
+        half[i % (nc // 2)] = part.astype(bf16)
+
+
+def mlp_back_kernel(
+    sizes, meta, near, far, every, down, attended, hidden, slope, second_in, normed, vecs,
+    grads, part, g_all, sums, pre_grad,
+):
+    f32, bf16 = jnp.float32, jnp.bfloat16
+    nd, nc, per_d, held, nb, rows = sizes
+    block, width = near.shape[1], near.shape[2]
+    cols = held * HD
+    ff = down.shape[0]
+    length = nc * block
+    for i in range(nc):
+        half = near if i < nc // 2 else far
+        g_all[pl.ds(pl.multiple_of(meta[i] * block, block), block), :] = half[i % (nc // 2)]
+    g = g_all[...]
+    rows_d = width // nd
+    units = ff // nd
+    side = width // 2
+    grad_down = mm(hidden[...], g, TN).astype(bf16)
+    for d in range(nd):
+        piece = grad_down[d * units : (d + 1) * units]
+        grads[d, rows_d : rows_d + units, :] = piece[:, :side]
+        grads[d, rows_d + units : rows_d + 2 * units, :] = piece[:, side:]
+    grad_out = mm(attended[...].astype(bf16), g, TN)
+    base = rows_d + 2 * units
+    for d in range(nd):
+        here = (meta[8] == d // held) & (meta[11] == 1)
+        k = d % held
+        piece = jnp.where(here, grad_out[k * HD : (k + 1) * HD], 0.0).astype(bf16)
+        grads[d, base : base + HD, :] = piece[:, :side]
+        grads[d, base + HD : base + 2 * HD, :] = piece[:, side:]
+    step = 2 * block
+    w_up = every[:, :, 3 * cols : 3 * cols + ff].reshape(width, ff)
+    g_two = vecs[2:3, :]
+    up_sum = jnp.zeros((1, ff), f32)
+    gain_sum = jnp.zeros((1, width), f32)
+    shift_sum = jnp.zeros((1, width), f32)
+    for b in range(length // step):
+        at = pl.ds(b * step, step)
+        back = (mm(g_all[at, :], down[...], NT) * slope[at, :].astype(f32)).astype(bf16)
+        pre_grad[at, :] = back
+        up_sum += jnp.sum(back.astype(f32), axis=0, keepdims=True)
+        second = mm(back, w_up, NT)
+        gain_sum += jnp.sum(second * normed[at, :].astype(f32), axis=0, keepdims=True)
+        shift_sum += jnp.sum(second, axis=0, keepdims=True)
+        part[at, :] = (second * g_two).astype(bf16)
+    sums[0:1, :] = gain_sum
+    sums[1:2, :] = shift_sum
+    sums[2:3, :ff] = up_sum
+    grad_up = mm(second_in[...], pre_grad[...], TN).astype(bf16)
+    for d in range(nd):
+        grads[d, :rows_d, :] = grad_up[d * rows_d : (d + 1) * rows_d]
+
+
+def attention_back_kernel(
+    sizes, meta, g_all, every, outs, cosine, sine, begin, query, key, value, attended, stats, first_in, normed, vecs,
+    part, sums, own24, pick24, own96, pick96,
+    grads, part_near, part_far, d_out, d_query, d_key, d_value, d_qkv, first_grad,
+):
+    f32, bf16 = jnp.float32, jnp.bfloat16
+    nd, nc, per_d, held, nb, rows = sizes
+    length, width = g_all.shape
+    block = length // nc
+    cols = held * HD
+    ff = own96.shape[1]
+    total = nd * nc
+    w_out = outs[pl.ds(held * meta[8], held)].reshape(cols, width)
+    w_qkv = every[:, :, : 3 * cols].reshape(width, 3 * cols)
+    step = 2 * block
+    scale = HD**-0.5
+    d_key[...] = jnp.zeros_like(d_key)
+    d_value[...] = jnp.zeros_like(d_value)
+    for b in range(length // step):
+        at = pl.ds(b * step, step)
+        keys = (b + 1) * step
+        allowed = allowed_pairs(begin[at, 0:1], b * step, step, keys)
+        q = query[at, :]
+        back = mm(g_all[at, :], w_out, NT).astype(bf16)
+        product = back.astype(f32) * attended[at, :]
+        result = jnp.zeros((step, cols), f32)
+        for h in range(held):
+            mine = head_lanes((step, cols), h)
+            q_h = jnp.where(mine, q, jnp.zeros_like(q))
+            back_h = jnp.where(mine, back, jnp.zeros_like(back))
+            delta = jnp.sum(jnp.where(mine, product, 0.0), axis=1, keepdims=True)
+            s = mm(q_h, key[:keys, :], NT) * scale
+            p = jnp.exp(s - stats[at, 2 * h : 2 * h + 1]) * stats[at, 2 * h + 1 : 2 * h + 2]
+            p = jnp.where(allowed, p, 0.0)
+            d_p = mm(back_h, value[:keys, :], NT)
+            d_s = (p * (d_p - delta)).astype(bf16)
+            result = jnp.where(mine, mm(d_s, key[:keys, :]), result)
+            d_key[:keys, :] += mm(d_s, q_h, TN)
+            d_value[:keys, :] += mm(p.astype(bf16), back_h, TN)
+        d_query[at, :] = result
+    for b in range(length // step):
+        at = pl.ds(b * step, step)
+        c, s = cosine[at, :], sine[at, :]
+        d_qkv[at, :cols] = turned(d_query[at, :] * scale, c, -s).astype(bf16)
+        d_qkv[at, cols : 2 * cols] = turned(d_key[at, :] * scale, c, -s).astype(bf16)
+        d_qkv[at, 2 * cols :] = d_value[at, :].astype(bf16)
+    g_one = vecs[0:1, :]
+    qkv_sum = jnp.zeros((1, 3 * cols), f32)
+    gain_sum = jnp.zeros((1, width), f32)
+    shift_sum = jnp.zeros((1, width), f32)
+    for i in range(nc):
+        half = part_near if i < nc // 2 else part_far
+        at = pl.ds(pl.multiple_of(meta[i] * block, block), block)
+        dq = d_qkv[at, :]
+        qkv_sum += jnp.sum(dq.astype(f32), axis=0, keepdims=True)
+        first = mm(dq, w_qkv, NT)
+        gain_sum += jnp.sum(first * normed[at, :].astype(f32), axis=0, keepdims=True)
+        shift_sum += jnp.sum(first, axis=0, keepdims=True)
+        half[i % (nc // 2)] = (first * g_one + part[at, :].astype(f32)).astype(bf16)
+    grad_qkv = mm(first_in[...], d_qkv[...], TN).astype(bf16)
+    rows_d = width // nd
+    for d in range(nd):
+        grads[d, :, : 3 * cols] = grad_qkv[d * rows_d : (d + 1) * rows_d]
+    own = g_all[pl.ds(pl.multiple_of(meta[0] * block, block), block), :].astype(f32)
+    own_sum = jnp.sum(own, axis=0, keepdims=True)
+
+    def halves(row):
+        high = row.astype(bf16).astype(f32)
+        return high, row - high
+
+    kept = iota((total, width), 0) == own24[...]
+    up_owner = iota((total, ff), 0) == own96[...] * nc + meta[10]
+    col_owner, col_place = column_places(meta, nb, cols, width, per_d, held)
+    col_pick = (iota((block, 3 * cols), 0) == col_place).astype(f32).astype(bf16)
+    col_kept = iota((total, 3 * cols), 0) == col_owner
+    kind = iota((total, rows, block), 1)
+    packed = jnp.zeros((total, rows, block), f32)
+    entries = [
+        (qkv_sum * meta[11].astype(f32), col_kept, col_pick),
+        (sums[2:3, :ff], up_owner, pick96[...]),
+        (own_sum, kept, pick24[...]),
+        (gain_sum, kept, pick24[...]),
+        (shift_sum, kept, pick24[...]),
+        (sums[0:1, :], kept, pick24[...]),
+        (sums[1:2, :], kept, pick24[...]),
+    ]
+    for k, (vector, where, pick) in enumerate(entries):
+        for n, piece in enumerate(halves(vector)):
+            spread = mm(jnp.where(where, piece, 0.0).astype(bf16), pick, NT)
+            packed = jnp.where(kind == k + 8 * n, spread[:, None, :], packed)
+    grads[:, :, 3 * cols :] = packed.reshape(nd, rows_d, block).astype(bf16)
+
+
+def unpack_kernel(per_d, nd, units, qkv, up, grad_qkv, grad_up, vector):
+    f32 = jnp.float32
+    nc = qkv.shape[0]
+    held = nd // 2
+    width = grad_qkv.shape[1] // 3
+    cols = held * HD
+    pieces = [None] * (3 * per_d * nd)
+    ups = [None] * (nd * nc)
+    total = jnp.zeros(vector.shape, f32)
+    for t in range(nc):
+        group, half = t // 3, t % 3
+        w = qkv[t].astype(f32)
+        if half < 2:
+            for part in range(3):
+                for k in range(held):
+                    at = part * cols + k * HD
+                    pieces[part * per_d * nd + per_d * (held * half + k) + group] = w[:, at : at + HD]
+        total = total + w[:, 3 * cols :]
+        u = up[t].astype(f32)
+        for k in range(nd):
+            ups[k * nc + t] = u[:, k * units : (k + 1) * units]
+    grad_qkv[...] = jnp.concatenate(pieces, axis=1)
+    grad_up[...] = jnp.concatenate(ups, axis=1)
+    vector[...] = total
+
+
+def head_split_plan(
+    tokens,
+    segment_numbers,
+    cotangent,
+    query_key_value_weight,
+    query_key_value_bias,
+    output_matrix,
+    output_bias,
+    up_matrix,
+    up_input_bias,
+    down_matrix,
+    down_output_bias,
+    first_gain,
+    first_shift,
+    second_gain,
+    second_shift,
+):
+    f32, bf16, i32 = jnp.float32, jnp.bfloat16, jnp.int32
+    nd, nc = lax.axis_size("dp"), lax.axis_size("ctx")
+    block, width = tokens.shape[1], tokens.shape[2]
+    per_d = width // HD // nd
+    held = nd // 2
+    cols = held * HD
+    rows = query_key_value_weight.shape[0]
+    units = down_matrix.shape[0]
+    ff = nd * units
+    nb, nu = query_key_value_bias.shape[0], up_input_bias.shape[0]
+    length = nc * block
+    rows_d = nc * rows
+    sizes = (nd, nc, per_d, held, nb, rows)
+    d, c = lax.axis_index("dp"), lax.axis_index("ctx")
+    group, half = c // 3, c % 3
+    half_in = jnp.minimum(half, 1)
+    meta = jnp.concatenate(
+        [c ^ jnp.asarray(slot_order(nc), i32), jnp.stack([half_in, group, c, (half < 2).astype(i32)]).astype(i32)]
+    )
+    lane = np.arange(width)
+    own24 = jnp.asarray((lane // rows)[None], i32)
+    pick24 = jnp.asarray(np.arange(block)[:, None] == lane[None] % rows, bf16)
+    unit = np.arange(ff)
+    own96 = jnp.asarray((unit // units)[None], i32)
+    pick96 = jnp.asarray(np.arange(block)[:, None] == unit[None] % units, bf16)
+    feature = np.arange(cols) % HD % (ROT // 2)
+    freq = jnp.asarray((10000.0 ** (-feature * 2.0 / ROT))[None], f32)
+
+    vectors = [
+        query_key_value_bias, up_input_bias, output_bias, down_output_bias, first_gain, first_shift, second_gain,
+        second_shift, segment_numbers.reshape(block).astype(bf16),
+    ]
+    vectors = jnp.stack([jnp.pad(v, (0, block - v.shape[0])) for v in vectors])
+    vectors = jnp.pad(vectors, ((0, rows - vectors.shape[0]), (0, 0)))
+    lanes = 3 * cols + ff + block
+    (message,) = call(
+        partial(message_kernel, per_d, nd, nc, units),
+        [like((nc, rows, lanes), bf16)],
+        [query_key_value_weight, up_matrix, vectors],
+        smem=False,
+    )
+    arrived = lax.all_to_all(message, "ctx", 0, 0, tiled=True)
+    x_near, x_far = gather_slots(tokens[0])
+    every = lax.all_gather(arrived.reshape(rows_d, lanes), "dp", axis=0, tiled=False)
+    w_down = lax.all_gather(down_matrix, "dp", axis=0, tiled=True)
+    cosine, sine, begin = call(
+        tables_kernel, [like((length, cols), f32)] * 3, [arrived, freq], smem=False
+    )
+
+    two = [2 if k < nd // 2 else -2 for k in range(nd)]
+    after = between(output_matrix, [1] * nd)
+    before = between(output_matrix, [-1] * nd)
+    far = between(output_matrix, two)
+    strip = jnp.concatenate([far, before, output_matrix, after, far], axis=0)
+    in_lower = d < nd // 2
+    target = jnp.where(in_lower, half == 0, half == 1)
+    cut = jnp.where(target, HD * group - rows * (c - 2), 0)
+    outs = lax.all_gather(lax.dynamic_slice_in_dim(strip, cut, HD, 0), "dp", axis=0, tiled=False)
+    g_near, g_far = gather_slots(cotangent[0])
+
+    full = lambda dtype: like((length, width), dtype)
+    part_shape = like((nc // 2, block, width), bf16)
+    (
+        part_near, part_far, first_in, second_in, normed, query, key, value, attended, stats, hidden, slope, vecs,
+    ) = call(
+        partial(forward_kernel, sizes),
+        [part_shape, part_shape, full(bf16), full(bf16), full(bf16)]
+        + [like((length, cols), bf16)] * 3
+        + [like((length, cols), f32), like((length, 128), f32)]
+        + [like((length, ff), bf16)] * 2
+        + [like((8, width), f32)],
+        [meta, x_near, x_far, every, w_down, outs, cosine, sine, begin, own24, pick24, own96, pick96],
+        flops=2 * length * width * (3 * cols + 2 * ff + cols) + 4 * held * length * length * HD,
+    )
+    mixed_sum = reduce_slots(part_near, part_far)
+    mixed = (tokens[0].astype(f32) + (mixed_sum + vecs[4])).astype(bf16)
+    grads_one, part, g_all, sums = call(
+        partial(mlp_back_kernel, sizes),
+        [like((nd, rows_d + 2 * units + 2 * HD, width // 2), bf16), full(bf16), full(bf16), like((8, width), f32)],
+        [meta, g_near, g_far, every, w_down, attended, hidden, slope, second_in, normed, vecs],
+        scratch=[pltpu.VMEM((length, ff), bf16)],
+        flops=2 * length * width * (4 * ff + cols),
+    )
+    grads_one = lax.psum_scatter(grads_one, "dp", scatter_dimension=0, tiled=False)
+    grads_two, n_near, n_far = call(
+        partial(attention_back_kernel, sizes),
+        [like((nd, rows_d, 3 * cols + block), bf16), part_shape, part_shape],
+        [meta, g_all, every, outs, cosine, sine, begin, query, key, value, attended, stats, first_in, normed, vecs, part,
+         sums, own24, pick24, own96, pick96],
+        scratch=[pltpu.VMEM((length, cols), bf16)]
+        + [pltpu.VMEM((length, cols), f32)] * 3
+        + [pltpu.VMEM((length, 3 * cols), bf16), pltpu.VMEM((8, 128), f32)],
+        flops=2 * length * width * (6 * cols + cols) + 10 * held * length * length * HD,
+    )
+    grads_two = lax.psum_scatter(grads_two, "dp", scatter_dimension=0, tiled=False)
+    inner_sum = reduce_slots(n_near, n_far)
+    own = cotangent[0].astype(f32)
+    own_x = tokens[0].astype(f32)
+    own_centered = own_x - jnp.mean(own_x, axis=-1, keepdims=True)
+    own_inverse = lax.rsqrt(jnp.mean(own_centered * own_centered, axis=-1, keepdims=True) + eps)
+    own_normed = own_centered * own_inverse
+    inner = (
+        inner_sum
+        - jnp.mean(inner_sum, axis=-1, keepdims=True)
+        - own_normed * jnp.mean(inner_sum * own_normed, axis=-1, keepdims=True)
+    )
+    tokens_grad = (own + inner * own_inverse).astype(bf16)
+
+    up_back = lax.all_to_all(grads_one[:rows_d].reshape(nc, rows, ff), "ctx", 0, 0, tiled=True)
+    at = rows_d + 2 * units
+    down_weight_grad = jnp.concatenate([grads_one[rows_d : rows_d + units], grads_one[rows_d + units : at]], axis=1)
+    head_rows = jnp.concatenate([grads_one[at : at + HD], grads_one[at + HD :]], axis=1)
+    head_rows = jnp.where(target, head_rows, jnp.zeros_like(head_rows))
+    strip_grad = lax.dynamic_update_slice(jnp.zeros((5 * rows, width), bf16), head_rows, (cut, 0))
+    strip_grad = strip_grad.reshape(5, rows, width)
+    out_weight_grad = (
+        strip_grad[2].astype(f32)
+        + between(strip_grad[1], [1] * nd).astype(f32)
+        + between(strip_grad[3], [-1] * nd).astype(f32)
+        + between(jnp.where(in_lower, strip_grad[4], strip_grad[0]), [-t for t in two]).astype(f32)
+    )
+    qkv_back = lax.all_to_all(grads_two.reshape(nc, rows, 3 * cols + block), "ctx", 0, 0, tiled=True)
+    qkv_weight_grad, up_weight_grad, vec = call(
+        partial(unpack_kernel, per_d, nd, units),
+        [like((rows, 3 * width), f32), like((rows, nc * ff), f32), like((rows, block), f32)],
+        [qkv_back, up_back],
+        smem=False,
+    )
+    vec = vec[:7] + vec[8:15]
+    small = [vec[k, :rows] for k in range(2, 7)]
+    return (
+        mixed[None],
+        tokens_grad[None],
+        qkv_weight_grad,
+        vec[0, :nb],
+        out_weight_grad,
+        small[0],
+        up_weight_grad,
+        vec[1, :nu],
+        down_weight_grad.astype(f32),
+        small[0],
+        small[1],
+        small[2],
+        small[3],
+        small[4],
+    )
+
+
+def head_split_fits(nd, nc, width):
+    return nd % 2 == 0 and width // HD == 3 * nd and nc == 8 and width // (nd * nc) * 8 == 3 * HD
+
+
+def per_device(tokens, *others):
+    nd, nc = lax.axis_size("dp"), lax.axis_size("ctx")
+    plan = head_split_plan if head_split_fits(nd, nc, tokens.shape[2]) else gathered_plan
+    return plan(tokens, *others)
+
+
 def solution(mesh):
     in_specs = (
         P("dp", "ctx", None),

time: 993 us -> 232 us (0.23)
  waiting for transfers between devices: 729 us -> 65.3 us
  matrix products: 80.3 us -> 0 us
  blocking collectives: 97.2 us -> 33 us
  starting transfers between devices: 1.1 us -> 50.3 us
  Pallas kernels: 0 us -> 48.1 us
  local copies, waits for them, and re-layouts: 48.6 us -> 12.2 us
  other arithmetic: 18 us -> 4.99 us
    reduce_scatter x5 -> x2, waiting for transfers between devices: 530 us -> 0.01 us  [the longest x1 0.01 us: head_split_plan(): lax.psum_scatter(grads_two, 'dp', scatter_dimension=0, tiled=False)]
    all_gather x6 -> x1, waiting for transfers between devices: 196 us -> 0.01 us  [head_split_plan(): lax.all_gather(arrived.reshape(rows_d, lanes), 'dp', axis=0, tiled=False)]
    unnamed x2 -> x0, blocking collectives: 82.9 us -> none
    dot_general x26 -> x0, matrix products: 80.3 us -> none  [the longest x2 8.59 us: query_step(): jnp.einsum('shqk,skhd->shqd', score_grad, keys, preferred_element_type=jn...]
    ppermute x0 -> x22, waiting for transfers between devices: none -> 61.2 us  [the longest x16 61.2 us: swapped(): return lax.ppermute(x, 'ctx', [(i, i ^ bit) for i in range(size)])]
    pallas_call x0 -> x6, Pallas kernels: none -> 48.1 us  [call(): pl.pallas_call(kernel, out_shape=[jax.ShapeDtypeStruct(o.shape, o.dtype)...]
    ppermute x0 -> x22, starting transfers between devices: none -> 35 us  [the longest x6 17.8 us: between(): return lax.ppermute(x, ('dp', 'ctx'), pairs)]
    all_to_all x0 -> x1, blocking collectives: none -> 15.3 us  [head_split_plan(): arrived = lax.all_to_all(message, 'ctx', 0, 0, tiled=True)]
  transfers between devices with their start and end apart: 11 -> 27, of which waited for: 11 -> 9; matrix products, arithmetic and copies ran while one was open for 14% -> 4% of each run, Pallas kernels for 0% -> 9%
where the time goes in v2:
time: 232 us; the launch traced here: 228 us
  waiting for transfers between devices  65.3 us (28%)
  starting transfers between devices  50.3 us (22%)
  Pallas kernels  48.1 us (21%)
  blocking collectives  33 us (14%)
  between operations  14.2 us (6%)
  local copies, waits for them, and re-layouts  12.2 us (5%)
  other arithmetic  4.99 us (2%)
    ppermute x16, waiting for transfers between devices, swapped(): return lax.ppermute(x, 'ctx', [(i, i ^ bit) for i in range(size)])  61.2 us
    pallas_call x6, Pallas kernels, call(): pl.pallas_call(kernel, out_shape=[jax.ShapeDtypeStruct(o.shape, o.dtype)...  48.1 us
    ppermute x6, starting transfers between devices, between(): return lax.ppermute(x, ('dp', 'ctx'), pairs)  17.8 us
    ppermute x16, starting transfers between devices, swapped(): return lax.ppermute(x, 'ctx', [(i, i ^ bit) for i in range(size)])  17.3 us
    all_to_all x1, blocking collectives, head_split_plan(): arrived = lax.all_to_all(message, 'ctx', 0, 0, tiled=True)  15.3 us
    all_gather x1, blocking collectives, head_split_plan(): w_down = lax.all_gather(down_matrix, 'dp', axis=0, tiled=True)  11.1 us
    all_to_all x1, starting transfers between devices, head_split_plan(): lax.all_to_all(grads_two.reshape(nc, rows, 3 * cols + block), 'ctx', 0, 0...  7.99 us
    all_to_all x1, starting transfers between devices, head_split_plan(): lax.all_to_all(grads_one[:rows_d].reshape(nc, rows, ff), 'ctx', 0, 0, til...  6.91 us
  transfers between devices with their start and end apart: 27, of which 9 were waited for; matrix products, arithmetic and copies ran while one was open for 4% of the time, Pallas kernels for 9%

profile of v2, /device:TPU:18, one launch (start us, length us, event | category | flops | bytes accessed | tf_op | source)
XLA Modules:
  0.0 228.0 jit_solution(3468049139262832855)
XLA Ops:
  7.3 0.7 convert_element_type.83
  8.0 0.7 pad_bitcast_fusion.6
  8.7 0.7 pad_bitcast_fusion
  10.1 0.7 pad_bitcast_fusion.4
  11.4 1.8 shard_map.308
  13.2 15.3 %all_to_all.15.arrived = bf16[8,24,896]{2,1,0:T(8,128)(2,1)} all-to-all(bf16[8,24,896]{2,1,0:T(8,128)(2,1)} %shard_map.308), channel_id=1, replica_groups=mesh['dp'=4,'ctx'=8] {'ctx'}, dimensions={0} | all-to-all | bytes 688128 | tf_op jit(solution)/shard_map/all_to_all | solution.py:817
  28.6 3.2 %collective-permute-start.4 = (bf16[24,768]{1,0:T(8,128)(2,1)S(1)}, bf16[24,768]{1,0:T(8,128)(2,1)S(1)}, u32[]{:S(2)}, u32[]{:S(2)}) collective-permute-start(bf16[24,768]{1,0:T(8,128)(2,1)S(1)} %copy-done.9), channel_id=1, source_target_pairs={{2,0},{3,1},{4,2},{5,3},{6,4},{7,5},{10,8},{11,9},{12,10},{13,11},... | collective-permute-start | bytes 110600 | tf_op jit(solution)/shard_map/ppermute | solution.py:427
  31.8 2.8 %collective-permute-start.5 = (bf16[24,768]{1,0:T(8,128)(2,1)S(1)}, bf16[24,768]{1,0:T(8,128)(2,1)S(1)}, u32[]{:S(2)}, u32[]{:S(2)}) collective-permute-start(bf16[24,768]{1,0:T(8,128)(2,1)S(1)} %copy-done.9), channel_id=1, source_target_pairs={{0,1},{1,2},{2,3},{3,4},{4,5},{5,6},{6,7},{8,9},{9,10},{10,11},{11... | collective-permute-start | bytes 110600 | tf_op jit(solution)/shard_map/ppermute | solution.py:427
  34.7 1.8 collective-permute-start.1
  36.5 1.7 collective-permute-start.2
  38.2 11.1 %all_gather.13.down = bf16[384,768]{1,0:T(8,128)(2,1)} all-gather(bf16[96,768]{1,0:T(8,128)(2,1)S(1)} %copy-done.8), channel_id=1, replica_groups=mesh['dp'=4,'ctx'=8] {'dp'}, dimensions={0}, use_global_device_ids=true | all-gather | bytes 737280 | tf_op jit(solution)/shard_map/all_gather | solution.py:820
  49.9 3.5 %collective-permute-start.6 = (bf16[24,768]{1,0:T(8,128)(2,1)S(1)}, bf16[24,768]{1,0:T(8,128)(2,1)S(1)}, u32[]{:S(2)}, u32[]{:S(2)}) collective-permute-start(bf16[24,768]{1,0:T(8,128)(2,1)S(1)} %copy-done.9), channel_id=1, source_target_pairs={{1,0},{2,1},{3,2},{4,3},{5,4},{6,5},{7,6},{9,8},{10,9},{11,10},{12... | collective-permute-start | bytes 110600 | tf_op jit(solution)/shard_map/ppermute | solution.py:427
  53.4 0.9 collective-permute-start.11
  54.4 1.1 collective-permute-start.12
  55.5 1.5 collective-permute-start.13
  57.6 4.2 %collective-permute-done.11 = bf16[128,768]{1,0:T(8,128)(2,1)S(1)} collective-permute-done((bf16[128,768]{1,0:T(8,128)(2,1)S(1)}, bf16[128,768]{1,0:T(8,128)(2,1)S(1)}, u32[]{:S(2)}, u32[]{:S(2)}) %collective-permute-start.11) | collective-permute-done | bytes 196640 | tf_op jit(solution)/shard_map/ppermute | solution.py:401
  61.8 7.4 %collective-permute-done.12 = bf16[128,768]{1,0:T(8,128)(2,1)S(1)} collective-permute-done((bf16[128,768]{1,0:T(8,128)(2,1)S(1)}, bf16[128,768]{1,0:T(8,128)(2,1)S(1)}, u32[]{:S(2)}, u32[]{:S(2)}) %collective-permute-start.12) | collective-permute-done | bytes 196640 | tf_op jit(solution)/shard_map/ppermute | solution.py:401
  69.3 5.0 %collective-permute-done.13 = bf16[128,768]{1,0:T(8,128)(2,1)S(1)} collective-permute-done((bf16[128,768]{1,0:T(8,128)(2,1)S(1)}, bf16[128,768]{1,0:T(8,128)(2,1)S(1)}, u32[]{:S(2)}, u32[]{:S(2)}) %collective-permute-start.13) | collective-permute-done | bytes 196640 | tf_op jit(solution)/shard_map/ppermute | solution.py:401
  74.9 6.6 %all-gather = bf16[256,768]{1,0:T(8,128)(2,1)} all-gather(bf16[64,768]{1,0:T(8,128)(2,1)S(1)} %constant_dynamic-slice_fusion), channel_id=2, replica_groups=mesh['dp'=4,'ctx'=8] {'dp'}, dimensions={0}, use_global_device_ids=true | all-gather | bytes 491520 | tf_op jit(solution)/shard_map/all_gather | solution.py:833
  81.5 4.6 %shard_map.309 = (f32[1024,128]{1,0:T(8,128)}, f32[1024,128]{1,0:T(8,128)}, f32[1024,128]{1,0:T(8,128)}) custom-call(bf16[8,24,896]{2,1,0:T(8,128)(2,1)} %all_to_all.15.arrived, f32[1,128]{1,0:T(1,128)} %constant.69.clone.freq), custom_call_target="tpu_custom_call" | custom-call | bytes 1917440 | tf_op jit(solution)/shard_map/pallas_call | solution.py:380
  86.1 0.9 copy-done.12
  87.0 15.3 %shard_map.310 = (bf16[4,128,768]{2,1,0:T(8,128)(2,1)}, bf16[4,128,768]{2,1,0:T(8,128)(2,1)}, bf16[1024,768]{1,0:T(8,128)(2,1)}, bf16[1024,768]{1,0:T(8,128)(2,1...) custom-call(s32[12]{0:T(128)} %concatenate.12.meta, ...), custom_call_target="tpu_custom_call" | custom-call | flops 2550136832 | bytes 15528496 | tf_op jit(solution)/shard_map/pallas_call | solution.py:380
  102.3 9.1 %shard_map.311 = (bf16[4,512,384]{2,1,0:T(8,128)(2,1)}, bf16[1024,768]{1,0:T(8,128)(2,1)}, bf16[1024,768]{1,0:T(8,128)(2,1)}, f32[8,768]{1,0:T(8,128)}) custom-call(s32[12]{0:T(128)} %concatenate.12.meta, bf16[4,128,768]{2,1,0:T(8,128)(2,1)} %copy-done.3, bf16[4,128,768]{2,1,0:T(8,128)(2,1)} %collective-permute-done.14.far, ...), custom_call_target="tpu_custom_call" | custom-call | flops 2617245696 | bytes 13549616 | tf_op jit(solution)/shard_map/pallas_call | solution.py:380
  111.4 15.4 %shard_map.312 = (bf16[4,192,512]{2,1,0:T(8,128)(2,1)}, bf16[4,128,768]{2,1,0:T(8,128)(2,1)}, bf16[4,128,768]{2,1,0:T(8,128)(2,1)}) custom-call(s32[12]{0:T(128)} %concatenate.12.meta, bf16[1024,768]{1,0:T(8,128)(2,1)} %get-tuple-element.51.g_all, bf16[4,192,896]{2,1,0:T(8,128)(2,1)} %all-gather.3.cloned.1.call-done.every, bf16[4,64,768]{2,1,0:T(8,128)(2,1)} %bitcast.104, ...), custom_call_target="tpu_custom_call" | custom-call | flops 2751463424 | bytes 14176816 | tf_op jit(solution)/shard_map/pallas_call | solution.py:380
  128.0 1.8 collective-permute-start.15
  130.4 0.8 slice_reduce_fusion
  131.2 17.2 %collective-permute-done.15 = bf16[4,128,768]{2,1,0:T(8,128)(2,1)S(1)} collective-permute-done((bf16[4,128,768]{2,1,0:T(8,128)(2,1)S(1)}, bf16[4,128,768]{2,1,0:T(8,128)(2,1)S(1)}, u32[]{:S(2)}, u32[]{:S(2)}) %collective-permute-start.15) | collective-permute-done | bytes 786464 | tf_op jit(solution)/shard_map/ppermute | solution.py:401
  148.7 2.3 %collective-permute-start.17 = (bf16[128,768]{1,0:T(8,128)(2,1)S(1)}, bf16[128,768]{1,0:T(8,128)(2,1)S(1)}, u32[]{:S(2)}, u32[]{:S(2)}) collective-permute-start(bf16[128,768]{1,0:T(8,128)(2,1)S(1)} %get-tuple-element.75), channel_id=1, source_target_pairs={{0,4},{1,5},{2,6},{3,7},{4,0},{5,1},{6,2},{7,3},{8,12},{9,13},{10,... | collective-permute-start | bytes 589832 | tf_op jit(solution)/shard_map/ppermute | solution.py:401
  151.0 1.2 collective-permute-start.18
  152.2 12.6 %collective-permute-done.7 = bf16[4,128,768]{2,1,0:T(8,128)(2,1)S(1)} collective-permute-done((bf16[4,128,768]{2,1,0:T(8,128)(2,1)S(1)}, bf16[4,128,768]{2,1,0:T(8,128)(2,1)S(1)}, u32[]{:S(2)}, u32[]{:S(2)}) %collective-permute-start.7) | collective-permute-done | bytes 786464 | tf_op jit(solution)/shard_map/ppermute | solution.py:401
  165.0 0.8 collective-permute-start.10
  165.8 2.7 %collective-permute-start.9 = (bf16[128,768]{1,0:T(8,128)(2,1)S(1)}, bf16[128,768]{1,0:T(8,128)(2,1)S(1)}, u32[]{:S(2)}, u32[]{:S(2)}) collective-permute-start(bf16[128,768]{1,0:T(8,128)(2,1)S(1)} %get-tuple-element.78), channel_id=1, source_target_pairs={{0,4},{1,5},{2,6},{3,7},{4,0},{5,1},{6,2},{7,3},{8,12},{9,13},{10,... | collective-permute-start | bytes 589832 | tf_op jit(solution)/shard_map/ppermute | solution.py:401
  168.6 8.7 %collective-permute-done.18 = bf16[128,768]{1,0:T(8,128)(2,1)S(1)} collective-permute-done((bf16[128,768]{1,0:T(8,128)(2,1)S(1)}, bf16[128,768]{1,0:T(8,128)(2,1)S(1)}, u32[]{:S(2)}, u32[]{:S(2)}) %collective-permute-start.18) | collective-permute-done | bytes 196640 | tf_op jit(solution)/shard_map/ppermute | solution.py:401
  177.5 5.3 %collective-permute-done.10 = bf16[128,768]{1,0:T(8,128)(2,1)S(1)} collective-permute-done((bf16[128,768]{1,0:T(8,128)(2,1)S(1)}, bf16[128,768]{1,0:T(8,128)(2,1)S(1)}, u32[]{:S(2)}, u32[]{:S(2)}) %collective-permute-start.10) | collective-permute-done | bytes 196640 | tf_op jit(solution)/shard_map/ppermute | solution.py:401
  182.9 0.8 collective-permute-done.9
  183.7 0.9 fusion.19
  184.6 8.0 %all-to-all-start.1 = ((bf16[8,24,512]{2,1,0:T(8,128)(2,1)}), bf16[8,24,512]{2,1,0:T(8,128)(2,1)S(1)}, u32[]{:S(2)}, u32[]{:S(2)}) async-start(bf16[8,24,512]{2,1,0:T(8,128)(2,1)} %bitcast.114), calls=%async_computation.2 | async-start | bytes 393216 | tf_op jit(solution)/shard_map/all_to_all | solution.py:897
  192.6 0.8 slice_bitcast_fusion.11
  193.5 3.4 %collective-permute-start.19 = (bf16[24,768]{1,0:T(8,128)(2,1)S(1)}, bf16[24,768]{1,0:T(8,128)(2,1)S(1)}, u32[]{:S(2)}, u32[]{:S(2)}) collective-permute-start(bf16[24,768]{1,0:T(8,128)(2,1)S(1)} %get-tuple-element.85), channel_id=1, source_target_pairs={{1,0},{2,1},{3,2},{4,3},{5,4},{6,5},{7,6},{9,8},{10,9},{11,10},{12... | collective-permute-start | bytes 110600 | tf_op jit(solution)/shard_map/ppermute | solution.py:427
  196.9 2.5 %collective-permute-start.20 = (bf16[24,768]{1,0:T(8,128)(2,1)S(1)}, bf16[24,768]{1,0:T(8,128)(2,1)S(1)}, u32[]{:S(2)}, u32[]{:S(2)}) collective-permute-start(bf16[24,768]{1,0:T(8,128)(2,1)S(1)} %get-tuple-element.87), channel_id=1, source_target_pairs={{0,1},{1,2},{2,3},{3,4},{4,5},{5,6},{6,7},{8,9},{9,10},{10,11},{11... | collective-permute-start | bytes 110600 | tf_op jit(solution)/shard_map/ppermute | solution.py:427
  199.4 2.5 %collective-permute-start.21 = (bf16[24,768]{1,0:T(8,128)(2,1)S(1)}, bf16[24,768]{1,0:T(8,128)(2,1)S(1)}, u32[]{:S(2)}, u32[]{:S(2)}) collective-permute-start(bf16[24,768]{1,0:T(8,128)(2,1)S(1)} %get-tuple-element.86), channel_id=1, source_target_pairs={{0,2},{1,3},{2,4},{3,5},{4,6},{5,7},{8,10},{9,11},{10,12},{11,13},... | collective-permute-start | bytes 110600 | tf_op jit(solution)/shard_map/ppermute | solution.py:427
  201.9 1.6 slice.142
  203.5 0.9 slice_bitcast_fusion.9
  204.4 6.9 %all-to-all-start.2 = ((bf16[8,24,384]{2,1,0:T(8,128)(2,1)}), bf16[8,24,384]{2,1,0:T(8,128)(2,1)S(1)}, u32[]{:S(2)}, u32[]{:S(2)}) async-start(bf16[8,24,384]{2,1,0:T(8,128)(2,1)} %bitcast.33), calls=%async_computation.4 | async-start | bytes 294912 | tf_op jit(solution)/shard_map/all_to_all | solution.py:884
  211.3 0.7 maximum_convert_fusion
  212.7 3.5 %all-to-all-done.2.up = bf16[8,24,384]{2,1,0:T(8,128)(2,1)S(1)} async-done(((bf16[8,24,384]{2,1,0:T(8,128)(2,1)}), bf16[8,24,384]{2,1,0:T(8,128)(2,1)S(1)}, u32[]{:S(2)}, u32[]{:S(2)}) %all-to-all-start.2) | async-done | bytes 147488 | tf_op jit(solution)/shard_map/all_to_all | solution.py:884
  216.9 1.9 shard_map.313
  218.8 0.7 slice_add_fusion
  (91 shorter events, 9.4 us)
Async XLA Ops:
  7.2 31.0 %copy-start.14 = (s32[8]{0:T(128)S(1)}, s32[8]{0:T(128)}, u32[]{:S(2)}) copy-start(s32[8]{0:T(128)} %constant.64.clone) | copy-start | bytes 100
  7.2 21.4 %copy-start.9 = (bf16[24,768]{1,0:T(8,128)(2,1)S(1)}, bf16[24,768]{1,0:T(8,128)(2,1)}, u32[]{:S(2)}) copy-start(bf16[24,768]{1,0:T(8,128)(2,1)} %param.26) | copy-start | bytes 110596
  7.2 27.4 %copy-start = (bf16[1,128,768]{2,1,0:T(8,128)(2,1)S(1)}, bf16[1,128,768]{2,1,0:T(8,128)(2,1)}, u32[]{:S(2)}) copy-start(bf16[1,128,768]{2,1,0:T(8,128)(2,1)} %param.21) | copy-start | bytes 589828
  7.2 31.0 %copy-start.8 = (bf16[96,768]{1,0:T(8,128)(2,1)S(1)}, bf16[96,768]{1,0:T(8,128)(2,1)}, u32[]{:S(2)}) copy-start(bf16[96,768]{1,0:T(8,128)(2,1)} %param.30) | copy-start | bytes 442372
  7.2 46.2 %copy-start.1 = (bf16[1,128,768]{2,1,0:T(8,128)(2,1)S(1)}, bf16[1,128,768]{2,1,0:T(8,128)(2,1)}, u32[]{:S(2)}) copy-start(bf16[1,128,768]{2,1,0:T(8,128)(2,1)} %param.23) | copy-start | bytes 589828
  7.2 78.9 %all-gather.3.cloned.1.call-start = ((), (), s32[]{:S(2)}) async-start(), calls=%async_computation.5 | async-start | bytes 1720320 | tf_op jit(solution)/shard_map/all_gather | solution.py:819
  28.6 156.1 %reduce-scatter.3.cloned.1.call-start = ((), (), s32[]{:S(2)}) async-start(), calls=%async_computation.6 | async-start | bytes 983040 | tf_op jit(solution)/shard_map/reduce_scatter | solution.py:870
  28.6 21.3 %collective-permute-start.4 = (bf16[24,768]{1,0:T(8,128)(2,1)S(1)}, bf16[24,768]{1,0:T(8,128)(2,1)S(1)}, u32[]{:S(2)}, u32[]{:S(2)}) collective-permute-start(bf16[24,768]{1,0:T(8,128)(2,1)S(1)} %copy-done.9), channel_id=1, source_target_pairs={{2,0},{3,1},{4,2},{5,3},{6,4},{7,5},{10,8},{11,9},{12,10},{13,11},... | collective-permute-start | bytes 110600 | tf_op jit(solution)/shard_map/ppermute | solution.py:427
  31.8 25.3 %collective-permute-start.5 = (bf16[24,768]{1,0:T(8,128)(2,1)S(1)}, bf16[24,768]{1,0:T(8,128)(2,1)S(1)}, u32[]{:S(2)}, u32[]{:S(2)}) collective-permute-start(bf16[24,768]{1,0:T(8,128)(2,1)S(1)} %copy-done.9), channel_id=1, source_target_pairs={{0,1},{1,2},{2,3},{3,4},{4,5},{5,6},{6,7},{8,9},{9,10},{10,11},{11... | collective-permute-start | bytes 110600 | tf_op jit(solution)/shard_map/ppermute | solution.py:427
  34.6 18.8 %collective-permute-start = (bf16[128,768]{1,0:T(8,128)(2,1)S(1)}, bf16[128,768]{1,0:T(8,128)(2,1)S(1)}, u32[]{:S(2)}, u32[]{:S(2)}) collective-permute-start(bf16[128,768]{1,0:T(8,128)(2,1)S(1)} %bitcast.99), channel_id=1, source_target_pairs={{0,2},{1,3},{2,0},{3,1},{4,6},{5,7},{6,4},{7,5},{8,10},{9,11},{10,... | collective-permute-start | bytes 589832 | tf_op jit(solution)/shard_map/ppermute | solution.py:401
  34.7 19.7 %collective-permute-start.1 = (bf16[128,768]{1,0:T(8,128)(2,1)S(1)}, bf16[128,768]{1,0:T(8,128)(2,1)S(1)}, u32[]{:S(2)}, u32[]{:S(2)}) collective-permute-start(bf16[128,768]{1,0:T(8,128)(2,1)S(1)} %bitcast.100), channel_id=1, source_target_pairs={{0,4},{1,5},{2,6},{3,7},{4,0},{5,1},{6,2},{7,3},{8,12},{9,13},{10,... | collective-permute-start | bytes 589832 | tf_op jit(solution)/shard_map/ppermute | solution.py:401
  36.5 19.0 %collective-permute-start.2 = (bf16[128,768]{1,0:T(8,128)(2,1)S(1)}, bf16[128,768]{1,0:T(8,128)(2,1)S(1)}, u32[]{:S(2)}, u32[]{:S(2)}) collective-permute-start(bf16[128,768]{1,0:T(8,128)(2,1)S(1)} %bitcast.101), channel_id=1, source_target_pairs={{0,6},{1,7},{2,4},{3,5},{4,2},{5,3},{6,0},{7,1},{8,14},{9,15},{10,... | collective-permute-start | bytes 589832 | tf_op jit(solution)/shard_map/ppermute | solution.py:401
  49.9 25.0 %collective-permute-start.6 = (bf16[24,768]{1,0:T(8,128)(2,1)S(1)}, bf16[24,768]{1,0:T(8,128)(2,1)S(1)}, u32[]{:S(2)}, u32[]{:S(2)}) collective-permute-start(bf16[24,768]{1,0:T(8,128)(2,1)S(1)} %copy-done.9), channel_id=1, source_target_pairs={{1,0},{2,1},{3,2},{4,3},{5,4},{6,5},{7,6},{9,8},{10,9},{11,10},{12... | collective-permute-start | bytes 110600 | tf_op jit(solution)/shard_map/ppermute | solution.py:427
  53.4 8.4 %collective-permute-start.11 = (bf16[128,768]{1,0:T(8,128)(2,1)S(1)}, bf16[128,768]{1,0:T(8,128)(2,1)S(1)}, u32[]{:S(2)}, u32[]{:S(2)}) collective-permute-start(bf16[128,768]{1,0:T(8,128)(2,1)S(1)} %bitcast.105), channel_id=1, source_target_pairs={{0,2},{1,3},{2,0},{3,1},{4,6},{5,7},{6,4},{7,5},{8,10},{9,11},{10,... | collective-permute-start | bytes 589832 | tf_op jit(solution)/shard_map/ppermute | solution.py:401
  54.4 14.9 %collective-permute-start.12 = (bf16[128,768]{1,0:T(8,128)(2,1)S(1)}, bf16[128,768]{1,0:T(8,128)(2,1)S(1)}, u32[]{:S(2)}, u32[]{:S(2)}) collective-permute-start(bf16[128,768]{1,0:T(8,128)(2,1)S(1)} %bitcast.106), channel_id=1, source_target_pairs={{0,4},{1,5},{2,6},{3,7},{4,0},{5,1},{6,2},{7,3},{8,12},{9,13},{10,... | collective-permute-start | bytes 589832 | tf_op jit(solution)/shard_map/ppermute | solution.py:401
  55.5 18.7 %collective-permute-start.13 = (bf16[128,768]{1,0:T(8,128)(2,1)S(1)}, bf16[128,768]{1,0:T(8,128)(2,1)S(1)}, u32[]{:S(2)}, u32[]{:S(2)}) collective-permute-start(bf16[128,768]{1,0:T(8,128)(2,1)S(1)} %bitcast.107), channel_id=1, source_target_pairs={{0,6},{1,7},{2,4},{3,5},{4,2},{5,3},{6,0},{7,1},{8,14},{9,15},{10,... | collective-permute-start | bytes 589832 | tf_op jit(solution)/shard_map/ppermute | solution.py:401
  57.1 29.0 %copy-start.2 = (bf16[4,128,768]{2,1,0:T(8,128)(2,1)}, bf16[4,128,768]{2,1,0:T(8,128)(2,1)S(1)}, u32[]{:S(2)}) copy-start(bf16[4,128,768]{2,1,0:T(8,128)(2,1)S(1)} %pad_maximum_fusion.near) | copy-start | bytes 2359300
  57.1 29.0 %collective-permute-start.3 = (bf16[4,128,768]{2,1,0:T(8,128)(2,1)S(1)}, bf16[4,128,768]{2,1,0:T(8,128)(2,1)S(1)}, u32[]{:S(2)}, u32[]{:S(2)}) collective-permute-start(bf16[4,128,768]{2,1,0:T(8,128)(2,1)S(1)} %pad_maximum_fusion.near), channel_id=1, source_target_pairs={{0,1},{1,0},{2,3},{3,2},{4,5},{5,4},{6,7},{7,6},{8,9},{9,8},{10,11... | collective-permute-start | bytes 2359304 | tf_op jit(solution)/shard_map/ppermute | solution.py:401
  74.4 28.0 %copy-start.3 = (bf16[4,128,768]{2,1,0:T(8,128)(2,1)}, bf16[4,128,768]{2,1,0:T(8,128)(2,1)S(1)}, u32[]{:S(2)}) copy-start(bf16[4,128,768]{2,1,0:T(8,128)(2,1)S(1)} %pad_maximum_fusion.1.near) | copy-start | bytes 2359300
  74.4 28.0 %collective-permute-start.14 = (bf16[4,128,768]{2,1,0:T(8,128)(2,1)S(1)}, bf16[4,128,768]{2,1,0:T(8,128)(2,1)}, u32[]{:S(2)}, u32[]{:S(2)}) collective-permute-start(bf16[4,128,768]{2,1,0:T(8,128)(2,1)S(1)} %pad_maximum_fusion.1.near), channel_id=1, source_target_pairs={{0,1},{1,0},{2,3},{3,2},{4,5},{5,4},{6,7},{7,6},{8,9},{9,8},{10,11... | collective-permute-start | bytes 2359304 | tf_op jit(solution)/shard_map/ppermute | solution.py:401
  86.1 0.9 copy-start.12
  126.9 1.1 copy-start.13
  126.9 3.3 %copy-start.11 = (bf16[4,128,768]{2,1,0:T(8,128)(2,1)S(1)}, bf16[4,128,768]{2,1,0:T(8,128)(2,1)}, u32[]{:S(2)}) copy-start(bf16[4,128,768]{2,1,0:T(8,128)(2,1)} %get-tuple-element.44) | copy-start | bytes 2359300
  126.9 21.5 %copy-start.6 = (bf16[4,128,768]{2,1,0:T(8,128)(2,1)S(1)}, bf16[4,128,768]{2,1,0:T(8,128)(2,1)}, u32[]{:S(2)}) copy-start(bf16[4,128,768]{2,1,0:T(8,128)(2,1)} %get-tuple-element.59) | copy-start | bytes 2359300
  126.9 65.7 %reduce-scatter.5.cloned.1.call-start = ((), (), s32[]{:S(2)}) async-start(), calls=%async_computation.7 | async-start | bytes 1966080 | tf_op jit(solution)/shard_map/reduce_scatter | solution.py:859
  128.0 20.3 %collective-permute-start.15 = (bf16[4,128,768]{2,1,0:T(8,128)(2,1)S(1)}, bf16[4,128,768]{2,1,0:T(8,128)(2,1)S(1)}, u32[]{:S(2)}, u32[]{:S(2)}) collective-permute-start(bf16[4,128,768]{2,1,0:T(8,128)(2,1)S(1)} %copy-done.13), channel_id=1, source_target_pairs={{0,1},{1,0},{2,3},{3,2},{4,5},{5,4},{6,7},{7,6},{8,9},{9,8},{10,11... | collective-permute-start | bytes 2359304 | tf_op jit(solution)/shard_map/ppermute | solution.py:401
  130.2 34.6 %collective-permute-start.7 = (bf16[4,128,768]{2,1,0:T(8,128)(2,1)S(1)}, bf16[4,128,768]{2,1,0:T(8,128)(2,1)S(1)}, u32[]{:S(2)}, u32[]{:S(2)}) collective-permute-start(bf16[4,128,768]{2,1,0:T(8,128)(2,1)S(1)} %copy-done.11), channel_id=1, source_target_pairs={{0,1},{1,0},{2,3},{3,2},{4,5},{5,4},{6,7},{7,6},{8,9},{9,8},{10,11... | collective-permute-start | bytes 2359304 | tf_op jit(solution)/shard_map/ppermute | solution.py:401
  148.6 16.2 %copy-start.5 = (bf16[4,128,768]{2,1,0:T(8,128)(2,1)S(1)}, bf16[4,128,768]{2,1,0:T(8,128)(2,1)}, u32[]{:S(2)}) copy-start(bf16[4,128,768]{2,1,0:T(8,128)(2,1)} %get-tuple-element.43) | copy-start | bytes 2359300
  148.6 17.2 %collective-permute-start.16 = (bf16[128,768]{1,0:T(8,128)(2,1)S(1)}, bf16[128,768]{1,0:T(8,128)(2,1)S(1)}, u32[]{:S(2)}, u32[]{:S(2)}) collective-permute-start(bf16[128,768]{1,0:T(8,128)(2,1)S(1)} %get-tuple-element.73), channel_id=1, source_target_pairs={{0,2},{1,3},{2,0},{3,1},{4,6},{5,7},{6,4},{7,5},{8,10},{9,11},{10,... | collective-permute-start | bytes 589832 | tf_op jit(solution)/shard_map/ppermute | solution.py:401
  148.7 19.9 %collective-permute-start.17 = (bf16[128,768]{1,0:T(8,128)(2,1)S(1)}, bf16[128,768]{1,0:T(8,128)(2,1)S(1)}, u32[]{:S(2)}, u32[]{:S(2)}) collective-permute-start(bf16[128,768]{1,0:T(8,128)(2,1)S(1)} %get-tuple-element.75), channel_id=1, source_target_pairs={{0,4},{1,5},{2,6},{3,7},{4,0},{5,1},{6,2},{7,3},{8,12},{9,13},{10,... | collective-permute-start | bytes 589832 | tf_op jit(solution)/shard_map/ppermute | solution.py:401
  151.0 26.3 %collective-permute-start.18 = (bf16[128,768]{1,0:T(8,128)(2,1)S(1)}, bf16[128,768]{1,0:T(8,128)(2,1)S(1)}, u32[]{:S(2)}, u32[]{:S(2)}) collective-permute-start(bf16[128,768]{1,0:T(8,128)(2,1)S(1)} %get-tuple-element.74), channel_id=1, source_target_pairs={{0,6},{1,7},{2,4},{3,5},{4,2},{5,3},{6,0},{7,1},{8,14},{9,15},{10,... | collective-permute-start | bytes 589832 | tf_op jit(solution)/shard_map/ppermute | solution.py:401
  165.0 17.9 %collective-permute-start.10 = (bf16[128,768]{1,0:T(8,128)(2,1)S(1)}, bf16[128,768]{1,0:T(8,128)(2,1)S(1)}, u32[]{:S(2)}, u32[]{:S(2)}) collective-permute-start(bf16[128,768]{1,0:T(8,128)(2,1)S(1)} %get-tuple-element.77), channel_id=1, source_target_pairs={{0,6},{1,7},{2,4},{3,5},{4,2},{5,3},{6,0},{7,1},{8,14},{9,15},{10,... | collective-permute-start | bytes 589832 | tf_op jit(solution)/shard_map/ppermute | solution.py:401
  165.8 17.1 %collective-permute-start.8 = (bf16[128,768]{1,0:T(8,128)(2,1)S(1)}, bf16[128,768]{1,0:T(8,128)(2,1)S(1)}, u32[]{:S(2)}, u32[]{:S(2)}) collective-permute-start(bf16[128,768]{1,0:T(8,128)(2,1)S(1)} %get-tuple-element.76), channel_id=1, source_target_pairs={{0,2},{1,3},{2,0},{3,1},{4,6},{5,7},{6,4},{7,5},{8,10},{9,11},{10,... | collective-permute-start | bytes 589832 | tf_op jit(solution)/shard_map/ppermute | solution.py:401
  165.8 17.9 %collective-permute-start.9 = (bf16[128,768]{1,0:T(8,128)(2,1)S(1)}, bf16[128,768]{1,0:T(8,128)(2,1)S(1)}, u32[]{:S(2)}, u32[]{:S(2)}) collective-permute-start(bf16[128,768]{1,0:T(8,128)(2,1)S(1)} %get-tuple-element.78), channel_id=1, source_target_pairs={{0,4},{1,5},{2,6},{3,7},{4,0},{5,1},{6,2},{7,3},{8,12},{9,13},{10,... | collective-permute-start | bytes 589832 | tf_op jit(solution)/shard_map/ppermute | solution.py:401
  184.6 19.8 %all-to-all-start.1 = ((bf16[8,24,512]{2,1,0:T(8,128)(2,1)}), bf16[8,24,512]{2,1,0:T(8,128)(2,1)S(1)}, u32[]{:S(2)}, u32[]{:S(2)}) async-start(bf16[8,24,512]{2,1,0:T(8,128)(2,1)} %bitcast.114), calls=%async_computation.2 | async-start | bytes 393216 | tf_op jit(solution)/shard_map/all_to_all | solution.py:897
  193.5 18.5 %collective-permute-start.19 = (bf16[24,768]{1,0:T(8,128)(2,1)S(1)}, bf16[24,768]{1,0:T(8,128)(2,1)S(1)}, u32[]{:S(2)}, u32[]{:S(2)}) collective-permute-start(bf16[24,768]{1,0:T(8,128)(2,1)S(1)} %get-tuple-element.85), channel_id=1, source_target_pairs={{1,0},{2,1},{3,2},{4,3},{5,4},{6,5},{7,6},{9,8},{10,9},{11,10},{12... | collective-permute-start | bytes 110600 | tf_op jit(solution)/shard_map/ppermute | solution.py:427
  196.9 15.2 %collective-permute-start.20 = (bf16[24,768]{1,0:T(8,128)(2,1)S(1)}, bf16[24,768]{1,0:T(8,128)(2,1)S(1)}, u32[]{:S(2)}, u32[]{:S(2)}) collective-permute-start(bf16[24,768]{1,0:T(8,128)(2,1)S(1)} %get-tuple-element.87), channel_id=1, source_target_pairs={{0,1},{1,2},{2,3},{3,4},{4,5},{5,6},{6,7},{8,9},{9,10},{10,11},{11... | collective-permute-start | bytes 110600 | tf_op jit(solution)/shard_map/ppermute | solution.py:427
  199.4 12.7 %collective-permute-start.21 = (bf16[24,768]{1,0:T(8,128)(2,1)S(1)}, bf16[24,768]{1,0:T(8,128)(2,1)S(1)}, u32[]{:S(2)}, u32[]{:S(2)}) collective-permute-start(bf16[24,768]{1,0:T(8,128)(2,1)S(1)} %get-tuple-element.86), channel_id=1, source_target_pairs={{0,2},{1,3},{2,4},{3,5},{4,6},{5,7},{8,10},{9,11},{10,12},{11,13},... | collective-permute-start | bytes 110600 | tf_op jit(solution)/shard_map/ppermute | solution.py:427
  204.4 11.8 %copy-start.4 = (bf16[8,24,512]{2,1,0:T(8,128)(2,1)}, bf16[8,24,512]{2,1,0:T(8,128)(2,1)S(1)}, u32[]{:S(2)}) copy-start(bf16[8,24,512]{2,1,0:T(8,128)(2,1)S(1)} %all-to-all-done.1.qkv) | copy-start | bytes 589828
  204.4 11.8 %all-to-all-start.2 = ((bf16[8,24,384]{2,1,0:T(8,128)(2,1)}), bf16[8,24,384]{2,1,0:T(8,128)(2,1)S(1)}, u32[]{:S(2)}, u32[]{:S(2)}) async-start(bf16[8,24,384]{2,1,0:T(8,128)(2,1)} %bitcast.33), calls=%async_computation.4 | async-start | bytes 294912 | tf_op jit(solution)/shard_map/all_to_all | solution.py:884
  216.2 0.7 copy-start.7
  220.0 1.5 copy-start.10
Sparse Core Ops, SparseCore 0:
  28.7 20.8 all-gather.2
  127.0 22.7 reduce-scatter.2
  152.5 28.1 reduce-scatter.4

commit v3 on v2

--- a/solution.py
+++ b/solution.py
@@ -358,7 +358,10 @@
     return (mixed, tokens_grad) + tuple(shards)
 
 
-VMEM_LIMIT = 56 * 1024 * 1024
+VMEM_LIMIT = 30 * 1024 * 1024
+VMEM_MOST = 56 * 1024 * 1024
+FORWARD_WORK = 10**8
+BACKWARD_WORK = 10**8
 NT = (((1,), (1,)), ((), ()))
 TN = (((0,), (0,)), ((), ()))
 NN = (((1,), (0,)), ((), ()))
@@ -368,23 +371,25 @@
     return lax.dot_general(a, b, dims, preferred_element_type=jnp.float32)
 
 
+HEAD_OF = (0, 1, None, 2)
+
+
 def vmem(count):
     return [pl.BlockSpec(memory_space=pltpu.VMEM)] * count
 
 
-def call(kernel, outs, operands, scratch=(), flops=0, smem=True):
+def call(kernel, outs, operands, scratch=(), flops=0, smem=True, limit=VMEM_LIMIT):
     specs = vmem(len(operands))
     if smem:
         specs[0] = pl.BlockSpec(memory_space=pltpu.SMEM)
-    size = sum(math.prod(o.shape) * o.dtype.itemsize for o in list(outs) + list(operands))
     return pl.pallas_call(
         kernel,
         out_shape=[jax.ShapeDtypeStruct(o.shape, o.dtype) for o in outs],
         in_specs=specs,
         out_specs=vmem(len(outs)),
         scratch_shapes=list(scratch),
-        compiler_params=pltpu.CompilerParams(vmem_limit_bytes=VMEM_LIMIT),
-        cost_estimate=pl.CostEstimate(flops=flops, bytes_accessed=size, transcendentals=0),
+        compiler_params=pltpu.CompilerParams(vmem_limit_bytes=limit),
+        cost_estimate=pl.CostEstimate(flops=flops, bytes_accessed=1024, transcendentals=0),
     )(*operands)
 
 
@@ -401,76 +406,126 @@
     return lax.ppermute(x, "ctx", [(i, i ^ bit) for i in range(size)])
 
 
-def gather_slots(x):
-    size = lax.axis_size("ctx")
-    near = jnp.stack([x] + [swapped(x, bit) for bit in range(2, size, 2)])
-    return near, swapped(near, 1)
-
-
-def reduce_slots(near, far):
-    near = near.astype(jnp.float32) + swapped(far, 1).astype(jnp.float32)
-    low = near.astype(jnp.bfloat16)
-    total = near[0]
-    for number in range(1, near.shape[0]):
-        total = total + swapped(low[number], 2 * number).astype(jnp.float32)
-    return total
-
-
-def between(x, offset):
+def swapped_dp(x, bit):
+    size = lax.axis_size("dp")
+    return lax.ppermute(x, "dp", [(i, i ^ bit) for i in range(size)])
+
+
+def after(x, *others):
+    return lax.optimization_barrier((x,) + others)[0]
+
+
+def sent(x, pairs):
     nd, nc = lax.axis_size("dp"), lax.axis_size("ctx")
-    pairs = [
-        (d * nc + c + offset[d], d * nc + c)
-        for d in range(nd)
-        for c in range(nc)
-        if 0 <= c + offset[d] < nc
-    ]
-    return lax.ppermute(x, ("dp", "ctx"), pairs)
+    flat = [(d * nc + a, d * nc + b) for d in range(nd) for a, b in pairs(d)]
+    return lax.ppermute(x, ("dp", "ctx"), flat)
 
 
 def iota(shape, dim):
     return lax.broadcasted_iota(jnp.int32, shape, dim)
 
 
-def message_kernel(per_d, nd, nc, units, qkv, up, vectors, out):
+def message_kernel(per_d, nd, nc, units, meta, qkv, up, out_rows, *refs):
     f32 = jnp.float32
+    vectors, out = refs[:-5], refs[-1]
+    mine, two, four, six = refs[-5:-1]
+    c = meta[10]
     rows = qkv.shape[0]
     width = qkv.shape[1] // 3
     held = nd // 2
     w = qkv[...].astype(f32)
     u = up[...].astype(f32)
-    v = vectors[...].astype(f32)
+    lines = []
+    for vector in vectors:
+        line = vector[...].astype(f32)
+        if line.shape[1] < 128:
+            line = jnp.concatenate([line, jnp.zeros((1, 128 - line.shape[1]), f32)], axis=1)
+        lines.append(line)
+    v = jnp.concatenate(lines + [jnp.zeros((rows - len(lines), 128), f32)], axis=0)
     for t in range(nc):
-        group, half = t // 3, t % 3
+        group, half = HEAD_OF[t // 2], t % 2
         pieces = []
         for part in range(3):
             for k in range(held):
-                at = part * width + HD * (per_d * (held * half + k) + group)
-                pieces.append(w[:, at : at + HD] if half < 2 else jnp.zeros((rows, HD), f32))
+                at = part * width + HD * (per_d * (held * half + k) + (group or 0))
+                pieces.append(jnp.zeros((rows, HD), f32) if group is None else w[:, at : at + HD])
         for k in range(nd):
             at = k * nc * units + t * units
             pieces.append(u[:, at : at + units])
-        out[t] = jnp.concatenate(pieces + [v], axis=1).astype(out.dtype)
-
-
-def tables_kernel(arrived, freq, cosine, sine, begin):
+        out[c ^ t] = jnp.concatenate(pieces + [v], axis=1).astype(out.dtype)
+    blank = jnp.zeros((rows, out.shape[2] - width), f32)
+    head = jnp.concatenate([out_rows[...].astype(f32), blank], axis=1).astype(out.dtype)
+    mine[0], mine[1], mine[2] = out[0], out[1], head
+    two[0], two[1], two[2] = out[2], out[3], head
+    four[0], four[1] = out[4], out[5]
+    six[0], six[1], six[2] = out[6], out[7], head
+
+
+def package_kernel(meta, mine, two, four, six, far, down, out, natural, strip):
     f32 = jnp.float32
-    nc, rows, lanes = arrived.shape
+    nc, rows, lanes = natural.shape
+    c = meta[10]
+    width = down.shape[1]
+    for k, near in enumerate((mine, two, four, six)):
+        natural[c ^ (2 * k)] = near[0].astype(f32)
+        natural[c ^ (2 * k + 1)] = far[k].astype(f32)
+    out[: nc * rows, :] = natural[...].reshape(nc * rows, lanes).astype(out.dtype)
+    strip[...] = jnp.zeros_like(strip)
+    strip[c] = mine[2].astype(f32)
+    strip[c ^ 2] = two[2].astype(f32)
+    strip[c ^ 6] = six[2].astype(f32)
+    strip[c ^ 1] = far[4].astype(f32)
+    strip[meta[13]] = far[5].astype(f32)
+    whole = strip[...].reshape(nc * rows, lanes)
+    group = meta[9]
+    head = jnp.where(group == 0, whole[:HD], jnp.where(group == 1, whole[HD : 2 * HD], whole[2 * HD : 3 * HD]))
+    tail = jnp.concatenate([down[...].astype(f32), head[:, :width]], axis=0)
+    blank = jnp.zeros((tail.shape[0], lanes - width), f32)
+    out[nc * rows :, :] = jnp.concatenate([tail, blank], axis=1).astype(out.dtype)
+
+
+def tables_kernel(nc, rows, package, freq, cosine, sine, begin):
+    f32 = jnp.float32
+    lanes = package.shape[1]
     block = 128
-    head = arrived[:, :, lanes - block :].astype(f32)
+    head = package[: nc * rows, lanes - block :].astype(f32).reshape(nc, rows, block)
     seg = jnp.sum(jnp.where(iota((nc, rows, block), 1) == 8, head, 0.0), axis=1)
-    row = jnp.concatenate([seg[b : b + 1] for b in range(nc)], axis=1)
-    eye = iota((block, block), 0) == iota((block, block), 1)
-    feature = iota((block, block), 1) % HD
-    for b in range(nc):
-        col = jnp.sum(jnp.where(eye, seg[b : b + 1], 0.0), axis=1, keepdims=True)
-        start = jnp.sum(jnp.where(row < col, 1.0, 0.0), axis=1, keepdims=True)
-        index = (iota((block, 1), 0) + b * block).astype(f32)
-        angle = (index - start) * freq[...]
-        at = pl.ds(b * block, block)
-        cosine[at, :] = jnp.where(feature < ROT, jnp.cos(angle), 1.0)
-        sign = jnp.where(feature < ROT // 2, -1.0, jnp.where(feature < ROT, 1.0, 0.0))
-        sine[at, :] = sign * jnp.sin(angle)
-        begin[at, :] = jnp.broadcast_to(start, (block, block))
+    start = jnp.zeros((nc, block), f32)
+    for number in range(1, 8):
+        earlier = jnp.where(seg < number, 1.0, 0.0)
+        count = jnp.sum(jnp.sum(earlier, axis=1, keepdims=True), axis=0, keepdims=True)
+        start = jnp.where(seg == number, count, start)
+    index = (iota((nc, block), 0) * block + iota((nc, block), 1)).astype(f32)
+
+    def as_row(x):
+        return jnp.concatenate([x[b : b + 1] for b in range(nc)], axis=1)
+
+    half = ROT // 2
+    angle = freq[...] * as_row(index - start)
+    table = jnp.concatenate(
+        [jnp.cos(angle), jnp.sin(angle), jnp.broadcast_to(as_row(start), angle.shape)], axis=0
+    )
+    feature = iota((3 * half, block), 1) % HD
+    row = iota((3 * half, block), 0)
+    first, second = feature == row, feature == row + half
+    rotary = feature < ROT
+    is_first, is_second = jnp.where(first & rotary, 1.0, 0.0), jnp.where(second & rotary, 1.0, 0.0)
+    pick_cos = jnp.where(row < half, is_first + is_second, 0.0)
+    row2 = row - half
+    sine_first = jnp.where((feature == row2) & rotary & (row2 >= 0), -1.0, 0.0)
+    sine_second = jnp.where((feature == row2 + half) & rotary & (row2 >= 0), 1.0, 0.0)
+    pick_sin = jnp.where(row < 2 * half, sine_first + sine_second, 0.0)
+    pick_start = jnp.where(row == 2 * half, 1.0, 0.0)
+
+    def spread(pick):
+        return lax.dot_general(
+            table, pick, TN, precision=lax.Precision.HIGHEST, preferred_element_type=f32
+        )
+
+    still = jnp.where(iota((1, block), 1) % HD < ROT, 0.0, 1.0)
+    cosine[...] = spread(pick_cos) + still
+    sine[...] = spread(pick_sin)
+    begin[...] = spread(pick_start)
 
 
 def turned(t, cosine, sine):
@@ -505,16 +560,27 @@
 
 
 def forward_kernel(
-    sizes, meta, near, far, every, down, outs, cosine, sine, begin, own24, pick24, own96, pick96,
-    part_near, part_far, first_in, second_in, normed, query, key, value, attended, stats, hidden, slope, vecs,
+    sizes, meta, near, far, own_pair, other_pair, cosine, sine, begin, own24, pick24, own96, pick96,
+    out_near, out_far, first_in, second_in, normed, query, key, value, attended, stats, hidden, slope, vecs, weights,
+    w_out, down, every, outs,
 ):
     f32, bf16 = jnp.float32, jnp.bfloat16
     nd, nc, per_d, held, nb, rows = sizes
     block, width = near.shape[1], near.shape[2]
     cols = held * HD
-    ff = down.shape[0]
+    ff = own96.shape[1]
     length = nc * block
     total = nd * nc
+    n1 = nc * rows
+    n2 = n1 + ff // nd
+    for i, pair in enumerate((own_pair, other_pair) * 2):
+        other = meta[12] ^ i
+        piece = pair.at[i // 2]
+        every[other] = piece[:n1]
+        down[pl.ds(pl.multiple_of(other * (ff // nd), ff // nd), ff // nd), :] = piece[n1:n2, :width]
+        outs[other] = piece[n2:, :width]
+    w_out[...] = outs[pl.ds(held * meta[8], held)].reshape(cols, width)
+    weights[...] = every[:, :, : 3 * cols + ff].reshape(width, 3 * cols + ff)
     packed = every[:, :, 3 * cols + ff :].astype(f32).reshape(total, rows, block)
     kind = iota(packed.shape, 1)
 
@@ -544,8 +610,8 @@
         normed[at, :] = n.astype(bf16)
         first_in[at, :] = (n * g_one + s_one).astype(bf16)
         second_in[at, :] = (n * g_two + s_two).astype(bf16)
-    w_qkv = every[:, :, : 3 * cols].reshape(width, 3 * cols)
-    w_up = every[:, :, 3 * cols : 3 * cols + ff].reshape(width, ff)
+    w_qkv = weights[:, : 3 * cols]
+    w_up = weights[:, 3 * cols :]
     step = 2 * block
     for b in range(length // step):
         at = pl.ds(b * step, step)
@@ -576,46 +642,48 @@
             stats[at, 2 * h : 2 * h + 1] = top
             stats[at, 2 * h + 1 : 2 * h + 2] = inverse
         attended[at, :] = result
-    w_out = outs[pl.ds(held * meta[8], held)].reshape(cols, width)
     for i in range(nc):
-        half = part_near if i < nc // 2 else part_far
+        half = out_near if i < nc // 2 else out_far
         at = pl.ds(pl.multiple_of(meta[i] * block, block), block)
-        part = mm(attended[at, :].astype(bf16), w_out) + mm(hidden[at, :], down[...])
-        half[i % (nc // 2)] = part.astype(bf16)
-
-
-def mlp_back_kernel(
-    sizes, meta, near, far, every, down, attended, hidden, slope, second_in, normed, vecs,
-    grads, part, g_all, sums, pre_grad,
+        piece = mm(attended[at, :].astype(bf16), w_out[...]) + mm(hidden[at, :], down[...])
+        half[i % (nc // 2)] = piece.astype(bf16)
+
+
+def mlp_back(
+    sizes, meta, near, far, weights, down, attended, hidden, slope, second_in, normed, vecs, part, g_all, sums, pre_grad,
+    grads, place,
 ):
     f32, bf16 = jnp.float32, jnp.bfloat16
     nd, nc, per_d, held, nb, rows = sizes
     block, width = near.shape[1], near.shape[2]
     cols = held * HD
     ff = down.shape[0]
+    units = ff // nd
     length = nc * block
     for i in range(nc):
         half = near if i < nc // 2 else far
         g_all[pl.ds(pl.multiple_of(meta[i] * block, block), block), :] = half[i % (nc // 2)]
     g = g_all[...]
     rows_d = width // nd
-    units = ff // nd
     side = width // 2
+
     grad_down = mm(hidden[...], g, TN).astype(bf16)
     for d in range(nd):
         piece = grad_down[d * units : (d + 1) * units]
-        grads[d, rows_d : rows_d + units, :] = piece[:, :side]
-        grads[d, rows_d + units : rows_d + 2 * units, :] = piece[:, side:]
+        slot = place(d)
+        grads[slot, rows_d : rows_d + units, :] = piece[:, :side]
+        grads[slot, rows_d + units : rows_d + 2 * units, :] = piece[:, side:]
     grad_out = mm(attended[...].astype(bf16), g, TN)
     base = rows_d + 2 * units
     for d in range(nd):
         here = (meta[8] == d // held) & (meta[11] == 1)
         k = d % held
         piece = jnp.where(here, grad_out[k * HD : (k + 1) * HD], 0.0).astype(bf16)
-        grads[d, base : base + HD, :] = piece[:, :side]
-        grads[d, base + HD : base + 2 * HD, :] = piece[:, side:]
+        slot = place(d)
+        grads[slot, base : base + HD, :] = piece[:, :side]
+        grads[slot, base + HD : base + 2 * HD, :] = piece[:, side:]
     step = 2 * block
-    w_up = every[:, :, 3 * cols : 3 * cols + ff].reshape(width, ff)
+    w_up = weights[:, 3 * cols :]
     g_two = vecs[2:3, :]
     up_sum = jnp.zeros((1, ff), f32)
     gain_sum = jnp.zeros((1, width), f32)
@@ -634,23 +702,17 @@
     sums[2:3, :ff] = up_sum
     grad_up = mm(second_in[...], pre_grad[...], TN).astype(bf16)
     for d in range(nd):
-        grads[d, :rows_d, :] = grad_up[d * rows_d : (d + 1) * rows_d]
-
-
-def attention_back_kernel(
-    sizes, meta, g_all, every, outs, cosine, sine, begin, query, key, value, attended, stats, first_in, normed, vecs,
-    part, sums, own24, pick24, own96, pick96,
-    grads, part_near, part_far, d_out, d_query, d_key, d_value, d_qkv, first_grad,
+        grads[place(d), :rows_d, :] = grad_up[d * rows_d : (d + 1) * rows_d]
+
+
+def attention_back(
+    sizes, meta, g_all, w_out, cosine, sine, begin, query, key, value, attended, stats, d_qkv, d_query, d_key, d_value
 ):
     f32, bf16 = jnp.float32, jnp.bfloat16
     nd, nc, per_d, held, nb, rows = sizes
     length, width = g_all.shape
     block = length // nc
     cols = held * HD
-    ff = own96.shape[1]
-    total = nd * nc
-    w_out = outs[pl.ds(held * meta[8], held)].reshape(cols, width)
-    w_qkv = every[:, :, : 3 * cols].reshape(width, 3 * cols)
     step = 2 * block
     scale = HD**-0.5
     d_key[...] = jnp.zeros_like(d_key)
@@ -660,7 +722,7 @@
         keys = (b + 1) * step
         allowed = allowed_pairs(begin[at, 0:1], b * step, step, keys)
         q = query[at, :]
-        back = mm(g_all[at, :], w_out, NT).astype(bf16)
+        back = mm(g_all[at, :], w_out[...], NT).astype(bf16)
         product = back.astype(f32) * attended[at, :]
         result = jnp.zeros((step, cols), f32)
         for h in range(held):
@@ -683,6 +745,20 @@
         d_qkv[at, :cols] = turned(d_query[at, :] * scale, c, -s).astype(bf16)
         d_qkv[at, cols : 2 * cols] = turned(d_key[at, :] * scale, c, -s).astype(bf16)
         d_qkv[at, 2 * cols :] = d_value[at, :].astype(bf16)
+
+
+def qkv_back(
+    sizes, meta, g_all, weights, d_qkv, first_in, normed, vecs, part, sums, own24, pick24, own96, pick96,
+    part_near, part_far, grads, place, base,
+):
+    f32, bf16 = jnp.float32, jnp.bfloat16
+    nd, nc, per_d, held, nb, rows = sizes
+    length, width = g_all.shape
+    block = length // nc
+    cols = held * HD
+    ff = own96.shape[1]
+    total = nd * nc
+    w_qkv = weights[:, : 3 * cols]
     g_one = vecs[0:1, :]
     qkv_sum = jnp.zeros((1, 3 * cols), f32)
     gain_sum = jnp.zeros((1, width), f32)
@@ -699,7 +775,7 @@
     grad_qkv = mm(first_in[...], d_qkv[...], TN).astype(bf16)
     rows_d = width // nd
     for d in range(nd):
-        grads[d, :, : 3 * cols] = grad_qkv[d * rows_d : (d + 1) * rows_d]
+        grads[place(d), base : base + rows_d, :] = grad_qkv[d * rows_d : (d + 1) * rows_d]
     own = g_all[pl.ds(pl.multiple_of(meta[0] * block, block), block), :].astype(f32)
     own_sum = jnp.sum(own, axis=0, keepdims=True)
 
@@ -712,8 +788,8 @@
     col_owner, col_place = column_places(meta, nb, cols, width, per_d, held)
     col_pick = (iota((block, 3 * cols), 0) == col_place).astype(f32).astype(bf16)
     col_kept = iota((total, 3 * cols), 0) == col_owner
-    kind = iota((total, rows, block), 1)
-    packed = jnp.zeros((total, rows, block), f32)
+    line = iota((total, 8, block), 1)
+    packed = [jnp.zeros((total, 8, block), f32)] * 3
     entries = [
         (qkv_sum * meta[11].astype(f32), col_kept, col_pick),
         (sums[2:3, :ff], up_owner, pick96[...]),
@@ -726,34 +802,90 @@
     for k, (vector, where, pick) in enumerate(entries):
         for n, piece in enumerate(halves(vector)):
             spread = mm(jnp.where(where, piece, 0.0).astype(bf16), pick, NT)
-            packed = jnp.where(kind == k + 8 * n, spread[:, None, :], packed)
-    grads[:, :, 3 * cols :] = packed.reshape(nd, rows_d, block).astype(bf16)
-
-
-def unpack_kernel(per_d, nd, units, qkv, up, grad_qkv, grad_up, vector):
+            number = k + 8 * n
+            packed[number % 3] = jnp.where(line == number // 3, spread[:, None, :], packed[number % 3])
+    vector_rows = jnp.concatenate(packed, axis=2).reshape(nd, nc * 8, 3 * block).astype(bf16)
+    for d in range(nd):
+        grads[place(d), base + rows_d :, :] = vector_rows[d]
+
+
+def backward_kernel(
+    sizes, meta, near, far, weights, w_out, down, cosine, sine, begin, query, key, value, attended, stats, hidden, slope,
+    first_in, second_in, normed, vecs, own24, pick24, own96, pick96,
+    keep, give, part_near, part_far,
+    g_all, part, sums, pre_grad, d_qkv, d_query, d_key, d_value, grads,
+):
+    nd, nc, rows = sizes[0], sizes[1], sizes[5]
+    base = nc * rows + 2 * (down.shape[0] // nd) + 2 * HD
+
+    def place(d):
+        other = meta[12] ^ d
+        return (other >> 1) + (other & 1) * 2
+
+    mlp_back(
+        sizes, meta, near, far, weights, down, attended, hidden, slope, second_in, normed, vecs, part, g_all, sums, pre_grad,
+        grads, place,
+    )
+    attention_back(
+        sizes, meta, g_all, w_out, cosine, sine, begin, query, key, value, attended, stats, d_qkv, d_query, d_key, d_value
+    )
+    qkv_back(
+        sizes, meta, g_all, weights, d_qkv, first_in, normed, vecs, part, sums, own24, pick24, own96, pick96,
+        part_near, part_far, grads, place, base,
+    )
+    keep[...] = grads[:2]
+    give[...] = grads[2:]
+
+
+def unpack_kernel(per_d, nd, units, rows, back, grad_qkv, grad_up, *vectors):
     f32 = jnp.float32
-    nc = qkv.shape[0]
+    nc = back.shape[0]
     held = nd // 2
     width = grad_qkv.shape[1] // 3
     cols = held * HD
     pieces = [None] * (3 * per_d * nd)
     ups = [None] * (nd * nc)
-    total = jnp.zeros(vector.shape, f32)
+    total = jnp.zeros((8, 3 * 128), f32)
     for t in range(nc):
-        group, half = t // 3, t % 3
-        w = qkv[t].astype(f32)
-        if half < 2:
+        group, half = HEAD_OF[t // 2], t % 2
+        w = back[t].astype(f32)
+        if group is not None:
             for part in range(3):
                 for k in range(held):
                     at = part * cols + k * HD
-                    pieces[part * per_d * nd + per_d * (held * half + k) + group] = w[:, at : at + HD]
-        total = total + w[:, 3 * cols :]
-        u = up[t].astype(f32)
+                    pieces[part * per_d * nd + per_d * (held * half + k) + group] = w[rows : 2 * rows, at : at + HD]
+        total = total + w[2 * rows :]
         for k in range(nd):
-            ups[k * nc + t] = u[:, k * units : (k + 1) * units]
+            ups[k * nc + t] = w[:rows, k * units : (k + 1) * units]
     grad_qkv[...] = jnp.concatenate(pieces, axis=1)
     grad_up[...] = jnp.concatenate(ups, axis=1)
-    vector[...] = total
+
+    def kind(k):
+        return total[k // 3 : k // 3 + 1, 128 * (k % 3) : 128 * (k % 3) + 128]
+
+    for k, vector in enumerate(vectors):
+        vector[...] = (kind(k) + kind(k + 8))[:, : vector.shape[1]]
+
+
+def device_table(nd, nc):
+    table = []
+    for d in range(nd):
+        for c in range(nc):
+            group = HEAD_OF[c // 2]
+            spare = c ^ 1 ^ (6 if c // 2 == 1 else 2)
+            table.append([c ^ k for k in slot_order(nc)] + [c % 2, group or 0, c, int(group is not None), d, spare])
+    return np.asarray(table, np.int32)
+
+
+def final_kernel(inner, tokens, cotangent, m1, m2, m3, out):
+    f32 = jnp.float32
+    x = tokens[...].astype(f32)
+    centered = x - jnp.mean(x, axis=1, keepdims=True)
+    inverse = lax.rsqrt(jnp.mean(centered * centered, axis=1, keepdims=True) + eps)
+    normed = centered * inverse
+    n = inner[...] + m1[...].astype(f32) + m2[...].astype(f32) + m3[...].astype(f32)
+    n = n - jnp.mean(n, axis=1, keepdims=True) - normed * jnp.mean(n * normed, axis=1, keepdims=True)
+    out[...] = (cotangent[...].astype(f32) + n * inverse).astype(out.dtype)
 
 
 def head_split_plan(
@@ -787,137 +919,166 @@
     rows_d = nc * rows
     sizes = (nd, nc, per_d, held, nb, rows)
     d, c = lax.axis_index("dp"), lax.axis_index("ctx")
-    group, half = c // 3, c % 3
-    half_in = jnp.minimum(half, 1)
-    meta = jnp.concatenate(
-        [c ^ jnp.asarray(slot_order(nc), i32), jnp.stack([half_in, group, c, (half < 2).astype(i32)]).astype(i32)]
-    )
+    pair_index, half = c // 2, c % 2
+    group = jnp.where(pair_index == 3, 2, jnp.minimum(pair_index, 1))
+    active = pair_index != 2
     lane = np.arange(width)
     own24 = jnp.asarray((lane // rows)[None], i32)
     pick24 = jnp.asarray(np.arange(block)[:, None] == lane[None] % rows, bf16)
     unit = np.arange(ff)
     own96 = jnp.asarray((unit // units)[None], i32)
     pick96 = jnp.asarray(np.arange(block)[:, None] == unit[None] % units, bf16)
-    feature = np.arange(cols) % HD % (ROT // 2)
-    freq = jnp.asarray((10000.0 ** (-feature * 2.0 / ROT))[None], f32)
+    freq = jnp.asarray((10000.0 ** (-np.arange(ROT // 2) * 2.0 / ROT))[:, None], f32)
 
     vectors = [
         query_key_value_bias, up_input_bias, output_bias, down_output_bias, first_gain, first_shift, second_gain,
-        second_shift, segment_numbers.reshape(block).astype(bf16),
+        second_shift, segment_numbers,
     ]
-    vectors = jnp.stack([jnp.pad(v, (0, block - v.shape[0])) for v in vectors])
-    vectors = jnp.pad(vectors, ((0, rows - vectors.shape[0]), (0, 0)))
     lanes = 3 * cols + ff + block
-    (message,) = call(
+    bits = list(range(2, nc, 2))
+    target = active & ((d < nd // 2) == (half == 0))
+    meta = jnp.asarray(device_table(nd, nc), i32)
+    meta = lax.dynamic_index_in_dim(meta, d * nc + c, 0, False)
+    payload = lambda count: like((count, rows, lanes), bf16)
+    mine, to_two, to_four, to_six, _ = call(
         partial(message_kernel, per_d, nd, nc, units),
-        [like((nc, rows, lanes), bf16)],
-        [query_key_value_weight, up_matrix, vectors],
-        smem=False,
-    )
-    arrived = lax.all_to_all(message, "ctx", 0, 0, tiled=True)
-    x_near, x_far = gather_slots(tokens[0])
-    every = lax.all_gather(arrived.reshape(rows_d, lanes), "dp", axis=0, tiled=False)
-    w_down = lax.all_gather(down_matrix, "dp", axis=0, tiled=True)
+        [payload(3), payload(3), payload(2), payload(3), payload(nc)],
+        [meta, query_key_value_weight, up_matrix, output_matrix] + [v.reshape(1, -1) for v in vectors],
+        limit=VMEM_MOST,
+    )
+    two, four, six = swapped(to_two, 2), swapped(to_four, 4), swapped(to_six, 6)
+    x_own = after(tokens[0], two)
+    x_moved = [swapped(x_own, bit) for bit in bits]
+    message_far = swapped(
+        jnp.stack([mine[1], two[1], four[1], six[1], mine[2], jnp.where(pair_index == 1, six[2], two[2])]), 1
+    )
+    (package,) = call(
+        package_kernel,
+        [like((rows_d + units + HD, lanes), bf16)],
+        [meta, mine, two, four, six, message_far, down_matrix],
+        scratch=[pltpu.VMEM((nc, rows, lanes), f32)] * 2,
+        limit=VMEM_MOST,
+    )
+    x_near = jnp.stack([after(tokens[0], package)] + x_moved)
+    x_far = swapped(x_near, 1)
+    g_own = after(cotangent[0], *x_moved)
+    g_moved = [swapped(g_own, bit) for bit in bits]
+    g_near = jnp.stack([g_own] + g_moved)
+    g_far = swapped(after(g_near, x_far), 1)
     cosine, sine, begin = call(
-        tables_kernel, [like((length, cols), f32)] * 3, [arrived, freq], smem=False
-    )
-
-    two = [2 if k < nd // 2 else -2 for k in range(nd)]
-    after = between(output_matrix, [1] * nd)
-    before = between(output_matrix, [-1] * nd)
-    far = between(output_matrix, two)
-    strip = jnp.concatenate([far, before, output_matrix, after, far], axis=0)
-    in_lower = d < nd // 2
-    target = jnp.where(in_lower, half == 0, half == 1)
-    cut = jnp.where(target, HD * group - rows * (c - 2), 0)
-    outs = lax.all_gather(lax.dynamic_slice_in_dim(strip, cut, HD, 0), "dp", axis=0, tiled=False)
-    g_near, g_far = gather_slots(cotangent[0])
+        partial(tables_kernel, nc, rows), [like((length, cols), f32)] * 3, [package, freq], smem=False
+    )
+    across = swapped_dp(package, 2)
+    own_pair = jnp.stack([package, after(across, cosine, x_far, *g_moved)])
+    other_pair = swapped_dp(own_pair, 1)
 
     full = lambda dtype: like((length, width), dtype)
     part_shape = like((nc // 2, block, width), bf16)
     (
-        part_near, part_far, first_in, second_in, normed, query, key, value, attended, stats, hidden, slope, vecs,
+        out_near, out_far, first_in, second_in, normed, query, key, value, attended, stats, hidden, slope, vecs, weights,
+        w_out, w_down,
     ) = call(
         partial(forward_kernel, sizes),
         [part_shape, part_shape, full(bf16), full(bf16), full(bf16)]
         + [like((length, cols), bf16)] * 3
         + [like((length, cols), f32), like((length, 128), f32)]
         + [like((length, ff), bf16)] * 2
-        + [like((8, width), f32)],
-        [meta, x_near, x_far, every, w_down, outs, cosine, sine, begin, own24, pick24, own96, pick96],
-        flops=2 * length * width * (3 * cols + 2 * ff + cols) + 4 * held * length * length * HD,
-    )
-    mixed_sum = reduce_slots(part_near, part_far)
+        + [like((8, width), f32), like((width, 3 * cols + ff), bf16), like((cols, width), bf16), like((ff, width), bf16)],
+        [meta, x_near, x_far, own_pair, other_pair, cosine, sine, begin, own24, pick24, own96, pick96],
+        scratch=[pltpu.VMEM((nd, rows_d, lanes), bf16), pltpu.VMEM((nd, HD, width), bf16)],
+        flops=FORWARD_WORK,
+    )
+    half_rows = rows_d + 2 * units + 2 * HD
+    grad_rows = half_rows + rows_d + 8 * nc
+    keep, give, n_near, n_far = call(
+        partial(backward_kernel, sizes),
+        [like((nd // 2, grad_rows, 3 * cols), bf16)] * 2 + [part_shape, part_shape],
+        [meta, g_near, g_far, weights, w_out, w_down, cosine, sine, begin, query, key, value, attended, stats, hidden, slope,
+         first_in, second_in, normed, vecs, own24, pick24, own96, pick96],
+        scratch=[
+            pltpu.VMEM((length, width), bf16),
+            pltpu.VMEM((length, width), bf16),
+            pltpu.VMEM((8, width), f32),
+            pltpu.VMEM((length, ff), bf16),
+            pltpu.VMEM((length, 3 * cols), bf16),
+        ]
+        + [pltpu.VMEM((length, cols), f32)] * 3
+        + [pltpu.VMEM((nd, grad_rows, 3 * cols), bf16)],
+        flops=BACKWARD_WORK,
+    )
+
+    def near_sum(near, far):
+        total = near.astype(f32) + swapped(far, 1).astype(f32)
+        return total, total.astype(bf16)
+
+    out_total, out_low = near_sum(out_near, after(out_far, g_far))
+    n_far, give = lax.optimization_barrier((n_far, give, out_low))[:2]
+    grads = keep.astype(f32) + swapped_dp(give, 1).astype(f32)
+    grads_low = grads[1].astype(bf16)
+    out_low = after(out_low, grads_low)
+    out_moved = [swapped(out_low[1 + k], bit) for k, bit in enumerate(bits)]
+    grads_moved = swapped_dp(grads_low, 2)
+    n_total, n_low = near_sum(after(n_near, out_moved[0]), n_far)
+    n_low = after(n_low, out_moved[1], out_moved[2], grads_moved)
+    n_moved = [swapped(n_low[1 + k], bit) for k, bit in enumerate(bits)]
+    grads = grads[0] + after(grads_moved, n_moved[0]).astype(f32)
+    mixed_sum = sum((m.astype(f32) for m in out_moved), out_total[0])
     mixed = (tokens[0].astype(f32) + (mixed_sum + vecs[4])).astype(bf16)
-    grads_one, part, g_all, sums = call(
-        partial(mlp_back_kernel, sizes),
-        [like((nd, rows_d + 2 * units + 2 * HD, width // 2), bf16), full(bf16), full(bf16), like((8, width), f32)],
-        [meta, g_near, g_far, every, w_down, attended, hidden, slope, second_in, normed, vecs],
-        scratch=[pltpu.VMEM((length, ff), bf16)],
-        flops=2 * length * width * (4 * ff + cols),
-    )
-    grads_one = lax.psum_scatter(grads_one, "dp", scatter_dimension=0, tiled=False)
-    grads_two, n_near, n_far = call(
-        partial(attention_back_kernel, sizes),
-        [like((nd, rows_d, 3 * cols + block), bf16), part_shape, part_shape],
-        [meta, g_all, every, outs, cosine, sine, begin, query, key, value, attended, stats, first_in, normed, vecs, part,
-         sums, own24, pick24, own96, pick96],
-        scratch=[pltpu.VMEM((length, cols), bf16)]
-        + [pltpu.VMEM((length, cols), f32)] * 3
-        + [pltpu.VMEM((length, 3 * cols), bf16), pltpu.VMEM((8, 128), f32)],
-        flops=2 * length * width * (6 * cols + cols) + 10 * held * length * length * HD,
-    )
-    grads_two = lax.psum_scatter(grads_two, "dp", scatter_dimension=0, tiled=False)
-    inner_sum = reduce_slots(n_near, n_far)
-    own = cotangent[0].astype(f32)
-    own_x = tokens[0].astype(f32)
-    own_centered = own_x - jnp.mean(own_x, axis=-1, keepdims=True)
-    own_inverse = lax.rsqrt(jnp.mean(own_centered * own_centered, axis=-1, keepdims=True) + eps)
-    own_normed = own_centered * own_inverse
-    inner = (
-        inner_sum
-        - jnp.mean(inner_sum, axis=-1, keepdims=True)
-        - own_normed * jnp.mean(inner_sum * own_normed, axis=-1, keepdims=True)
-    )
-    tokens_grad = (own + inner * own_inverse).astype(bf16)
-
-    up_back = lax.all_to_all(grads_one[:rows_d].reshape(nc, rows, ff), "ctx", 0, 0, tiled=True)
-    at = rows_d + 2 * units
-    down_weight_grad = jnp.concatenate([grads_one[rows_d : rows_d + units], grads_one[rows_d + units : at]], axis=1)
-    head_rows = jnp.concatenate([grads_one[at : at + HD], grads_one[at + HD :]], axis=1)
+    (tokens_grad,) = call(
+        final_kernel, [like((block, width), bf16)], [n_total[0], tokens[0], cotangent[0]] + n_moved, smem=False
+    )
+    at_out = rows_d + 2 * units
+    at_qkv = at_out + 2 * HD
+    at_vec = at_qkv + rows_d
+    back = jnp.concatenate(
+        [
+            grads[:rows_d].reshape(nc, rows, ff),
+            grads[at_qkv:at_vec].reshape(nc, rows, 3 * cols),
+            grads[at_vec:].reshape(nc, 8, 3 * cols),
+        ],
+        axis=1,
+    )
+    back = lax.all_to_all(back.astype(bf16), "ctx", 0, 0, tiled=True)
+    down_weight_grad = jnp.concatenate([grads[rows_d : rows_d + units], grads[rows_d + units : at_out]], axis=1)
+    head_rows = jnp.concatenate([grads[at_out : at_out + HD], grads[at_out + HD : at_qkv]], axis=1).astype(bf16)
     head_rows = jnp.where(target, head_rows, jnp.zeros_like(head_rows))
-    strip_grad = lax.dynamic_update_slice(jnp.zeros((5 * rows, width), bf16), head_rows, (cut, 0))
-    strip_grad = strip_grad.reshape(5, rows, width)
-    out_weight_grad = (
-        strip_grad[2].astype(f32)
-        + between(strip_grad[1], [1] * nd).astype(f32)
-        + between(strip_grad[3], [-1] * nd).astype(f32)
-        + between(jnp.where(in_lower, strip_grad[4], strip_grad[0]), [-t for t in two]).astype(f32)
-    )
-    qkv_back = lax.all_to_all(grads_two.reshape(nc, rows, 3 * cols + block), "ctx", 0, 0, tiled=True)
-    qkv_weight_grad, up_weight_grad, vec = call(
-        partial(unpack_kernel, per_d, nd, units),
-        [like((rows, 3 * width), f32), like((rows, nc * ff), f32), like((rows, block), f32)],
-        [qkv_back, up_back],
+    strip = lax.dynamic_update_slice(jnp.zeros((rows_d, width), bf16), head_rows, (HD * group, 0))
+    strip = after(strip, n_moved[0], mixed)
+
+    def strip_block(index):
+        return lax.dynamic_slice_in_dim(strip, index * rows, rows, 0)
+
+    third = jnp.where(group == 0, 2, jnp.where(group == 1, 4, 5))
+    strips = [
+        swapped(strip_block(c ^ 1), 1),
+        sent(strip_block(third), lambda k: [(0, 2), (2, 4), (6, 5)] if k < nd // 2 else [(1, 2), (3, 4), (7, 5)]),
+        sent(strip_block(jnp.int32(5)), lambda k: [(2, 5)] if k < nd // 2 else [(3, 5)]),
+    ]
+    out_weight_grad = sum((m.astype(f32) for m in strips), strip_block(c).astype(f32))
+
+    qkv_weight_grad, up_weight_grad, *small = call(
+        partial(unpack_kernel, per_d, nd, units, rows),
+        [like((rows, 3 * width), f32), like((rows, nc * ff), f32), like((1, nb), f32), like((1, nu), f32)]
+        + [like((1, rows), f32)] * 5,
+        [back],
         smem=False,
     )
-    vec = vec[:7] + vec[8:15]
-    small = [vec[k, :rows] for k in range(2, 7)]
+    small = [v.reshape(-1) for v in small]
     return (
         mixed[None],
         tokens_grad[None],
         qkv_weight_grad,
-        vec[0, :nb],
+        small[0],
         out_weight_grad,
-        small[0],
+        small[2],
         up_weight_grad,
-        vec[1, :nu],
-        down_weight_grad.astype(f32),
-        small[0],
         small[1],
+        down_weight_grad,
         small[2],
         small[3],
         small[4],
+        small[5],
+        small[6],
     )
 
 

time: 232 us -> 160 us (0.69); the launches traced: 228 us -> 159 us
  blocking collectives: 33 us -> 0 us
  Pallas kernels: 48.1 us -> 32.4 us
  starting transfers between devices: 50.3 us -> 36.3 us
  between operations: 14.2 us -> 0.96 us
  waiting for transfers between devices: 65.3 us -> 75.2 us
  local copies, waits for them, and re-layouts: 12.2 us -> 7.32 us
    all_gather x2 -> x0, blocking collectives: 17.7 us -> none  [the longest x1 11.1 us: head_split_plan(): w_down = lax.all_gather(down_matrix, 'dp', axis=0, tiled=True)]
    pallas_call x6 -> x7, Pallas kernels: 48.1 us -> 32.4 us  [call(): pl.pallas_call(kernel, out_shape=[jax.ShapeDtypeStruct(o.shape, o.dtype)...]
    all_to_all x1 -> x0, blocking collectives: 15.3 us -> none  [head_split_plan(): arrived = lax.all_to_all(message, 'ctx', 0, 0, tiled=True)]
    ppermute x6, starting transfers between devices: 17.8 us -> 4.04 us  [the longest x4 2.1 us: swapped_dp(): return lax.ppermute(x, 'dp', [(i, i ^ bit) for i in range(size)])]
    ppermute x16 -> x21, starting transfers between devices: 17.3 us -> 26.8 us  [swapped(): return lax.ppermute(x, 'ctx', [(i, i ^ bit) for i in range(size)])]
    all_to_all x2 -> x1, starting transfers between devices: 14.9 us -> 5.49 us  [head_split_plan(): back = lax.all_to_all(back.astype(bf16), 'ctx', 0, 0, tiled=True)]
    ppermute x16 -> x21, waiting for transfers between devices: 61.2 us -> 69.7 us  [swapped(): return lax.ppermute(x, 'ctx', [(i, i ^ bit) for i in range(size)])]
    ppermute x6, waiting for transfers between devices: 0.02 us -> 5.51 us  [the longest x2 2.93 us: sent(): return lax.ppermute(x, ('dp', 'ctx'), flat)]
  transfers between devices with their start and end apart: 27 -> 28, of which waited for: 9 -> 19; matrix products, arithmetic and copies ran while one was open for 4% -> 4% of each run, Pallas kernels for 9% -> 18%
where the time goes in v3:
time: 160 us; the launch traced here: 159 us
  waiting for transfers between devices  75.2 us (47%)
  starting transfers between devices  36.3 us (23%)
  Pallas kernels  32.4 us (20%)
  local copies, waits for them, and re-layouts  7.32 us (5%)
  other arithmetic  6.72 us (4%)
    ppermute x21, waiting for transfers between devices, swapped(): return lax.ppermute(x, 'ctx', [(i, i ^ bit) for i in range(size)])  69.7 us
    pallas_call x7, Pallas kernels, call(): pl.pallas_call(kernel, out_shape=[jax.ShapeDtypeStruct(o.shape, o.dtype)...  32.4 us
    ppermute x21, starting transfers between devices, swapped(): return lax.ppermute(x, 'ctx', [(i, i ^ bit) for i in range(size)])  26.8 us
    all_to_all x1, starting transfers between devices, head_split_plan(): back = lax.all_to_all(back.astype(bf16), 'ctx', 0, 0, tiled=True)  5.49 us
    unnamed x36, local copies, waits for them, and re-layouts  4.99 us
  transfers between devices with their start and end apart: 28, of which 19 were waited for; matrix products, arithmetic and copies ran while one was open for 4% of the time, Pallas kernels for 18%

profile of v3, /device:TPU:18, one launch (start us, length us, event | category | flops | bytes accessed | tf_op | source)
XLA Modules:
  0.0 158.9 jit_solution(11135213818245934311)
XLA Ops:
  0.7 1.2 fusion.10.meta
  1.9 2.1 %shard_map.308 = (bf16[3,24,896]{2,1,0:T(8,128)(2,1)}, bf16[3,24,896]{2,1,0:T(8,128)(2,1)}, bf16[2,24,896]{2,1,0:T(8,128)(2,1)}, bf16[3,24,896]{2,1,0:T(8,128)(2,1)}, bf16[8,24,896]{2,1,0:T(8,128)(2,1)}) custom-call(s32[14]{0:T(128)} %fusion.10.meta, bf16[24,2304]{1,0:T(8,128)(2,1)} %qkv.1, bf16[24,3072]{1,0:T(8,128)(2,1)} %up.1, bf16[24,768]{1,0:T(8,128)(2,1)} %out_rows.1, ...), custom_call_target="tpu_custom_call" | custom-call | bytes 1024 | tf_op jit(solution)/shard_map/pallas_call | solution.py:385
  4.0 1.6 collective-permute-start
  5.9 1.6 collective-permute-start.2
  8.3 2.3 %collective-permute-done.two = bf16[3,24,896]{2,1,0:T(8,128)(2,1)S(1)} collective-permute-done((bf16[3,24,896]{2,1,0:T(8,128)(2,1)}, bf16[3,24,896]{2,1,0:T(8,128)(2,1)S(1)}, u32[]{:S(2)}, u32[]{:S(2)}) %collective-permute-start) | collective-permute-done | bytes 129056 | tf_op jit(solution)/shard_map/ppermute | solution.py:406
  10.6 3.1 %collective-permute-done.1.four = bf16[2,24,896]{2,1,0:T(8,128)(2,1)S(1)} collective-permute-done((bf16[2,24,896]{2,1,0:T(8,128)(2,1)}, bf16[2,24,896]{2,1,0:T(8,128)(2,1)S(1)}, u32[]{:S(2)}, u32[]{:S(2)}) %collective-permute-start.1) | collective-permute-done | bytes 86048 | tf_op jit(solution)/shard_map/ppermute | solution.py:406
  13.7 3.4 %collective-permute-done.2.six = bf16[3,24,896]{2,1,0:T(8,128)(2,1)S(1)} collective-permute-done((bf16[3,24,896]{2,1,0:T(8,128)(2,1)}, bf16[3,24,896]{2,1,0:T(8,128)(2,1)S(1)}, u32[]{:S(2)}, u32[]{:S(2)}) %collective-permute-start.2) | collective-permute-done | bytes 129056 | tf_op jit(solution)/shard_map/ppermute | solution.py:406
  18.0 1.6 collective-permute-start.3
  19.6 2.3 %collective-permute-start.5 = (bf16[128,768]{1,0:T(8,128)(2,1)}, bf16[128,768]{1,0:T(8,128)(2,1)S(1)}, u32[]{:S(2)}, u32[]{:S(2)}) collective-permute-start(bf16[128,768]{1,0:T(8,128)(2,1)} %bitcast.73), channel_id=1, source_target_pairs={{0,4},{1,5},{2,6},{3,7},{4,0},{5,1},{6,2},{7,3},{8,12},{9,13},{10,... | collective-permute-start | bytes 589832 | tf_op jit(solution)/shard_map/ppermute | solution.py:406
  21.8 1.2 collective-permute-start.6
  23.0 1.9 %collective-permute-done.3.far = bf16[6,24,896]{2,1,0:T(8,128)(2,1)S(1)} collective-permute-done((bf16[6,24,896]{2,1,0:T(8,128)(2,1)S(1)}, bf16[6,24,896]{2,1,0:T(8,128)(2,1)S(1)}, u32[]{:S(2)}, u32[]{:S(2)}) %collective-permute-start.3) | collective-permute-done | bytes 258080 | tf_op jit(solution)/shard_map/ppermute | solution.py:406
  25.7 2.3 %shard_map.309.package = bf16[352,896]{1,0:T(8,128)(2,1)} custom-call(s32[14]{0:T(128)} %fusion.10.meta, bf16[3,24,896]{2,1,0:T(8,128)(2,1)} %get-tuple-element.63.mine, bf16[3,24,896]{2,1,0:T(8,128)(2,1)} %copy-done.11, bf16[2,24,896]{2,1,0:T(8,128)(2,1)} %copy-done.14, bf16[3,24,896]{2,1,0:T(8,128)(2,1)} %copy-done.12, bf16[6,24,896]{2,1,0:T(8,128)(2,1)} %copy-done.13, ...), custom_call_target="tpu_custom_call" | custom-call | bytes 1024 | tf_op jit(solution)/shard_map/pallas_call | solution.py:385
  28.0 7.2 %collective-permute-done.5 = bf16[128,768]{1,0:T(8,128)(2,1)S(1)} collective-permute-done((bf16[128,768]{1,0:T(8,128)(2,1)}, bf16[128,768]{1,0:T(8,128)(2,1)S(1)}, u32[]{:S(2)}, u32[]{:S(2)}) %collective-permute-start.5) | collective-permute-done | bytes 196640 | tf_op jit(solution)/shard_map/ppermute | solution.py:406
  35.2 3.8 %collective-permute-done.6 = bf16[128,768]{1,0:T(8,128)(2,1)S(1)} collective-permute-done((bf16[128,768]{1,0:T(8,128)(2,1)}, bf16[128,768]{1,0:T(8,128)(2,1)S(1)}, u32[]{:S(2)}, u32[]{:S(2)}) %collective-permute-start.6) | collective-permute-done | bytes 196640 | tf_op jit(solution)/shard_map/ppermute | solution.py:406
  40.2 1.1 collective-permute-start.11
  41.3 3.3 %collective-permute-start.9 = (bf16[128,768]{1,0:T(8,128)(2,1)S(1)}, bf16[128,768]{1,0:T(8,128)(2,1)S(1)}, u32[]{:S(2)}, u32[]{:S(2)}) collective-permute-start(bf16[128,768]{1,0:T(8,128)(2,1)S(1)} %bitcast.78), channel_id=1, source_target_pairs={{0,2},{1,3},{2,0},{3,1},{4,6},{5,7},{6,4},{7,5},{8,10},{9,11},{10,... | collective-permute-start | bytes 589832 | tf_op jit(solution)/shard_map/ppermute | solution.py:406
  44.6 1.6 %shard_map.310 = (f32[1024,128]{1,0:T(8,128)S(1)}, f32[1024,128]{1,0:T(8,128)S(1)}, f32[1024,128]{1,0:T(8,128)S(1)}) custom-call(bf16[352,896]{1,0:T(8,128)(2,1)S(1)} %copy-done, f32[8,1]{1,0:T(8,128)S(1)} %copy-done.8), custom_call_target="tpu_custom_call" | custom-call | bytes 1024 | tf_op jit(solution)/shard_map/pallas_call | solution.py:385
  46.3 6.7 %collective-permute-done.10 = bf16[128,768]{1,0:T(8,128)(2,1)S(1)} collective-permute-done((bf16[128,768]{1,0:T(8,128)(2,1)S(1)}, bf16[128,768]{1,0:T(8,128)(2,1)S(1)}, u32[]{:S(2)}, u32[]{:S(2)}) %collective-permute-start.10) | collective-permute-done | bytes 196640 | tf_op jit(solution)/shard_map/ppermute | solution.py:406
  53.0 3.9 %collective-permute-done.11 = bf16[128,768]{1,0:T(8,128)(2,1)S(1)} collective-permute-done((bf16[128,768]{1,0:T(8,128)(2,1)S(1)}, bf16[128,768]{1,0:T(8,128)(2,1)S(1)}, u32[]{:S(2)}, u32[]{:S(2)}) %collective-permute-start.11) | collective-permute-done | bytes 196640 | tf_op jit(solution)/shard_map/ppermute | solution.py:406
  57.2 1.6 collective-permute-start.13
  58.8 1.3 collective-permute-done.12.other_pair
  60.1 10.6 %shard_map.311 = (bf16[4,128,768]{2,1,0:T(8,128)(2,1)S(1)}, bf16[4,128,768]{2,1,0:T(8,128)(2,1)S(1)}, bf16[1024,768]{1,0:T(8,128)(2,1)S(1)}, bf16[1024,768]{1,0:...) custom-call(s32[14]{0:T(128)S(1)} %copy-done.6, ...), custom_call_target="tpu_custom_call" | custom-call | flops 100000000 | bytes 1024 | tf_op jit(solution)/shard_map/pallas_call | solution.py:385
  70.7 6.5 %collective-permute-done.13.far = bf16[4,128,768]{2,1,0:T(8,128)(2,1)S(1)} collective-permute-done((bf16[4,128,768]{2,1,0:T(8,128)(2,1)S(1)}, bf16[4,128,768]{2,1,0:T(8,128)(2,1)S(1)}, u32[]{:S(2)}, u32[]{:S(2)}) %collective-permute-start.13) | collective-permute-done | bytes 786464 | tf_op jit(solution)/shard_map/ppermute | solution.py:406
  77.3 1.5 collective-permute-start.14
  78.8 13.8 %shard_map.312 = (bf16[2,768,384]{2,1,0:T(8,128)(2,1)S(1)}, bf16[2,768,384]{2,1,0:T(8,128)(2,1)S(1)}, bf16[4,128,768]{2,1,0:T(8,128)(2,1)S(1)}, bf16[4,128,768]{2,1,0:T(8,128)(2,1)S(1)}) custom-call(s32[14]{0:T(128)S(1)} %copy-done.6, bf16[4,128,768]{2,1,0:T(8,128)(2,1)S(1)} %pad_maximum_fusion.2.near, bf16[4,128,768]{2,1,0:T(8,128)(2,1)S(1)} %collective-permute-done.13.far, ...), custom_call_target="tpu_custom_call" | custom-call | flops 100000000 | bytes 1024 | tf_op jit(solution)/shard_map/pallas_call | solution.py:385
  92.5 3.9 %collective-permute-done.14 = bf16[4,128,768]{2,1,0:T(8,128)(2,1)S(1)} collective-permute-done((bf16[4,128,768]{2,1,0:T(8,128)(2,1)S(1)}, bf16[4,128,768]{2,1,0:T(8,128)(2,1)S(1)}, u32[]{:S(2)}, u32[]{:S(2)}) %collective-permute-start.14) | collective-permute-done | bytes 786464 | tf_op jit(solution)/shard_map/ppermute | solution.py:406
  96.4 1.6 fusion.11
  98.0 1.5 collective-permute-start.19
  99.5 1.3 collective-permute-done.15
  101.1 1.4 copy-done.9
  103.4 2.6 %collective-permute-start.17 = (bf16[128,768]{1,0:T(8,128)(2,1)}, bf16[128,768]{1,0:T(8,128)(2,1)}, u32[]{:S(2)}, u32[]{:S(2)}) collective-permute-start(bf16[128,768]{1,0:T(8,128)(2,1)} %get-tuple-element.125), channel_id=1, source_target_pairs={{0,4},{1,5},{2,6},{3,7},{4,0},{5,1},{6,2},{7,3},{8,12},{9,13},{10,... | collective-permute-start | bytes 589832 | tf_op jit(solution)/shard_map/ppermute | solution.py:406
  106.0 0.9 collective-permute-start.18
  106.9 1.5 collective-permute-start.20
  108.4 3.5 %collective-permute-done.16 = bf16[128,768]{1,0:T(8,128)(2,1)} collective-permute-done((bf16[128,768]{1,0:T(8,128)(2,1)}, bf16[128,768]{1,0:T(8,128)(2,1)}, u32[]{:S(2)}, u32[]{:S(2)}) %collective-permute-start.16) | collective-permute-done | bytes 196640 | tf_op jit(solution)/shard_map/ppermute | solution.py:406
  111.8 8.2 %collective-permute-done.17 = bf16[128,768]{1,0:T(8,128)(2,1)} collective-permute-done((bf16[128,768]{1,0:T(8,128)(2,1)}, bf16[128,768]{1,0:T(8,128)(2,1)}, u32[]{:S(2)}, u32[]{:S(2)}) %collective-permute-start.17) | collective-permute-done | bytes 196640 | tf_op jit(solution)/shard_map/ppermute | solution.py:406
  120.0 4.5 %collective-permute-done.18 = bf16[128,768]{1,0:T(8,128)(2,1)} collective-permute-done((bf16[128,768]{1,0:T(8,128)(2,1)}, bf16[128,768]{1,0:T(8,128)(2,1)}, u32[]{:S(2)}, u32[]{:S(2)}) %collective-permute-start.18) | collective-permute-done | bytes 196640 | tf_op jit(solution)/shard_map/ppermute | solution.py:406
  124.5 2.0 %fusion.7 = bf16[128,768]{1,0:T(8,128)(2,1)} fusion(f32[4,128,768]{2,1,0:T(8,128)} %get-tuple-element.117, bf16[128,768]{1,0:T(8,128)(2,1)} %collective-permute-done.18, bf16[128,768]{1,0:T(8,128)(2,1)} %collective-permute-done.17, bf16[128,768]{1,0:T(8,128)(2,1)} %collective-permute-done.16, f32[768]{0:T(1024)S(1)} %slice_reduce_fusion, ...), kind=kLoop, calls=%fused_computation.17 | loop fusion | flops 983040 | bytes 1379328 | tf_op jit(solution)/shard_map/convert_element_type | solution.py:1026
  126.9 2.7 %collective-permute-start.22 = (bf16[128,768]{1,0:T(8,128)(2,1)S(1)}, bf16[128,768]{1,0:T(8,128)(2,1)S(1)}, u32[]{:S(2)}, u32[]{:S(2)}) collective-permute-start(bf16[128,768]{1,0:T(8,128)(2,1)S(1)} %get-tuple-element.121), channel_id=1, source_target_pairs={{0,4},{1,5},{2,6},{3,7},{4,0},{5,1},{6,2},{7,3},{8,12},{9,13},{10,... | collective-permute-start | bytes 589832 | tf_op jit(solution)/shard_map/ppermute | solution.py:406
  130.4 4.3 %collective-permute-done.21.m1 = bf16[128,768]{1,0:T(8,128)(2,1)S(1)} collective-permute-done((bf16[128,768]{1,0:T(8,128)(2,1)S(1)}, bf16[128,768]{1,0:T(8,128)(2,1)S(1)}, u32[]{:S(2)}, u32[]{:S(2)}) %collective-permute-start.21) | collective-permute-done | bytes 196640 | tf_op jit(solution)/shard_map/ppermute | solution.py:406
  135.7 5.5 %all-to-all-start = ((bf16[8,56,384]{2,1,0:T(8,128)(2,1)}), bf16[8,56,384]{2,1,0:T(8,128)(2,1)S(1)}, u32[]{:S(2)}, u32[]{:S(2)}) async-start(bf16[8,56,384]{2,1,0:T(8,128)(2,1)} %pad_maximum_fusion.3), calls=%async_computation | async-start | bytes 688128 | tf_op jit(solution)/shard_map/all_to_all | solution.py:1041
  141.3 1.5 collective-permute-start.24
  142.8 1.3 collective-permute-start.25
  145.5 0.9 collective-permute-done.22.m2
  146.4 5.8 %collective-permute-done.23.m3 = bf16[128,768]{1,0:T(8,128)(2,1)S(1)} collective-permute-done((bf16[128,768]{1,0:T(8,128)(2,1)S(1)}, bf16[128,768]{1,0:T(8,128)(2,1)S(1)}, u32[]{:S(2)}, u32[]{:S(2)}) %collective-permute-start.23) | collective-permute-done | bytes 196640 | tf_op jit(solution)/shard_map/ppermute | solution.py:406
  152.2 1.1 shard_map.313
  153.3 2.9 %collective-permute-done.25 = bf16[24,768]{1,0:T(8,128)(2,1)S(1)} collective-permute-done((bf16[24,768]{1,0:T(8,128)(2,1)S(1)}, bf16[24,768]{1,0:T(8,128)(2,1)S(1)}, u32[]{:S(2)}, u32[]{:S(2)}) %collective-permute-start.25) | collective-permute-done | bytes 36896 | tf_op jit(solution)/shard_map/ppermute | solution.py:421
  156.8 0.9 shard_map.314
  157.7 1.2 copy.42
  (75 shorter events, 9.8 us)
Async XLA Ops:
  0.6 38.4 %copy-start.1 = (bf16[1,128,768]{2,1,0:T(8,128)(2,1)S(1)}, bf16[1,128,768]{2,1,0:T(8,128)(2,1)}, u32[]{:S(2)}) copy-start(bf16[1,128,768]{2,1,0:T(8,128)(2,1)} %param.21) | copy-start | bytes 589828
  4.0 6.5 %collective-permute-start = (bf16[3,24,896]{2,1,0:T(8,128)(2,1)}, bf16[3,24,896]{2,1,0:T(8,128)(2,1)S(1)}, u32[]{:S(2)}, u32[]{:S(2)}) collective-permute-start(bf16[3,24,896]{2,1,0:T(8,128)(2,1)} %get-tuple-element.64), channel_id=1, source_target_pairs={{0,2},{1,3},{2,0},{3,1},{4,6},{5,7},{6,4},{7,5},{8,10},{9,11},{10,... | collective-permute-start | bytes 387080 | tf_op jit(solution)/shard_map/ppermute | solution.py:406
  5.6 8.0 %collective-permute-start.1 = (bf16[2,24,896]{2,1,0:T(8,128)(2,1)}, bf16[2,24,896]{2,1,0:T(8,128)(2,1)S(1)}, u32[]{:S(2)}, u32[]{:S(2)}) collective-permute-start(bf16[2,24,896]{2,1,0:T(8,128)(2,1)} %get-tuple-element.65), channel_id=1, source_target_pairs={{0,4},{1,5},{2,6},{3,7},{4,0},{5,1},{6,2},{7,3},{8,12},{9,13},{10,... | collective-permute-start | bytes 258056 | tf_op jit(solution)/shard_map/ppermute | solution.py:406
  5.9 11.1 %collective-permute-start.2 = (bf16[3,24,896]{2,1,0:T(8,128)(2,1)}, bf16[3,24,896]{2,1,0:T(8,128)(2,1)S(1)}, u32[]{:S(2)}, u32[]{:S(2)}) collective-permute-start(bf16[3,24,896]{2,1,0:T(8,128)(2,1)} %get-tuple-element.66), channel_id=1, source_target_pairs={{0,6},{1,7},{2,4},{3,5},{4,2},{5,3},{6,0},{7,1},{8,14},{9,15},{10,... | collective-permute-start | bytes 387080 | tf_op jit(solution)/shard_map/ppermute | solution.py:406
  10.6 14.4 %copy-start.11 = (bf16[3,24,896]{2,1,0:T(8,128)(2,1)}, bf16[3,24,896]{2,1,0:T(8,128)(2,1)S(1)}, u32[]{:S(2)}) copy-start(bf16[3,24,896]{2,1,0:T(8,128)(2,1)S(1)} %collective-permute-done.two) | copy-start | bytes 387076
  13.6 11.4 %copy-start.14 = (bf16[2,24,896]{2,1,0:T(8,128)(2,1)}, bf16[2,24,896]{2,1,0:T(8,128)(2,1)S(1)}, u32[]{:S(2)}) copy-start(bf16[2,24,896]{2,1,0:T(8,128)(2,1)S(1)} %collective-permute-done.1.four) | copy-start | bytes 258052
  17.1 7.9 %copy-start.12 = (bf16[3,24,896]{2,1,0:T(8,128)(2,1)}, bf16[3,24,896]{2,1,0:T(8,128)(2,1)S(1)}, u32[]{:S(2)}) copy-start(bf16[3,24,896]{2,1,0:T(8,128)(2,1)S(1)} %collective-permute-done.2.six) | copy-start | bytes 387076
  17.9 22.3 %copy-start.2 = (bf16[1,128,768]{2,1,0:T(8,128)(2,1)S(1)}, bf16[1,128,768]{2,1,0:T(8,128)(2,1)}, u32[]{:S(2)}) copy-start(bf16[1,128,768]{2,1,0:T(8,128)(2,1)} %param.23) | copy-start | bytes 589828
  17.9 26.7 %copy-start.8 = (f32[8,1]{1,0:T(8,128)S(1)}, f32[8,1]{1,0:T(8,128)}, u32[]{:S(2)}) copy-start(f32[8,1]{1,0:T(8,128)} %constant.72.clone.freq) | copy-start | bytes 100
  18.0 7.0 %collective-permute-start.3 = (bf16[6,24,896]{2,1,0:T(8,128)(2,1)S(1)}, bf16[6,24,896]{2,1,0:T(8,128)(2,1)S(1)}, u32[]{:S(2)}, u32[]{:S(2)}) collective-permute-start(bf16[6,24,896]{2,1,0:T(8,128)(2,1)S(1)} %fusion.9), channel_id=1, source_target_pairs={{0,1},{1,0},{2,3},{3,2},{4,5},{5,4},{6,7},{7,6},{8,9},{9,8},{10,11... | collective-permute-start | bytes 774152 | tf_op jit(solution)/shard_map/ppermute | solution.py:406
  19.5 8.5 %collective-permute-start.4 = (bf16[128,768]{1,0:T(8,128)(2,1)}, bf16[128,768]{1,0:T(8,128)(2,1)S(1)}, u32[]{:S(2)}, u32[]{:S(2)}) collective-permute-start(bf16[128,768]{1,0:T(8,128)(2,1)} %bitcast.72), channel_id=1, source_target_pairs={{0,2},{1,3},{2,0},{3,1},{4,6},{5,7},{6,4},{7,5},{8,10},{9,11},{10,... | collective-permute-start | bytes 589832 | tf_op jit(solution)/shard_map/ppermute | solution.py:406
  19.6 15.6 %collective-permute-start.5 = (bf16[128,768]{1,0:T(8,128)(2,1)}, bf16[128,768]{1,0:T(8,128)(2,1)S(1)}, u32[]{:S(2)}, u32[]{:S(2)}) collective-permute-start(bf16[128,768]{1,0:T(8,128)(2,1)} %bitcast.73), channel_id=1, source_target_pairs={{0,4},{1,5},{2,6},{3,7},{4,0},{5,1},{6,2},{7,3},{8,12},{9,13},{10,... | collective-permute-start | bytes 589832 | tf_op jit(solution)/shard_map/ppermute | solution.py:406
  21.8 17.2 %collective-permute-start.6 = (bf16[128,768]{1,0:T(8,128)(2,1)}, bf16[128,768]{1,0:T(8,128)(2,1)S(1)}, u32[]{:S(2)}, u32[]{:S(2)}) collective-permute-start(bf16[128,768]{1,0:T(8,128)(2,1)} %bitcast.74), channel_id=1, source_target_pairs={{0,6},{1,7},{2,4},{3,5},{4,2},{5,3},{6,0},{7,1},{8,14},{9,15},{10,... | collective-permute-start | bytes 589832 | tf_op jit(solution)/shard_map/ppermute | solution.py:406
  25.0 0.7 copy-start.13
  28.0 11.7 %copy-start = (bf16[352,896]{1,0:T(8,128)(2,1)S(1)}, bf16[352,896]{1,0:T(8,128)(2,1)}, u32[]{:S(2)}) copy-start(bf16[352,896]{1,0:T(8,128)(2,1)} %shard_map.309.package) | copy-start | bytes 1892356
  39.1 17.8 %collective-permute-start.7 = (bf16[4,128,768]{2,1,0:T(8,128)(2,1)S(1)}, bf16[4,128,768]{2,1,0:T(8,128)(2,1)S(1)}, u32[]{:S(2)}, u32[]{:S(2)}) collective-permute-start(bf16[4,128,768]{2,1,0:T(8,128)(2,1)S(1)} %pad_maximum_fusion.1.near), channel_id=1, source_target_pairs={{0,1},{1,0},{2,3},{3,2},{4,5},{5,4},{6,7},{7,6},{8,9},{9,8},{10,11... | collective-permute-start | bytes 2359304 | tf_op jit(solution)/shard_map/ppermute | solution.py:406
  39.7 17.2 %collective-permute-start.8 = (bf16[352,896]{1,0:T(8,128)(2,1)S(1)}, bf16[352,896]{1,0:T(8,128)(2,1)S(1)}, u32[]{:S(2)}, u32[]{:S(2)}) collective-permute-start(bf16[352,896]{1,0:T(8,128)(2,1)S(1)} %copy-done), channel_id=1, source_target_pairs={{0,16},{8,24},{16,0},{24,8},{1,17},{9,25},{17,1},{25,9},{2,18},{10... | collective-permute-start | bytes 1892360 | tf_op jit(solution)/shard_map/ppermute | solution.py:411
  40.2 12.7 %collective-permute-start.10 = (bf16[128,768]{1,0:T(8,128)(2,1)S(1)}, bf16[128,768]{1,0:T(8,128)(2,1)S(1)}, u32[]{:S(2)}, u32[]{:S(2)}) collective-permute-start(bf16[128,768]{1,0:T(8,128)(2,1)S(1)} %bitcast.76), channel_id=1, source_target_pairs={{0,4},{1,5},{2,6},{3,7},{4,0},{5,1},{6,2},{7,3},{8,12},{9,13},{10,... | collective-permute-start | bytes 589832 | tf_op jit(solution)/shard_map/ppermute | solution.py:406
  40.2 16.6 %collective-permute-start.11 = (bf16[128,768]{1,0:T(8,128)(2,1)S(1)}, bf16[128,768]{1,0:T(8,128)(2,1)S(1)}, u32[]{:S(2)}, u32[]{:S(2)}) collective-permute-start(bf16[128,768]{1,0:T(8,128)(2,1)S(1)} %bitcast.77), channel_id=1, source_target_pairs={{0,6},{1,7},{2,4},{3,5},{4,2},{5,3},{6,0},{7,1},{8,14},{9,15},{10,... | collective-permute-start | bytes 589832 | tf_op jit(solution)/shard_map/ppermute | solution.py:406
  41.3 15.6 %collective-permute-start.9 = (bf16[128,768]{1,0:T(8,128)(2,1)S(1)}, bf16[128,768]{1,0:T(8,128)(2,1)S(1)}, u32[]{:S(2)}, u32[]{:S(2)}) collective-permute-start(bf16[128,768]{1,0:T(8,128)(2,1)S(1)} %bitcast.78), channel_id=1, source_target_pairs={{0,2},{1,3},{2,0},{3,1},{4,6},{5,7},{6,4},{7,5},{8,10},{9,11},{10,... | collective-permute-start | bytes 589832 | tf_op jit(solution)/shard_map/ppermute | solution.py:406
  56.9 3.2 %copy-start.3 = (bf16[128,768]{1,0:T(8,128)(2,1)S(1)}, bf16[128,768]{1,0:T(8,128)(2,1)}, u32[]{:S(2)}) copy-start(bf16[128,768]{1,0:T(8,128)(2,1)} %constant.69.clone.pick24) | copy-start | bytes 589828
  56.9 3.2 %copy-start.4 = (bf16[128,384]{1,0:T(8,128)(2,1)S(1)}, bf16[128,384]{1,0:T(8,128)(2,1)}, u32[]{:S(2)}) copy-start(bf16[128,384]{1,0:T(8,128)(2,1)} %constant.71.clone.pick96) | copy-start | bytes 294916
  56.9 3.2 %copy-start.5 = (s32[1,768]{1,0:T(1,128)S(1)}, s32[1,768]{1,0:T(1,128)}, u32[]{:S(2)}) copy-start(s32[1,768]{1,0:T(1,128)} %constant.68.clone.own24) | copy-start | bytes 9220
  56.9 3.2 %copy-start.6 = (s32[14]{0:T(128)S(1)}, s32[14]{0:T(128)}, u32[]{:S(2)}) copy-start(s32[14]{0:T(128)} %fusion.10.meta) | copy-start | bytes 172
  56.9 3.2 %copy-start.7 = (s32[1,384]{1,0:T(1,128)S(1)}, s32[1,384]{1,0:T(1,128)}, u32[]{:S(2)}) copy-start(s32[1,384]{1,0:T(1,128)} %constant.70.clone.own96) | copy-start | bytes 4612
  57.1 3.0 %collective-permute-start.12 = (bf16[2,352,896]{2,1,0:T(8,128)(2,1)S(1)}, bf16[2,352,896]{2,1,0:T(8,128)(2,1)S(1)}, u32[]{:S(2)}, u32[]{:S(2)}) collective-permute-start(bf16[2,352,896]{2,1,0:T(8,128)(2,1)S(1)} %pad_maximum_fusion.own_pair), channel_id=1, source_target_pairs={{0,8},{8,0},{16,24},{24,16},{1,9},{9,1},{17,25},{25,17},{2,10},{10... | collective-permute-start | bytes 3784712 | tf_op jit(solution)/shard_map/ppermute | solution.py:411
  57.2 20.0 %collective-permute-start.13 = (bf16[4,128,768]{2,1,0:T(8,128)(2,1)S(1)}, bf16[4,128,768]{2,1,0:T(8,128)(2,1)S(1)}, u32[]{:S(2)}, u32[]{:S(2)}) collective-permute-start(bf16[4,128,768]{2,1,0:T(8,128)(2,1)S(1)} %pad_maximum_fusion.2.near), channel_id=1, source_target_pairs={{0,1},{1,0},{2,3},{3,2},{4,5},{5,4},{6,7},{7,6},{8,9},{9,8},{10,11... | collective-permute-start | bytes 2359304 | tf_op jit(solution)/shard_map/ppermute | solution.py:406
  77.3 19.2 %collective-permute-start.14 = (bf16[4,128,768]{2,1,0:T(8,128)(2,1)S(1)}, bf16[4,128,768]{2,1,0:T(8,128)(2,1)S(1)}, u32[]{:S(2)}, u32[]{:S(2)}) collective-permute-start(bf16[4,128,768]{2,1,0:T(8,128)(2,1)S(1)} %get-tuple-element.77), channel_id=1, source_target_pairs={{0,1},{1,0},{2,3},{3,2},{4,5},{5,4},{6,7},{7,6},{8,9},{9,8},{10,11... | collective-permute-start | bytes 2359304 | tf_op jit(solution)/shard_map/ppermute | solution.py:406
  98.0 2.8 %collective-permute-start.15 = (bf16[2,768,384]{2,1,0:T(8,128)(2,1)S(1)}, bf16[2,768,384]{2,1,0:T(8,128)(2,1)S(1)}, u32[]{:S(2)}, u32[]{:S(2)}) collective-permute-start(bf16[2,768,384]{2,1,0:T(8,128)(2,1)S(1)} %get-tuple-element.95), channel_id=1, source_target_pairs={{0,8},{8,0},{16,24},{24,16},{1,9},{9,1},{17,25},{25,17},{2,10},{10... | collective-permute-start | bytes 3538952 | tf_op jit(solution)/shard_map/ppermute | solution.py:411
  98.0 28.5 %collective-permute-start.19 = (bf16[4,128,768]{2,1,0:T(8,128)(2,1)S(1)}, bf16[4,128,768]{2,1,0:T(8,128)(2,1)S(1)}, u32[]{:S(2)}, u32[]{:S(2)}) collective-permute-start(bf16[4,128,768]{2,1,0:T(8,128)(2,1)S(1)} %get-tuple-element.99), channel_id=1, source_target_pairs={{0,1},{1,0},{2,3},{3,2},{4,5},{5,4},{6,7},{7,6},{8,9},{9,8},{10,11... | collective-permute-start | bytes 2359304 | tf_op jit(solution)/shard_map/ppermute | solution.py:406
  101.1 1.4 copy-start.9
  103.4 8.5 %collective-permute-start.16 = (bf16[128,768]{1,0:T(8,128)(2,1)}, bf16[128,768]{1,0:T(8,128)(2,1)}, u32[]{:S(2)}, u32[]{:S(2)}) collective-permute-start(bf16[128,768]{1,0:T(8,128)(2,1)} %get-tuple-element.123), channel_id=1, source_target_pairs={{0,2},{1,3},{2,0},{3,1},{4,6},{5,7},{6,4},{7,5},{8,10},{9,11},{10,... | collective-permute-start | bytes 589832 | tf_op jit(solution)/shard_map/ppermute | solution.py:406
  103.4 16.7 %collective-permute-start.17 = (bf16[128,768]{1,0:T(8,128)(2,1)}, bf16[128,768]{1,0:T(8,128)(2,1)}, u32[]{:S(2)}, u32[]{:S(2)}) collective-permute-start(bf16[128,768]{1,0:T(8,128)(2,1)} %get-tuple-element.125), channel_id=1, source_target_pairs={{0,4},{1,5},{2,6},{3,7},{4,0},{5,1},{6,2},{7,3},{8,12},{9,13},{10,... | collective-permute-start | bytes 589832 | tf_op jit(solution)/shard_map/ppermute | solution.py:406
  106.0 18.5 %collective-permute-start.18 = (bf16[128,768]{1,0:T(8,128)(2,1)}, bf16[128,768]{1,0:T(8,128)(2,1)}, u32[]{:S(2)}, u32[]{:S(2)}) collective-permute-start(bf16[128,768]{1,0:T(8,128)(2,1)} %get-tuple-element.124), channel_id=1, source_target_pairs={{0,6},{1,7},{2,4},{3,5},{4,2},{5,3},{6,0},{7,1},{8,14},{9,15},{10,... | collective-permute-start | bytes 589832 | tf_op jit(solution)/shard_map/ppermute | solution.py:406
  106.9 19.9 %collective-permute-start.20 = (bf16[768,384]{1,0:T(8,128)(2,1)S(1)}, bf16[768,384]{1,0:T(8,128)(2,1)S(1)}, u32[]{:S(2)}, u32[]{:S(2)}) collective-permute-start(bf16[768,384]{1,0:T(8,128)(2,1)S(1)} %fusion.1), channel_id=1, source_target_pairs={{0,16},{8,24},{16,0},{24,8},{1,17},{9,25},{17,1},{25,9},{2,18},{10... | collective-permute-start | bytes 1769480 | tf_op jit(solution)/shard_map/ppermute | solution.py:411
  126.5 8.2 %copy-start.10 = (f32[2,768,384]{2,1,0:T(8,128)S(1)}, f32[2,768,384]{2,1,0:T(8,128)}, u32[]{:S(2)}) copy-start(f32[2,768,384]{2,1,0:T(8,128)} %copy-done.9) | copy-start | bytes 7077892
  126.8 7.9 %collective-permute-start.21 = (bf16[128,768]{1,0:T(8,128)(2,1)S(1)}, bf16[128,768]{1,0:T(8,128)(2,1)S(1)}, u32[]{:S(2)}, u32[]{:S(2)}) collective-permute-start(bf16[128,768]{1,0:T(8,128)(2,1)S(1)} %get-tuple-element.122), channel_id=1, source_target_pairs={{0,2},{1,3},{2,0},{3,1},{4,6},{5,7},{6,4},{7,5},{8,10},{9,11},{10,... | collective-permute-start | bytes 589832 | tf_op jit(solution)/shard_map/ppermute | solution.py:406
  126.9 19.5 %collective-permute-start.22 = (bf16[128,768]{1,0:T(8,128)(2,1)S(1)}, bf16[128,768]{1,0:T(8,128)(2,1)S(1)}, u32[]{:S(2)}, u32[]{:S(2)}) collective-permute-start(bf16[128,768]{1,0:T(8,128)(2,1)S(1)} %get-tuple-element.121), channel_id=1, source_target_pairs={{0,4},{1,5},{2,6},{3,7},{4,0},{5,1},{6,2},{7,3},{8,12},{9,13},{10,... | collective-permute-start | bytes 589832 | tf_op jit(solution)/shard_map/ppermute | solution.py:406
  129.6 22.6 %collective-permute-start.23 = (bf16[128,768]{1,0:T(8,128)(2,1)S(1)}, bf16[128,768]{1,0:T(8,128)(2,1)S(1)}, u32[]{:S(2)}, u32[]{:S(2)}) collective-permute-start(bf16[128,768]{1,0:T(8,128)(2,1)S(1)} %get-tuple-element.120), channel_id=1, source_target_pairs={{0,6},{1,7},{2,4},{3,5},{4,2},{5,3},{6,0},{7,1},{8,14},{9,15},{10,... | collective-permute-start | bytes 589832 | tf_op jit(solution)/shard_map/ppermute | solution.py:406
  135.7 21.1 %all-to-all-start = ((bf16[8,56,384]{2,1,0:T(8,128)(2,1)}), bf16[8,56,384]{2,1,0:T(8,128)(2,1)S(1)}, u32[]{:S(2)}, u32[]{:S(2)}) async-start(bf16[8,56,384]{2,1,0:T(8,128)(2,1)} %pad_maximum_fusion.3), calls=%async_computation | async-start | bytes 688128 | tf_op jit(solution)/shard_map/all_to_all | solution.py:1041
  141.3 12.0 %collective-permute-start.24 = (bf16[24,768]{1,0:T(8,128)(2,1)S(1)}, bf16[24,768]{1,0:T(8,128)(2,1)S(1)}, u32[]{:S(2)}, u32[]{:S(2)}) collective-permute-start(bf16[24,768]{1,0:T(8,128)(2,1)S(1)} %get-tuple-element.131), channel_id=1, source_target_pairs={{0,1},{1,0},{2,3},{3,2},{4,5},{5,4},{6,7},{7,6},{8,9},{9,8},{10,11... | collective-permute-start | bytes 110600 | tf_op jit(solution)/shard_map/ppermute | solution.py:406
  142.8 13.4 %collective-permute-start.25 = (bf16[24,768]{1,0:T(8,128)(2,1)S(1)}, bf16[24,768]{1,0:T(8,128)(2,1)S(1)}, u32[]{:S(2)}, u32[]{:S(2)}) collective-permute-start(bf16[24,768]{1,0:T(8,128)(2,1)S(1)} %get-tuple-element.133), channel_id=1, source_target_pairs={{0,2},{2,4},{6,5},{8,10},{10,12},{14,13},{17,18},{19,20},{23,21},{... | collective-permute-start | bytes 110600 | tf_op jit(solution)/shard_map/ppermute | solution.py:421
  144.1 12.1 %collective-permute-start.26 = (bf16[24,768]{1,0:T(8,128)(2,1)S(1)}, bf16[24,768]{1,0:T(8,128)(2,1)S(1)}, u32[]{:S(2)}, u32[]{:S(2)}) collective-permute-start(bf16[24,768]{1,0:T(8,128)(2,1)S(1)} %get-tuple-element.132), channel_id=1, source_target_pairs={{2,5},{10,13},{19,21},{27,29}} | collective-permute-start | bytes 110600 | tf_op jit(solution)/shard_map/ppermute | solution.py:421

commit v4 on v3

--- a/solution.py
+++ b/solution.py
@@ -421,6 +421,16 @@
     return lax.ppermute(x, ("dp", "ctx"), flat)
 
 
+def gathered_block(meta, i, pairs):
+    return 2 * (i % pairs) + ((meta[8] + i // pairs) & 1)
+
+
+def pair_exchange(x):
+    size = lax.axis_size("ctx")
+    groups = [list(range(half, size, 2)) for half in range(2)]
+    return lax.all_to_all(x, "ctx", 0, 0, axis_index_groups=groups, tiled=True)
+
+
 def iota(shape, dim):
     return lax.broadcasted_iota(jnp.int32, shape, dim)
 
@@ -561,7 +571,7 @@
 
 def forward_kernel(
     sizes, meta, near, far, own_pair, other_pair, cosine, sine, begin, own24, pick24, own96, pick96,
-    out_near, out_far, first_in, second_in, normed, query, key, value, attended, stats, hidden, slope, vecs, weights,
+    out_near, out_near_own, out_far, out_far_own, first_in, second_in, normed, query, key, value, attended, probs, hidden, slope, vecs, weights,
     w_out, down, every, outs,
 ):
     f32, bf16 = jnp.float32, jnp.bfloat16
@@ -606,7 +616,7 @@
         x = half[i % (nc // 2)].astype(f32)
         centered = x - jnp.mean(x, axis=1, keepdims=True)
         n = centered * lax.rsqrt(jnp.mean(centered * centered, axis=1, keepdims=True) + eps)
-        at = pl.ds(pl.multiple_of(meta[i] * block, block), block)
+        at = pl.ds(pl.multiple_of(gathered_block(meta, i, nc // 2) * block, block), block)
         normed[at, :] = n.astype(bf16)
         first_in[at, :] = (n * g_one + s_one).astype(bf16)
         second_in[at, :] = (n * g_two + s_two).astype(bf16)
@@ -638,15 +648,19 @@
             top = jnp.max(s, axis=1, keepdims=True)
             p = jnp.exp(s - top)
             inverse = 1.0 / jnp.sum(p, axis=1, keepdims=True)
-            result = jnp.where(mine, mm((p * inverse).astype(bf16), value[:keys, :]), result)
-            stats[at, 2 * h : 2 * h + 1] = top
-            stats[at, 2 * h + 1 : 2 * h + 2] = inverse
+            low = (p * inverse).astype(bf16)
+            probs[h, at, :keys] = low
+            result = jnp.where(mine, mm(low, value[:keys, :]), result)
         attended[at, :] = result
     for i in range(nc):
-        half = out_near if i < nc // 2 else out_far
+        slot = i % (nc // 2)
+        rest, own = (out_near, out_near_own) if i < nc // 2 else (out_far, out_far_own)
         at = pl.ds(pl.multiple_of(meta[i] * block, block), block)
         piece = mm(attended[at, :].astype(bf16), w_out[...]) + mm(hidden[at, :], down[...])
-        half[i % (nc // 2)] = piece.astype(bf16)
+        if slot == 0:
+            own[...] = piece.astype(bf16)
+        else:
+            rest[slot - 1] = piece.astype(bf16)
 
 
 def mlp_back(
@@ -662,7 +676,8 @@
     length = nc * block
     for i in range(nc):
         half = near if i < nc // 2 else far
-        g_all[pl.ds(pl.multiple_of(meta[i] * block, block), block), :] = half[i % (nc // 2)]
+        at = pl.ds(pl.multiple_of(meta[i] * block, block), block)
+        g_all[at, :] = half[i % (nc // 2)]
     g = g_all[...]
     rows_d = width // nd
     side = width // 2
@@ -706,7 +721,7 @@
 
 
 def attention_back(
-    sizes, meta, g_all, w_out, cosine, sine, begin, query, key, value, attended, stats, d_qkv, d_query, d_key, d_value
+    sizes, meta, g_all, w_out, cosine, sine, query, key, value, attended, probs, d_qkv, d_query, d_key, d_value
 ):
     f32, bf16 = jnp.float32, jnp.bfloat16
     nd, nc, per_d, held, nb, rows = sizes
@@ -720,7 +735,6 @@
     for b in range(length // step):
         at = pl.ds(b * step, step)
         keys = (b + 1) * step
-        allowed = allowed_pairs(begin[at, 0:1], b * step, step, keys)
         q = query[at, :]
         back = mm(g_all[at, :], w_out[...], NT).astype(bf16)
         product = back.astype(f32) * attended[at, :]
@@ -730,14 +744,13 @@
             q_h = jnp.where(mine, q, jnp.zeros_like(q))
             back_h = jnp.where(mine, back, jnp.zeros_like(back))
             delta = jnp.sum(jnp.where(mine, product, 0.0), axis=1, keepdims=True)
-            s = mm(q_h, key[:keys, :], NT) * scale
-            p = jnp.exp(s - stats[at, 2 * h : 2 * h + 1]) * stats[at, 2 * h + 1 : 2 * h + 2]
-            p = jnp.where(allowed, p, 0.0)
+            low = probs[h, at, :keys]
+            p = low.astype(f32)
             d_p = mm(back_h, value[:keys, :], NT)
             d_s = (p * (d_p - delta)).astype(bf16)
             result = jnp.where(mine, mm(d_s, key[:keys, :]), result)
             d_key[:keys, :] += mm(d_s, q_h, TN)
-            d_value[:keys, :] += mm(p.astype(bf16), back_h, TN)
+            d_value[:keys, :] += mm(low, back_h, TN)
         d_query[at, :] = result
     for b in range(length // step):
         at = pl.ds(b * step, step)
@@ -810,7 +823,7 @@
 
 
 def backward_kernel(
-    sizes, meta, near, far, weights, w_out, down, cosine, sine, begin, query, key, value, attended, stats, hidden, slope,
+    sizes, meta, near, far, weights, w_out, down, cosine, sine, query, key, value, attended, probs, hidden, slope,
     first_in, second_in, normed, vecs, own24, pick24, own96, pick96,
     keep, give, part_near, part_far,
     g_all, part, sums, pre_grad, d_qkv, d_query, d_key, d_value, grads,
@@ -827,7 +840,7 @@
         grads, place,
     )
     attention_back(
-        sizes, meta, g_all, w_out, cosine, sine, begin, query, key, value, attended, stats, d_qkv, d_query, d_key, d_value
+        sizes, meta, g_all, w_out, cosine, sine, query, key, value, attended, probs, d_qkv, d_query, d_key, d_value
     )
     qkv_back(
         sizes, meta, g_all, weights, d_qkv, first_in, normed, vecs, part, sums, own24, pick24, own96, pick96,
@@ -947,8 +960,11 @@
         limit=VMEM_MOST,
     )
     two, four, six = swapped(to_two, 2), swapped(to_four, 4), swapped(to_six, 6)
-    x_own = after(tokens[0], two)
-    x_moved = [swapped(x_own, bit) for bit in bits]
+    copies = (nc // 2, block, width)
+    x_near = pair_exchange(jnp.broadcast_to(after(tokens, two), copies))
+    g_own = after(cotangent[0], x_near)
+    g_moved = [swapped(g_own, bit) for bit in bits]
+    g_near = jnp.stack([g_own] + g_moved)
     message_far = swapped(
         jnp.stack([mine[1], two[1], four[1], six[1], mine[2], jnp.where(pair_index == 1, six[2], two[2])]), 1
     )
@@ -959,11 +975,7 @@
         scratch=[pltpu.VMEM((nc, rows, lanes), f32)] * 2,
         limit=VMEM_MOST,
     )
-    x_near = jnp.stack([after(tokens[0], package)] + x_moved)
-    x_far = swapped(x_near, 1)
-    g_own = after(cotangent[0], *x_moved)
-    g_moved = [swapped(g_own, bit) for bit in bits]
-    g_near = jnp.stack([g_own] + g_moved)
+    x_far = swapped(after(x_near, package), 1)
     g_far = swapped(after(g_near, x_far), 1)
     cosine, sine, begin = call(
         partial(tables_kernel, nc, rows), [like((length, cols), f32)] * 3, [package, freq], smem=False
@@ -975,13 +987,13 @@
     full = lambda dtype: like((length, width), dtype)
     part_shape = like((nc // 2, block, width), bf16)
     (
-        out_near, out_far, first_in, second_in, normed, query, key, value, attended, stats, hidden, slope, vecs, weights,
+        out_near, out_near_own, out_far, out_far_own, first_in, second_in, normed, query, key, value, attended, probs, hidden, slope, vecs, weights,
         w_out, w_down,
     ) = call(
         partial(forward_kernel, sizes),
-        [part_shape, part_shape, full(bf16), full(bf16), full(bf16)]
+        [like((nc // 2 - 1, block, width), bf16), like((block, width), bf16)] * 2 + [full(bf16)] * 3
         + [like((length, cols), bf16)] * 3
-        + [like((length, cols), f32), like((length, 128), f32)]
+        + [like((length, cols), f32), like((held, length, length), bf16)]
         + [like((length, ff), bf16)] * 2
         + [like((8, width), f32), like((width, 3 * cols + ff), bf16), like((cols, width), bf16), like((ff, width), bf16)],
         [meta, x_near, x_far, own_pair, other_pair, cosine, sine, begin, own24, pick24, own96, pick96],
@@ -993,7 +1005,7 @@
     keep, give, n_near, n_far = call(
         partial(backward_kernel, sizes),
         [like((nd // 2, grad_rows, 3 * cols), bf16)] * 2 + [part_shape, part_shape],
-        [meta, g_near, g_far, weights, w_out, w_down, cosine, sine, begin, query, key, value, attended, stats, hidden, slope,
+        [meta, g_near, g_far, weights, w_out, w_down, cosine, sine, query, key, value, attended, probs, hidden, slope,
          first_in, second_in, normed, vecs, own24, pick24, own96, pick96],
         scratch=[
             pltpu.VMEM((length, width), bf16),
@@ -1011,22 +1023,18 @@
         total = near.astype(f32) + swapped(far, 1).astype(f32)
         return total, total.astype(bf16)
 
-    out_total, out_low = near_sum(out_near, after(out_far, g_far))
+    out_low = near_sum(out_near, after(out_far, g_far))[1]
     n_far, give = lax.optimization_barrier((n_far, give, out_low))[:2]
-    grads = keep.astype(f32) + swapped_dp(give, 1).astype(f32)
+    give_moved = swapped_dp(give, 1)
+    grads = keep.astype(f32) + give_moved.astype(f32)
     grads_low = grads[1].astype(bf16)
     out_low = after(out_low, grads_low)
-    out_moved = [swapped(out_low[1 + k], bit) for k, bit in enumerate(bits)]
+    out_moved = [swapped(out_low[k], bit) for k, bit in enumerate(bits)]
     grads_moved = swapped_dp(grads_low, 2)
     n_total, n_low = near_sum(after(n_near, out_moved[0]), n_far)
     n_low = after(n_low, out_moved[1], out_moved[2], grads_moved)
     n_moved = [swapped(n_low[1 + k], bit) for k, bit in enumerate(bits)]
-    grads = grads[0] + after(grads_moved, n_moved[0]).astype(f32)
-    mixed_sum = sum((m.astype(f32) for m in out_moved), out_total[0])
-    mixed = (tokens[0].astype(f32) + (mixed_sum + vecs[4])).astype(bf16)
-    (tokens_grad,) = call(
-        final_kernel, [like((block, width), bf16)], [n_total[0], tokens[0], cotangent[0]] + n_moved, smem=False
-    )
+    grads = grads[0] + grads_moved.astype(f32)
     at_out = rows_d + 2 * units
     at_qkv = at_out + 2 * HD
     at_vec = at_qkv + rows_d
@@ -1043,14 +1051,18 @@
     head_rows = jnp.concatenate([grads[at_out : at_out + HD], grads[at_out + HD : at_qkv]], axis=1).astype(bf16)
     head_rows = jnp.where(target, head_rows, jnp.zeros_like(head_rows))
     strip = lax.dynamic_update_slice(jnp.zeros((rows_d, width), bf16), head_rows, (HD * group, 0))
-    strip = after(strip, n_moved[0], mixed)
+    out_sum = sum((m.astype(f32) for m in out_moved), out_near_own.astype(f32))
+    strip = after(strip, n_moved[0], out_sum)
 
     def strip_block(index):
         return lax.dynamic_slice_in_dim(strip, index * rows, rows, 0)
 
     third = jnp.where(group == 0, 2, jnp.where(group == 1, 4, 5))
+    both = swapped(jnp.concatenate([strip_block(c ^ 1), out_far_own], axis=0), 1)
+    mixed_sum = out_sum + both[rows:].astype(f32)
+    mixed = (tokens[0].astype(f32) + (mixed_sum + vecs[4])).astype(bf16)
     strips = [
-        swapped(strip_block(c ^ 1), 1),
+        both[:rows],
         sent(strip_block(third), lambda k: [(0, 2), (2, 4), (6, 5)] if k < nd // 2 else [(1, 2), (3, 4), (7, 5)]),
         sent(strip_block(jnp.int32(5)), lambda k: [(2, 5)] if k < nd // 2 else [(3, 5)]),
     ]
@@ -1061,6 +1073,12 @@
         [like((rows, 3 * width), f32), like((rows, nc * ff), f32), like((1, nb), f32), like((1, nu), f32)]
         + [like((1, rows), f32)] * 5,
         [back],
+        smem=False,
+    )
+    (tokens_grad,) = call(
+        final_kernel,
+        [like((block, width), bf16)],
+        [after(n_total[0], small[0]), tokens[0], cotangent[0]] + n_moved,
         smem=False,
     )
     small = [v.reshape(-1) for v in small]

time: 160 us -> 157 us (0.981)
  waiting for transfers between devices: 75.2 us -> 70.1 us
  local copies, waits for them, and re-layouts: 7.32 us -> 11.9 us
  other arithmetic: 6.72 us -> 4.84 us
    ppermute x21 -> x18, waiting for transfers between devices: 69.7 us -> 36.7 us  [swapped(): return lax.ppermute(x, 'ctx', [(i, i ^ bit) for i in range(size)])]
    ppermute x2, waiting for transfers between devices: 2.93 us -> 15.8 us  [sent(): return lax.ppermute(x, ('dp', 'ctx'), flat)]
    ppermute x4, waiting for transfers between devices: 2.58 us -> 12.5 us  [swapped_dp(): return lax.ppermute(x, 'dp', [(i, i ^ bit) for i in range(size)])]
    all_to_all x0 -> x1, starting transfers between devices: none -> 5.49 us  [pair_exchange(): return lax.all_to_all(x, 'ctx', 0, 0, axis_index_groups=groups, tiled=True)]
    all_to_all x0 -> x1, waiting for transfers between devices: none -> 5.07 us  [pair_exchange(): return lax.all_to_all(x, 'ctx', 0, 0, axis_index_groups=groups, tiled=True)]
    ppermute x21 -> x18, starting transfers between devices: 26.8 us -> 23.4 us  [swapped(): return lax.ppermute(x, 'ctx', [(i, i ^ bit) for i in range(size)])]
    convert_element_type x1 -> x0, other arithmetic: 2.01 us -> none  [head_split_plan(): mixed = (tokens[0].astype(f32) + (mixed_sum + vecs[4])).astype(bf16)]
    broadcast_in_dim x0 -> x1, local copies, waits for them, and re-layouts: none -> 1.91 us  [head_split_plan(): x_near = pair_exchange(jnp.broadcast_to(after(tokens, two), copies))]
  transfers between devices with their start and end apart: 28 -> 26, of which waited for: 19 -> 16; matrix products, arithmetic and copies ran while one was open for 4% -> 6% of each run, Pallas kernels for 18% -> 18%
where the time goes in v4:
time: 157 us; the launch traced here: 156 us
  waiting for transfers between devices  70.1 us (45%)
  starting transfers between devices  37.3 us (24%)
  Pallas kernels  31.4 us (20%)
  local copies, waits for them, and re-layouts  11.9 us (8%)
  other arithmetic  4.84 us (3%)
    ppermute x18, waiting for transfers between devices, swapped(): return lax.ppermute(x, 'ctx', [(i, i ^ bit) for i in range(size)])  36.7 us
    pallas_call x7, Pallas kernels, call(): pl.pallas_call(kernel, out_shape=[jax.ShapeDtypeStruct(o.shape, o.dtype)...  31.4 us
    ppermute x18, starting transfers between devices, swapped(): return lax.ppermute(x, 'ctx', [(i, i ^ bit) for i in range(size)])  23.4 us
    ppermute x2, waiting for transfers between devices, sent(): return lax.ppermute(x, ('dp', 'ctx'), flat)  15.8 us
    ppermute x4, waiting for transfers between devices, swapped_dp(): return lax.ppermute(x, 'dp', [(i, i ^ bit) for i in range(size)])  12.5 us
    all_to_all x1, starting transfers between devices, pair_exchange(): return lax.all_to_all(x, 'ctx', 0, 0, axis_index_groups=groups, tiled=True)  5.49 us
    unnamed x38, local copies, waits for them, and re-layouts  5.48 us
    all_to_all x1, waiting for transfers between devices, pair_exchange(): return lax.all_to_all(x, 'ctx', 0, 0, axis_index_groups=groups, tiled=True)  5.07 us
  transfers between devices with their start and end apart: 26, of which 16 were waited for; matrix products, arithmetic and copies ran while one was open for 6% of the time, Pallas kernels for 18%

profile of v4, /device:TPU:18, one launch (start us, length us, event | category | flops | bytes accessed | tf_op | source)
XLA Modules:
  0.0 156.5 jit_solution(11825405880158922143)
XLA Ops:
  0.7 1.2 fusion.5.meta
  1.9 2.1 %shard_map.308 = (bf16[3,24,896]{2,1,0:T(8,128)(2,1)}, bf16[3,24,896]{2,1,0:T(8,128)(2,1)}, bf16[2,24,896]{2,1,0:T(8,128)(2,1)}, bf16[3,24,896]{2,1,0:T(8,128)(2,1)}, bf16[8,24,896]{2,1,0:T(8,128)(2,1)}) custom-call(s32[14]{0:T(128)} %fusion.5.meta, bf16[24,2304]{1,0:T(8,128)(2,1)} %qkv.1, bf16[24,3072]{1,0:T(8,128)(2,1)} %up.1, bf16[24,768]{1,0:T(8,128)(2,1)} %out_rows.1, ...), custom_call_target="tpu_custom_call" | custom-call | bytes 1024 | tf_op jit(solution)/shard_map/pallas_call | solution.py:385
  4.0 1.6 %collective-permute-start = (bf16[3,24,896]{2,1,0:T(8,128)(2,1)}, bf16[3,24,896]{2,1,0:T(8,128)(2,1)S(1)}, u32[]{:S(2)}, u32[]{:S(2)}) collective-permute-start(bf16[3,24,896]{2,1,0:T(8,128)(2,1)} %get-tuple-element.65), channel_id=1, source_target_pairs={{0,2},{1,3},{2,0},{3,1},{4,6},{5,7},{6,4},{7,5},{8,10},{9,11},{10,... | collective-permute-start | bytes 387080 | tf_op jit(solution)/shard_map/ppermute | solution.py:406
  5.9 1.6 %collective-permute-start.2 = (bf16[3,24,896]{2,1,0:T(8,128)(2,1)}, bf16[3,24,896]{2,1,0:T(8,128)(2,1)S(1)}, u32[]{:S(2)}, u32[]{:S(2)}) collective-permute-start(bf16[3,24,896]{2,1,0:T(8,128)(2,1)} %get-tuple-element.69), channel_id=1, source_target_pairs={{0,6},{1,7},{2,4},{3,5},{4,2},{5,3},{6,0},{7,1},{8,14},{9,15},{10,... | collective-permute-start | bytes 387080 | tf_op jit(solution)/shard_map/ppermute | solution.py:406
  7.5 0.8 slice_dynamic-update-slice_fusion.4
  8.2 2.3 %collective-permute-done.two = bf16[3,24,896]{2,1,0:T(8,128)(2,1)S(1)} collective-permute-done((bf16[3,24,896]{2,1,0:T(8,128)(2,1)}, bf16[3,24,896]{2,1,0:T(8,128)(2,1)S(1)}, u32[]{:S(2)}, u32[]{:S(2)}) %collective-permute-start) | collective-permute-done | bytes 129056 | tf_op jit(solution)/shard_map/ppermute | solution.py:406
  10.5 1.9 %broadcast_in_dim.20 = bf16[4,128,768]{2,1,0:T(8,128)(2,1)} broadcast(bf16[128,768]{1,0:T(8,128)(2,1)} %bitcast.56), dimensions={1,2} | broadcast | bytes 983040 | tf_op jit(solution)/shard_map/broadcast_in_dim | solution.py:964
  12.4 5.5 %all-to-all-start = ((bf16[4,128,768]{2,1,0:T(8,128)(2,1)}), bf16[4,128,768]{2,1,0:T(8,128)(2,1)S(1)}, u32[]{:S(2)}, u32[]{:S(2)}) async-start(bf16[4,128,768]{2,1,0:T(8,128)(2,1)} %broadcast_in_dim.20), calls=%async_computation | async-start | bytes 1572864 | tf_op jit(solution)/shard_map/all_to_all | solution.py:431
  18.0 0.9 slice_dynamic-update-slice_fusion.3
  18.9 1.6 %collective-permute-start.3 = (bf16[6,24,896]{2,1,0:T(8,128)(2,1)S(1)}, bf16[6,24,896]{2,1,0:T(8,128)(2,1)S(1)}, u32[]{:S(2)}, u32[]{:S(2)}) collective-permute-start(bf16[6,24,896]{2,1,0:T(8,128)(2,1)S(1)} %fusion.4), channel_id=1, source_target_pairs={{0,1},{1,0},{2,3},{3,2},{4,5},{5,4},{6,7},{7,6},{8,9},{9,8},{10,11... | collective-permute-start | bytes 774152 | tf_op jit(solution)/shard_map/ppermute | solution.py:406
  20.5 4.8 %collective-permute-done.3.far = bf16[6,24,896]{2,1,0:T(8,128)(2,1)S(1)} collective-permute-done((bf16[6,24,896]{2,1,0:T(8,128)(2,1)S(1)}, bf16[6,24,896]{2,1,0:T(8,128)(2,1)S(1)}, u32[]{:S(2)}, u32[]{:S(2)}) %collective-permute-start.3) | collective-permute-done | bytes 258080 | tf_op jit(solution)/shard_map/ppermute | solution.py:406
  26.0 2.3 %shard_map.309.package = bf16[352,896]{1,0:T(8,128)(2,1)} custom-call(s32[14]{0:T(128)} %fusion.5.meta, bf16[3,24,896]{2,1,0:T(8,128)(2,1)} %get-tuple-element.67.mine, bf16[3,24,896]{2,1,0:T(8,128)(2,1)} %copy-done.11, bf16[2,24,896]{2,1,0:T(8,128)(2,1)} %copy-done.14, bf16[3,24,896]{2,1,0:T(8,128)(2,1)} %copy-done.12, bf16[6,24,896]{2,1,0:T(8,128)(2,1)} %copy-done.13, ...), custom_call_target="tpu_custom_call" | custom-call | bytes 1024 | tf_op jit(solution)/shard_map/pallas_call | solution.py:385
  28.3 5.1 %all-to-all-done.near = bf16[4,128,768]{2,1,0:T(8,128)(2,1)S(1)} async-done(((bf16[4,128,768]{2,1,0:T(8,128)(2,1)}), bf16[4,128,768]{2,1,0:T(8,128)(2,1)S(1)}, u32[]{:S(2)}, u32[]{:S(2)}) %all-to-all-start) | async-done | bytes 786464 | tf_op jit(solution)/shard_map/all_to_all | solution.py:431
  33.4 1.5 collective-permute-start.4
  35.4 2.4 %collective-permute-start.6 = (bf16[128,768]{1,0:T(8,128)(2,1)S(1)}, bf16[128,768]{1,0:T(8,128)(2,1)S(1)}, u32[]{:S(2)}, u32[]{:S(2)}) collective-permute-start(bf16[128,768]{1,0:T(8,128)(2,1)S(1)} %bitcast.58), channel_id=1, source_target_pairs={{0,2},{1,3},{2,0},{3,1},{4,6},{5,7},{6,4},{7,5},{8,10},{9,11},{10,... | collective-permute-start | bytes 589832 | tf_op jit(solution)/shard_map/ppermute | solution.py:406
  37.8 0.9 collective-permute-start.7
  39.3 1.1 copy-done
  40.4 1.6 %shard_map.310 = (f32[1024,128]{1,0:T(8,128)S(1)}, f32[1024,128]{1,0:T(8,128)S(1)}, f32[1024,128]{1,0:T(8,128)S(1)}) custom-call(bf16[352,896]{1,0:T(8,128)(2,1)S(1)} %copy-done, f32[8,1]{1,0:T(8,128)S(1)} %copy-done.8), custom_call_target="tpu_custom_call" | custom-call | bytes 1024 | tf_op jit(solution)/shard_map/pallas_call | solution.py:385
  42.0 8.0 %collective-permute-done.5 = bf16[352,896]{1,0:T(8,128)(2,1)S(1)} collective-permute-done((bf16[352,896]{1,0:T(8,128)(2,1)}, bf16[352,896]{1,0:T(8,128)(2,1)S(1)}, u32[]{:S(2)}, u32[]{:S(2)}) %collective-permute-start.5) | collective-permute-done | bytes 630816 | tf_op jit(solution)/shard_map/ppermute | solution.py:411
  50.0 1.9 %collective-permute-done.7 = bf16[128,768]{1,0:T(8,128)(2,1)S(1)} collective-permute-done((bf16[128,768]{1,0:T(8,128)(2,1)S(1)}, bf16[128,768]{1,0:T(8,128)(2,1)S(1)}, u32[]{:S(2)}, u32[]{:S(2)}) %collective-permute-start.7) | collective-permute-done | bytes 196640 | tf_op jit(solution)/shard_map/ppermute | solution.py:406
  51.9 3.3 %collective-permute-done.8 = bf16[128,768]{1,0:T(8,128)(2,1)S(1)} collective-permute-done((bf16[128,768]{1,0:T(8,128)(2,1)S(1)}, bf16[128,768]{1,0:T(8,128)(2,1)S(1)}, u32[]{:S(2)}, u32[]{:S(2)}) %collective-permute-start.8) | collective-permute-done | bytes 196640 | tf_op jit(solution)/shard_map/ppermute | solution.py:406
  56.2 2.3 %collective-permute-done.9.other_pair = bf16[2,352,896]{2,1,0:T(8,128)(2,1)S(1)} collective-permute-done((bf16[2,352,896]{2,1,0:T(8,128)(2,1)S(1)}, bf16[2,352,896]{2,1,0:T(8,128)(2,1)S(1)}, u32[]{:S(2)}, u32[]{:S(2)}) %collective-permute-start.9) | collective-permute-done | bytes 1261600 | tf_op jit(solution)/shard_map/ppermute | solution.py:411
  58.5 10.4 %shard_map.311 = (bf16[3,128,768]{2,1,0:T(8,128)(2,1)S(1)}, bf16[128,768]{1,0:T(8,128)(2,1)S(1)}, bf16[3,128,768]{2,1,0:T(8,128)(2,1)S(1)}, bf16[128,768]{1,0:T(...) custom-call(s32[14]{0:T(128)S(1)} %copy-done.6, ...), custom_call_target="tpu_custom_call" | custom-call | flops 100000000 | bytes 1024 | tf_op jit(solution)/shard_map/pallas_call | solution.py:385
  68.9 6.7 %collective-permute-done.10.far = bf16[4,128,768]{2,1,0:T(8,128)(2,1)S(1)} collective-permute-done((bf16[4,128,768]{2,1,0:T(8,128)(2,1)S(1)}, bf16[4,128,768]{2,1,0:T(8,128)(2,1)S(1)}, u32[]{:S(2)}, u32[]{:S(2)}) %collective-permute-start.10) | collective-permute-done | bytes 786464 | tf_op jit(solution)/shard_map/ppermute | solution.py:406
  76.1 12.9 %shard_map.312 = (bf16[2,768,384]{2,1,0:T(8,128)(2,1)S(1)}, bf16[2,768,384]{2,1,0:T(8,128)(2,1)S(1)}, bf16[4,128,768]{2,1,0:T(8,128)(2,1)S(1)}, bf16[4,128,768]{2,1,0:T(8,128)(2,1)S(1)}) custom-call(s32[14]{0:T(128)S(1)} %copy-done.6, bf16[4,128,768]{2,1,0:T(8,128)(2,1)S(1)} %pad_maximum_fusion.1.near, bf16[4,128,768]{2,1,0:T(8,128)(2,1)S(1)} %collective-permute-done.10.far, ...), custom_call_target="tpu_custom_call" | custom-call | flops 100000000 | bytes 1024 | tf_op jit(solution)/shard_map/pallas_call | solution.py:385
  89.0 1.5 collective-permute-done.11
  91.3 2.3 %collective-permute-done.12 = bf16[2,768,384]{2,1,0:T(8,128)(2,1)S(1)} collective-permute-done((bf16[2,768,384]{2,1,0:T(8,128)(2,1)S(1)}, bf16[2,768,384]{2,1,0:T(8,128)(2,1)S(1)}, u32[]{:S(2)}, u32[]{:S(2)}) %collective-permute-start.12) | collective-permute-done | bytes 1179680 | tf_op jit(solution)/shard_map/ppermute | solution.py:411
  93.8 1.4 copy-done.9
  95.2 0.9 fusion.1
  96.1 0.8 slice_bitcast_fusion.7
  96.9 1.6 collective-permute-start.16
  98.5 1.5 collective-permute-start.15
  100.0 2.9 %collective-permute-start.14 = (bf16[128,768]{1,0:T(8,128)(2,1)S(1)}, bf16[128,768]{1,0:T(8,128)(2,1)S(1)}, u32[]{:S(2)}, u32[]{:S(2)}) collective-permute-start(bf16[128,768]{1,0:T(8,128)(2,1)S(1)} %get-tuple-element.132), channel_id=1, source_target_pairs={{0,4},{1,5},{2,6},{3,7},{4,0},{5,1},{6,2},{7,3},{8,12},{9,13},{10,... | collective-permute-start | bytes 589832 | tf_op jit(solution)/shard_map/ppermute | solution.py:406
  102.9 1.9 %collective-permute-done.13 = bf16[128,768]{1,0:T(8,128)(2,1)S(1)} collective-permute-done((bf16[128,768]{1,0:T(8,128)(2,1)}, bf16[128,768]{1,0:T(8,128)(2,1)S(1)}, u32[]{:S(2)}, u32[]{:S(2)}) %collective-permute-start.13) | collective-permute-done | bytes 196640 | tf_op jit(solution)/shard_map/ppermute | solution.py:406
  104.8 5.9 %collective-permute-done.17 = bf16[4,128,768]{2,1,0:T(8,128)(2,1)S(1)} collective-permute-done((bf16[4,128,768]{2,1,0:T(8,128)(2,1)S(1)}, bf16[4,128,768]{2,1,0:T(8,128)(2,1)S(1)}, u32[]{:S(2)}, u32[]{:S(2)}) %collective-permute-start.17) | collective-permute-done | bytes 786464 | tf_op jit(solution)/shard_map/ppermute | solution.py:406
  111.0 3.9 %collective-permute-done.15 = bf16[128,768]{1,0:T(8,128)(2,1)S(1)} collective-permute-done((bf16[128,768]{1,0:T(8,128)(2,1)}, bf16[128,768]{1,0:T(8,128)(2,1)S(1)}, u32[]{:S(2)}, u32[]{:S(2)}) %collective-permute-start.15) | collective-permute-done | bytes 196640 | tf_op jit(solution)/shard_map/ppermute | solution.py:406
  114.9 2.1 %collective-permute-done.14 = bf16[128,768]{1,0:T(8,128)(2,1)S(1)} collective-permute-done((bf16[128,768]{1,0:T(8,128)(2,1)S(1)}, bf16[128,768]{1,0:T(8,128)(2,1)S(1)}, u32[]{:S(2)}, u32[]{:S(2)}) %collective-permute-start.14) | collective-permute-done | bytes 196640 | tf_op jit(solution)/shard_map/ppermute | solution.py:406
  118.0 0.8 slice_bitcast_fusion.2
  118.8 2.4 %collective-permute-start.18 = (bf16[128,768]{1,0:T(8,128)(2,1)}, bf16[128,768]{1,0:T(8,128)(2,1)S(1)}, u32[]{:S(2)}, u32[]{:S(2)}) collective-permute-start(bf16[128,768]{1,0:T(8,128)(2,1)} %get-tuple-element.124), channel_id=1, source_target_pairs={{0,2},{1,3},{2,0},{3,1},{4,6},{5,7},{6,4},{7,5},{8,10},{9,11},{10,... | collective-permute-start | bytes 589832 | tf_op jit(solution)/shard_map/ppermute | solution.py:406
  122.0 4.3 %all-to-all-start.1 = ((bf16[8,56,384]{2,1,0:T(8,128)(2,1)}), bf16[8,56,384]{2,1,0:T(8,128)(2,1)S(1)}, u32[]{:S(2)}, u32[]{:S(2)}) async-start(bf16[8,56,384]{2,1,0:T(8,128)(2,1)} %pad_maximum_fusion.2), calls=%async_computation.1 | async-start | bytes 688128 | tf_op jit(solution)/shard_map/all_to_all | solution.py:1049
  126.5 2.8 %collective-permute-start.21 = (bf16[128,768]{1,0:T(8,128)(2,1)}, bf16[128,768]{1,0:T(8,128)(2,1)S(1)}, u32[]{:S(2)}, u32[]{:S(2)}) collective-permute-start(bf16[128,768]{1,0:T(8,128)(2,1)} %get-tuple-element.122), channel_id=1, source_target_pairs={{0,6},{1,7},{2,4},{3,5},{4,2},{5,3},{6,0},{7,1},{8,14},{9,15},{10,... | collective-permute-start | bytes 589832 | tf_op jit(solution)/shard_map/ppermute | solution.py:406
  129.3 0.8 fusion.3
  130.2 1.5 collective-permute-start.19
  133.1 1.3 collective-permute-start.22
  134.4 2.4 %collective-permute-done.19 = bf16[152,768]{1,0:T(8,128)(2,1)S(1)} collective-permute-done((bf16[152,768]{1,0:T(8,128)(2,1)S(1)}, bf16[152,768]{1,0:T(8,128)(2,1)S(1)}, u32[]{:S(2)}, u32[]{:S(2)}) %collective-permute-start.19) | collective-permute-done | bytes 233504 | tf_op jit(solution)/shard_map/ppermute | solution.py:406
  137.5 15.8 %collective-permute-done.22 = bf16[24,768]{1,0:T(8,128)(2,1)S(1)} collective-permute-done((bf16[24,768]{1,0:T(8,128)(2,1)S(1)}, bf16[24,768]{1,0:T(8,128)(2,1)S(1)}, u32[]{:S(2)}, u32[]{:S(2)}) %collective-permute-start.22) | collective-permute-done | bytes 36896 | tf_op jit(solution)/shard_map/ppermute | solution.py:421
  154.0 0.9 shard_map.313
  154.9 1.1 shard_map.314
  (75 shorter events, 10.2 us)
Async XLA Ops:
  4.0 6.5 %collective-permute-start = (bf16[3,24,896]{2,1,0:T(8,128)(2,1)}, bf16[3,24,896]{2,1,0:T(8,128)(2,1)S(1)}, u32[]{:S(2)}, u32[]{:S(2)}) collective-permute-start(bf16[3,24,896]{2,1,0:T(8,128)(2,1)} %get-tuple-element.65), channel_id=1, source_target_pairs={{0,2},{1,3},{2,0},{3,1},{4,6},{5,7},{6,4},{7,5},{8,10},{9,11},{10,... | collective-permute-start | bytes 387080 | tf_op jit(solution)/shard_map/ppermute | solution.py:406
  5.5 12.4 %collective-permute-start.1 = (bf16[2,24,896]{2,1,0:T(8,128)(2,1)}, bf16[2,24,896]{2,1,0:T(8,128)(2,1)S(1)}, u32[]{:S(2)}, u32[]{:S(2)}) collective-permute-start(bf16[2,24,896]{2,1,0:T(8,128)(2,1)} %get-tuple-element.68), channel_id=1, source_target_pairs={{0,4},{1,5},{2,6},{3,7},{4,0},{5,1},{6,2},{7,3},{8,12},{9,13},{10,... | collective-permute-start | bytes 258056 | tf_op jit(solution)/shard_map/ppermute | solution.py:406
  5.9 12.1 %collective-permute-start.2 = (bf16[3,24,896]{2,1,0:T(8,128)(2,1)}, bf16[3,24,896]{2,1,0:T(8,128)(2,1)S(1)}, u32[]{:S(2)}, u32[]{:S(2)}) collective-permute-start(bf16[3,24,896]{2,1,0:T(8,128)(2,1)} %get-tuple-element.69), channel_id=1, source_target_pairs={{0,6},{1,7},{2,4},{3,5},{4,2},{5,3},{6,0},{7,1},{8,14},{9,15},{10,... | collective-permute-start | bytes 387080 | tf_op jit(solution)/shard_map/ppermute | solution.py:406
  10.5 8.4 %copy-start.11 = (bf16[3,24,896]{2,1,0:T(8,128)(2,1)}, bf16[3,24,896]{2,1,0:T(8,128)(2,1)S(1)}, u32[]{:S(2)}) copy-start(bf16[3,24,896]{2,1,0:T(8,128)(2,1)S(1)} %collective-permute-done.two) | copy-start | bytes 387076
  12.4 21.0 %all-to-all-start = ((bf16[4,128,768]{2,1,0:T(8,128)(2,1)}), bf16[4,128,768]{2,1,0:T(8,128)(2,1)S(1)}, u32[]{:S(2)}, u32[]{:S(2)}) async-start(bf16[4,128,768]{2,1,0:T(8,128)(2,1)} %broadcast_in_dim.20), calls=%async_computation | async-start | bytes 1572864 | tf_op jit(solution)/shard_map/all_to_all | solution.py:431
  17.9 17.5 %copy-start.3 = (bf16[1,128,768]{2,1,0:T(8,128)(2,1)S(1)}, bf16[1,128,768]{2,1,0:T(8,128)(2,1)}, u32[]{:S(2)}) copy-start(bf16[1,128,768]{2,1,0:T(8,128)(2,1)} %param.23) | copy-start | bytes 589828
  17.9 21.4 %copy-start.8 = (f32[8,1]{1,0:T(8,128)S(1)}, f32[8,1]{1,0:T(8,128)}, u32[]{:S(2)}) copy-start(f32[8,1]{1,0:T(8,128)} %constant.72.clone.freq) | copy-start | bytes 100
  18.0 7.4 %copy-start.14 = (bf16[2,24,896]{2,1,0:T(8,128)(2,1)}, bf16[2,24,896]{2,1,0:T(8,128)(2,1)S(1)}, u32[]{:S(2)}) copy-start(bf16[2,24,896]{2,1,0:T(8,128)(2,1)S(1)} %collective-permute-done.1.four) | copy-start | bytes 258052
  18.0 7.3 %copy-start.12 = (bf16[3,24,896]{2,1,0:T(8,128)(2,1)}, bf16[3,24,896]{2,1,0:T(8,128)(2,1)S(1)}, u32[]{:S(2)}) copy-start(bf16[3,24,896]{2,1,0:T(8,128)(2,1)S(1)} %collective-permute-done.2.six) | copy-start | bytes 387076
  18.9 6.4 %collective-permute-start.3 = (bf16[6,24,896]{2,1,0:T(8,128)(2,1)S(1)}, bf16[6,24,896]{2,1,0:T(8,128)(2,1)S(1)}, u32[]{:S(2)}, u32[]{:S(2)}) collective-permute-start(bf16[6,24,896]{2,1,0:T(8,128)(2,1)S(1)} %fusion.4), channel_id=1, source_target_pairs={{0,1},{1,0},{2,3},{3,2},{4,5},{5,4},{6,7},{7,6},{8,9},{9,8},{10,11... | collective-permute-start | bytes 774152 | tf_op jit(solution)/shard_map/ppermute | solution.py:406
  25.3 0.7 copy-start.13
  33.4 21.8 %collective-permute-start.4 = (bf16[4,128,768]{2,1,0:T(8,128)(2,1)S(1)}, bf16[4,128,768]{2,1,0:T(8,128)(2,1)S(1)}, u32[]{:S(2)}, u32[]{:S(2)}) collective-permute-start(bf16[4,128,768]{2,1,0:T(8,128)(2,1)S(1)} %all-to-all-done.near), channel_id=1, source_target_pairs={{0,1},{1,0},{2,3},{3,2},{4,5},{5,4},{6,7},{7,6},{8,9},{9,8},{10,11... | collective-permute-start | bytes 2359304 | tf_op jit(solution)/shard_map/ppermute | solution.py:406
  34.9 15.1 %collective-permute-start.5 = (bf16[352,896]{1,0:T(8,128)(2,1)}, bf16[352,896]{1,0:T(8,128)(2,1)S(1)}, u32[]{:S(2)}, u32[]{:S(2)}) collective-permute-start(bf16[352,896]{1,0:T(8,128)(2,1)} %shard_map.309.package), channel_id=1, source_target_pairs={{0,16},{8,24},{16,0},{24,8},{1,17},{9,25},{17,1},{25,9},{2,18},{10... | collective-permute-start | bytes 1892360 | tf_op jit(solution)/shard_map/ppermute | solution.py:411
  35.4 14.6 %collective-permute-start.6 = (bf16[128,768]{1,0:T(8,128)(2,1)S(1)}, bf16[128,768]{1,0:T(8,128)(2,1)S(1)}, u32[]{:S(2)}, u32[]{:S(2)}) collective-permute-start(bf16[128,768]{1,0:T(8,128)(2,1)S(1)} %bitcast.58), channel_id=1, source_target_pairs={{0,2},{1,3},{2,0},{3,1},{4,6},{5,7},{6,4},{7,5},{8,10},{9,11},{10,... | collective-permute-start | bytes 589832 | tf_op jit(solution)/shard_map/ppermute | solution.py:406
  37.8 14.0 %collective-permute-start.7 = (bf16[128,768]{1,0:T(8,128)(2,1)S(1)}, bf16[128,768]{1,0:T(8,128)(2,1)S(1)}, u32[]{:S(2)}, u32[]{:S(2)}) collective-permute-start(bf16[128,768]{1,0:T(8,128)(2,1)S(1)} %bitcast.59), channel_id=1, source_target_pairs={{0,4},{1,5},{2,6},{3,7},{4,0},{5,1},{6,2},{7,3},{8,12},{9,13},{10,... | collective-permute-start | bytes 589832 | tf_op jit(solution)/shard_map/ppermute | solution.py:406
  38.7 16.5 %collective-permute-start.8 = (bf16[128,768]{1,0:T(8,128)(2,1)S(1)}, bf16[128,768]{1,0:T(8,128)(2,1)S(1)}, u32[]{:S(2)}, u32[]{:S(2)}) collective-permute-start(bf16[128,768]{1,0:T(8,128)(2,1)S(1)} %bitcast.60), channel_id=1, source_target_pairs={{0,6},{1,7},{2,4},{3,5},{4,2},{5,3},{6,0},{7,1},{8,14},{9,15},{10,... | collective-permute-start | bytes 589832 | tf_op jit(solution)/shard_map/ppermute | solution.py:406
  39.3 1.1 copy-start
  55.3 3.1 %copy-start.2 = (bf16[128,768]{1,0:T(8,128)(2,1)S(1)}, bf16[128,768]{1,0:T(8,128)(2,1)}, u32[]{:S(2)}) copy-start(bf16[128,768]{1,0:T(8,128)(2,1)} %constant.69.clone.pick24) | copy-start | bytes 589828
  55.4 3.1 %copy-start.4 = (bf16[128,384]{1,0:T(8,128)(2,1)S(1)}, bf16[128,384]{1,0:T(8,128)(2,1)}, u32[]{:S(2)}) copy-start(bf16[128,384]{1,0:T(8,128)(2,1)} %constant.71.clone.pick96) | copy-start | bytes 294916
  55.4 3.1 %copy-start.5 = (s32[1,768]{1,0:T(1,128)S(1)}, s32[1,768]{1,0:T(1,128)}, u32[]{:S(2)}) copy-start(s32[1,768]{1,0:T(1,128)} %constant.68.clone.own24) | copy-start | bytes 9220
  55.4 3.1 %copy-start.6 = (s32[14]{0:T(128)S(1)}, s32[14]{0:T(128)}, u32[]{:S(2)}) copy-start(s32[14]{0:T(128)} %fusion.5.meta) | copy-start | bytes 172
  55.4 3.1 %copy-start.7 = (s32[1,384]{1,0:T(1,128)S(1)}, s32[1,384]{1,0:T(1,128)}, u32[]{:S(2)}) copy-start(s32[1,384]{1,0:T(1,128)} %constant.70.clone.own96) | copy-start | bytes 4612
  55.4 3.0 %collective-permute-start.9 = (bf16[2,352,896]{2,1,0:T(8,128)(2,1)S(1)}, bf16[2,352,896]{2,1,0:T(8,128)(2,1)S(1)}, u32[]{:S(2)}, u32[]{:S(2)}) collective-permute-start(bf16[2,352,896]{2,1,0:T(8,128)(2,1)S(1)} %pad_maximum_fusion.own_pair), channel_id=1, source_target_pairs={{0,8},{8,0},{16,24},{24,16},{1,9},{9,1},{17,25},{25,17},{2,10},{10... | collective-permute-start | bytes 3784712 | tf_op jit(solution)/shard_map/ppermute | solution.py:411
  55.6 20.0 %collective-permute-start.10 = (bf16[4,128,768]{2,1,0:T(8,128)(2,1)S(1)}, bf16[4,128,768]{2,1,0:T(8,128)(2,1)S(1)}, u32[]{:S(2)}, u32[]{:S(2)}) collective-permute-start(bf16[4,128,768]{2,1,0:T(8,128)(2,1)S(1)} %pad_maximum_fusion.1.near), channel_id=1, source_target_pairs={{0,1},{1,0},{2,3},{3,2},{4,5},{5,4},{6,7},{7,6},{8,9},{9,8},{10,11... | collective-permute-start | bytes 2359304 | tf_op jit(solution)/shard_map/ppermute | solution.py:406
  75.6 14.9 %collective-permute-start.11 = (bf16[3,128,768]{2,1,0:T(8,128)(2,1)S(1)}, bf16[3,128,768]{2,1,0:T(8,128)(2,1)S(1)}, u32[]{:S(2)}, u32[]{:S(2)}) collective-permute-start(bf16[3,128,768]{2,1,0:T(8,128)(2,1)S(1)} %get-tuple-element.80), channel_id=1, source_target_pairs={{0,1},{1,0},{2,3},{3,2},{4,5},{5,4},{6,7},{7,6},{8,9},{9,8},{10,11... | collective-permute-start | bytes 1769480 | tf_op jit(solution)/shard_map/ppermute | solution.py:406
  90.7 2.9 %collective-permute-start.12 = (bf16[2,768,384]{2,1,0:T(8,128)(2,1)S(1)}, bf16[2,768,384]{2,1,0:T(8,128)(2,1)S(1)}, u32[]{:S(2)}, u32[]{:S(2)}) collective-permute-start(bf16[2,768,384]{2,1,0:T(8,128)(2,1)S(1)} %get-tuple-element.98), channel_id=1, source_target_pairs={{0,8},{8,0},{16,24},{24,16},{1,9},{9,1},{17,25},{25,17},{2,10},{10... | collective-permute-start | bytes 3538952 | tf_op jit(solution)/shard_map/ppermute | solution.py:411
  90.8 20.0 %collective-permute-start.17 = (bf16[4,128,768]{2,1,0:T(8,128)(2,1)S(1)}, bf16[4,128,768]{2,1,0:T(8,128)(2,1)S(1)}, u32[]{:S(2)}, u32[]{:S(2)}) collective-permute-start(bf16[4,128,768]{2,1,0:T(8,128)(2,1)S(1)} %get-tuple-element.102), channel_id=1, source_target_pairs={{0,1},{1,0},{2,3},{3,2},{4,5},{5,4},{6,7},{7,6},{8,9},{9,8},{10,11... | collective-permute-start | bytes 2359304 | tf_op jit(solution)/shard_map/ppermute | solution.py:406
  93.8 1.4 copy-start.9
  96.9 7.9 %collective-permute-start.13 = (bf16[128,768]{1,0:T(8,128)(2,1)}, bf16[128,768]{1,0:T(8,128)(2,1)S(1)}, u32[]{:S(2)}, u32[]{:S(2)}) collective-permute-start(bf16[128,768]{1,0:T(8,128)(2,1)} %get-tuple-element.130), channel_id=1, source_target_pairs={{0,2},{1,3},{2,0},{3,1},{4,6},{5,7},{6,4},{7,5},{8,10},{9,11},{10,... | collective-permute-start | bytes 589832 | tf_op jit(solution)/shard_map/ppermute | solution.py:406
  96.9 20.2 %collective-permute-start.16 = (bf16[768,384]{1,0:T(8,128)(2,1)}, bf16[768,384]{1,0:T(8,128)(2,1)S(1)}, u32[]{:S(2)}, u32[]{:S(2)}) collective-permute-start(bf16[768,384]{1,0:T(8,128)(2,1)} %fusion.1), channel_id=1, source_target_pairs={{0,16},{8,24},{16,0},{24,8},{1,17},{9,25},{17,1},{25,9},{2,18},{10... | collective-permute-start | bytes 1769480 | tf_op jit(solution)/shard_map/ppermute | solution.py:411
  98.5 16.4 %collective-permute-start.15 = (bf16[128,768]{1,0:T(8,128)(2,1)}, bf16[128,768]{1,0:T(8,128)(2,1)S(1)}, u32[]{:S(2)}, u32[]{:S(2)}) collective-permute-start(bf16[128,768]{1,0:T(8,128)(2,1)} %get-tuple-element.131), channel_id=1, source_target_pairs={{0,6},{1,7},{2,4},{3,5},{4,2},{5,3},{6,0},{7,1},{8,14},{9,15},{10,... | collective-permute-start | bytes 589832 | tf_op jit(solution)/shard_map/ppermute | solution.py:406
  100.0 17.0 %collective-permute-start.14 = (bf16[128,768]{1,0:T(8,128)(2,1)S(1)}, bf16[128,768]{1,0:T(8,128)(2,1)S(1)}, u32[]{:S(2)}, u32[]{:S(2)}) collective-permute-start(bf16[128,768]{1,0:T(8,128)(2,1)S(1)} %get-tuple-element.132), channel_id=1, source_target_pairs={{0,4},{1,5},{2,6},{3,7},{4,0},{5,1},{6,2},{7,3},{8,12},{9,13},{10,... | collective-permute-start | bytes 589832 | tf_op jit(solution)/shard_map/ppermute | solution.py:406
  110.7 6.4 %copy-start.10 = (f32[2,768,384]{2,1,0:T(8,128)S(1)}, f32[2,768,384]{2,1,0:T(8,128)}, u32[]{:S(2)}) copy-start(f32[2,768,384]{2,1,0:T(8,128)} %copy-done.9) | copy-start | bytes 7077892
  118.8 11.3 %collective-permute-start.18 = (bf16[128,768]{1,0:T(8,128)(2,1)}, bf16[128,768]{1,0:T(8,128)(2,1)S(1)}, u32[]{:S(2)}, u32[]{:S(2)}) collective-permute-start(bf16[128,768]{1,0:T(8,128)(2,1)} %get-tuple-element.124), channel_id=1, source_target_pairs={{0,2},{1,3},{2,0},{3,1},{4,6},{5,7},{6,4},{7,5},{8,10},{9,11},{10,... | collective-permute-start | bytes 589832 | tf_op jit(solution)/shard_map/ppermute | solution.py:406
  122.0 32.0 %all-to-all-start.1 = ((bf16[8,56,384]{2,1,0:T(8,128)(2,1)}), bf16[8,56,384]{2,1,0:T(8,128)(2,1)S(1)}, u32[]{:S(2)}, u32[]{:S(2)}) async-start(bf16[8,56,384]{2,1,0:T(8,128)(2,1)} %pad_maximum_fusion.2), calls=%async_computation.1 | async-start | bytes 688128 | tf_op jit(solution)/shard_map/all_to_all | solution.py:1049
  126.3 10.5 %copy-start.1 = (bf16[1,128,768]{2,1,0:T(8,128)(2,1)S(1)}, bf16[1,128,768]{2,1,0:T(8,128)(2,1)}, u32[]{:S(2)}) copy-start(bf16[1,128,768]{2,1,0:T(8,128)(2,1)} %param.21) | copy-start | bytes 589828
  126.3 28.6 %collective-permute-start.20 = (bf16[128,768]{1,0:T(8,128)(2,1)}, bf16[128,768]{1,0:T(8,128)(2,1)S(1)}, u32[]{:S(2)}, u32[]{:S(2)}) collective-permute-start(bf16[128,768]{1,0:T(8,128)(2,1)} %get-tuple-element.123), channel_id=1, source_target_pairs={{0,4},{1,5},{2,6},{3,7},{4,0},{5,1},{6,2},{7,3},{8,12},{9,13},{10,... | collective-permute-start | bytes 589832 | tf_op jit(solution)/shard_map/ppermute | solution.py:406
  126.5 28.4 %collective-permute-start.21 = (bf16[128,768]{1,0:T(8,128)(2,1)}, bf16[128,768]{1,0:T(8,128)(2,1)S(1)}, u32[]{:S(2)}, u32[]{:S(2)}) collective-permute-start(bf16[128,768]{1,0:T(8,128)(2,1)} %get-tuple-element.122), channel_id=1, source_target_pairs={{0,6},{1,7},{2,4},{3,5},{4,2},{5,3},{6,0},{7,1},{8,14},{9,15},{10,... | collective-permute-start | bytes 589832 | tf_op jit(solution)/shard_map/ppermute | solution.py:406
  130.2 6.6 %collective-permute-start.19 = (bf16[152,768]{1,0:T(8,128)(2,1)S(1)}, bf16[152,768]{1,0:T(8,128)(2,1)S(1)}, u32[]{:S(2)}, u32[]{:S(2)}) collective-permute-start(bf16[152,768]{1,0:T(8,128)(2,1)S(1)} %pad_maximum_fusion.4), channel_id=1, source_target_pairs={{0,1},{1,0},{2,3},{3,2},{4,5},{5,4},{6,7},{7,6},{8,9},{9,8},{10,11... | collective-permute-start | bytes 700424 | tf_op jit(solution)/shard_map/ppermute | solution.py:406
  132.5 5.1 %collective-permute-start.23 = (bf16[24,768]{1,0:T(8,128)(2,1)S(1)}, bf16[24,768]{1,0:T(8,128)(2,1)S(1)}, u32[]{:S(2)}, u32[]{:S(2)}) collective-permute-start(bf16[24,768]{1,0:T(8,128)(2,1)S(1)} %get-tuple-element.134), channel_id=1, source_target_pairs={{2,5},{10,13},{19,21},{27,29}} | collective-permute-start | bytes 110600 | tf_op jit(solution)/shard_map/ppermute | solution.py:421
  133.1 20.2 %collective-permute-start.22 = (bf16[24,768]{1,0:T(8,128)(2,1)S(1)}, bf16[24,768]{1,0:T(8,128)(2,1)S(1)}, u32[]{:S(2)}, u32[]{:S(2)}) collective-permute-start(bf16[24,768]{1,0:T(8,128)(2,1)S(1)} %get-tuple-element.133), channel_id=1, source_target_pairs={{0,2},{2,4},{6,5},{8,10},{10,12},{14,13},{17,18},{19,20},{23,21},{... | collective-permute-start | bytes 110600 | tf_op jit(solution)/shard_map/ppermute | solution.py:421
  154.9 1.1 copy-start.15
